TPU v7x, 32 devices: a whole 2x2x4 slice. The times are simulated.
32 devices in a mesh: groups: 2 (over y), expert: 4 (over z), head: 4 (over x, core).
Axes of the slice: x: 2, y: 2, z: 4, core: 2. Of those that a mesh axis runs over, the one named last changes fastest.
Arguments:
- residual: bfloat16 [64, 3584], P(('groups', 'expert')), parts along dimension 0, may hold values from -6 to 6
- query_latent: bfloat16 [64, 32, 512], P(('groups', 'expert'), 'head'), parts along dimension 0, may hold values from -16 to 16
- query_rope: bfloat16 [64, 32, 64], P(('groups', 'expert'), 'head'), parts along dimension 0, may hold values from -5 to 5
- cache_latent: bfloat16 [64, 32, 512], P(('groups', 'expert')), parts along dimension 0, may hold values from -4 to 4
- cache_rope: bfloat16 [64, 32, 64], P(('groups', 'expert')), parts along dimension 0, may hold values from -5 to 5
- absorb_value: bfloat16 [32, 512, 128], P('head'), may hold values from -0.25 to 0.25
- out_proj: bfloat16 [4096, 3584], P('head', 'expert'), may hold values from -0.09375 to 0.09375
- norm_gain: float32 [3584], replicated, may hold values from 0.5 to 1.5
- routes: int32 [64, 8], P(('groups', 'expert')), parts along dimension 0, may hold values from 0 to 31, all different within a row; in each aligned block of 4 rows (0 to 3, 4 to 7, ...) at most 2 rows name the same one
- route_weights: float32 [64, 8], P(('groups', 'expert')), parts along dimension 0, may hold values from 0.1 to 1
- w_gate: bfloat16 [32, 3584, 1024], P('expert', None, 'head'), may hold values from -0.09375 to 0.09375
- w_up: bfloat16 [32, 3584, 1024], P('expert', None, 'head'), may hold values from -0.09375 to 0.09375
- w_down: bfloat16 [32, 1024, 3584], P('expert', 'head'), may hold values from -0.1875 to 0.1875
Outputs:
- mid_state: bfloat16 [64, 3584], P(('groups', 'expert')), parts along dimension 0
- mixed: bfloat16 [64, 3584], P(('groups', 'expert')), parts along dimension 0
There are 2 independent parts, one for each index of `groups`. A program takes and returns all parts, laid end to end along the dimension named above; an argument that names none is the same for every part. Nothing has to cross between parts.
Inputs may be any that keep to these rules, and one draw needn't show every extreme that they name: `routes`: each row names 8 different experts. In each aligned block of 4 rows (the rows of one micro-batch of one index of expert) no expert is named by more than 2 rows, a bound that some block reaches.
All inputs are finite; a program needn't handle non-finite values.
Results may differ from a plain program's by a relative error of at most 0.012.
Values may be sent and summed in bfloat16 or wider, within the bound.
No kernel may reach another device: no remote copies, remote signals or barrier semaphores. Data moves between devices by JAX's collectives and lax.ppermute only.
A program may use at most 192 MiB of HBM per device.

v0:
```python
import jax
import jax.numpy as jnp
from jax import lax
from jax.sharding import PartitionSpec as P

CAP = 2


def attend(query_lat, query_rot, cache_lat, cache_rot, absorb_value, score_scale):
    scores = jnp.einsum("thl,tcl->thc", query_lat, cache_lat, preferred_element_type=jnp.float32)
    scores = scores + jnp.einsum(
        "thr,tcr->thc", query_rot, cache_rot, preferred_element_type=jnp.float32
    )
    scores = scores * score_scale
    probs = jax.nn.softmax(scores, axis=-1).astype(jnp.bfloat16)
    latent = jnp.einsum(
        "thc,tcl->thl", probs, cache_lat, preferred_element_type=jnp.float32
    ).astype(jnp.bfloat16)
    per_head = jnp.einsum(
        "thl,hlv->thv", latent, absorb_value, preferred_element_type=jnp.float32
    ).astype(jnp.bfloat16)
    return per_head.reshape(per_head.shape[0], per_head.shape[1] * per_head.shape[2])


def slot_codes(chosen_ids, capacity, expert_total):
    row_count, top_count = chosen_ids.shape
    flat_ids = chosen_ids.reshape(row_count * top_count)
    onehot = (flat_ids[:, None] == jnp.arange(expert_total, dtype=jnp.int32)[None, :]).astype(
        jnp.int32
    )
    before = jnp.cumsum(onehot, axis=0) - onehot
    slot_rank = jnp.sum(before * onehot, axis=1)
    return (flat_ids * capacity + slot_rank).reshape(row_count, top_count)


def dispatch_matrix(codes, slot_total):
    slot_index = jnp.arange(slot_total, dtype=jnp.int32)
    matches = codes[None, :, :] == slot_index[:, None, None]
    return jnp.any(matches, axis=2).astype(jnp.bfloat16)


def combine_matrix(codes, weights, slot_total):
    slot_index = jnp.arange(slot_total, dtype=jnp.int32)
    matches = codes[:, :, None] == slot_index[None, None, :]
    return jnp.sum(jnp.where(matches, weights[:, :, None], 0.0), axis=1)


def expert_terms(arrived, w_gate, w_up, w_down, sources):
    local_count = w_gate.shape[0]
    slot_grid = arrived.reshape(sources, local_count, arrived.shape[1], arrived.shape[2])
    gate_act = jnp.einsum("secd,edf->secf", slot_grid, w_gate, preferred_element_type=jnp.float32)
    up_act = jnp.einsum("secd,edf->secf", slot_grid, w_up, preferred_element_type=jnp.float32)
    hidden = (jax.nn.silu(gate_act) * up_act).astype(jnp.bfloat16)
    return jnp.einsum("secf,efd->secd", hidden, w_down, preferred_element_type=jnp.float32)


def shards(
    residual,
    query_latent,
    query_rope,
    cache_latent,
    cache_rope,
    absorb_value,
    out_proj,
    norm_gain,
    routes,
    route_weights,
    w_gate,
    w_up,
    w_down,
):
    sources = lax.axis_size("expert")
    experts = w_gate.shape[0] * sources
    row_count = residual.shape[0] // 2
    model_d = residual.shape[1]
    slot_total = experts * CAP
    score_scale = (absorb_value.shape[2] + query_rope.shape[2]) ** (-0.5)
    mid_list = []
    mix_list = []
    for micro_batch in range(2):
        start_row = micro_batch * row_count
        end_row = start_row + row_count
        per_head = attend(
            query_latent[start_row:end_row],
            query_rope[start_row:end_row],
            cache_latent[start_row:end_row],
            cache_rope[start_row:end_row],
            absorb_value,
            score_scale,
        )
        partial_cols = jnp.dot(
            lax.all_gather(per_head, "expert", axis=0, tiled=True),
            out_proj,
            preferred_element_type=jnp.float32,
        )
        summed = lax.psum(partial_cols, "head").astype(jnp.bfloat16)
        attention = lax.all_to_all(summed, "expert", split_axis=0, concat_axis=1, tiled=True)
        mid_state = (
            residual[start_row:end_row].astype(jnp.float32) + attention.astype(jnp.float32)
        ).astype(jnp.bfloat16)
        mid_float = mid_state.astype(jnp.float32)
        normed = (
            mid_float
            * lax.rsqrt(jnp.mean(mid_float * mid_float, axis=-1, keepdims=True) + 1e-06)
            * norm_gain
        ).astype(jnp.bfloat16)
        codes = slot_codes(routes[start_row:end_row], CAP, experts)
        placing = dispatch_matrix(codes, slot_total)
        outgoing = (
            jnp.dot(placing, normed, preferred_element_type=jnp.float32)
            .astype(jnp.bfloat16)
            .reshape(experts, CAP, model_d)
        )
        mixing = combine_matrix(codes, route_weights[start_row:end_row], slot_total)
        arrived = lax.all_to_all(outgoing, "expert", split_axis=0, concat_axis=0, tiled=True)
        expert_out = expert_terms(arrived, w_gate, w_up, w_down, sources)
        outputs = lax.psum(expert_out, "head").astype(jnp.bfloat16)
        returned = lax.all_to_all(
            outputs.reshape(experts, CAP, model_d),
            "expert",
            split_axis=0,
            concat_axis=0,
            tiled=True,
        )
        mixed = jnp.dot(
            mixing,
            returned.reshape(slot_total, model_d).astype(jnp.float32),
            precision=lax.Precision.HIGHEST,
        ).astype(jnp.bfloat16)
        mid_list.append(mid_state)
        mix_list.append(mixed)
    return (jnp.concatenate(mid_list, axis=0), jnp.concatenate(mix_list, axis=0))


def solution(mesh):
    in_specs = (
        P(("groups", "expert"), None),
        P(("groups", "expert"), "head", None),
        P(("groups", "expert"), "head", None),
        P(("groups", "expert"), None, None),
        P(("groups", "expert"), None, None),
        P("head", None, None),
        P("head", "expert"),
        P(),
        P(("groups", "expert"), None),
        P(("groups", "expert"), None),
        P("expert", None, "head"),
        P("expert", None, "head"),
        P("expert", "head", None),
    )
    out_specs = (P(("groups", "expert"), None), P(("groups", "expert"), None))
    return jax.shard_map(shards, mesh=mesh, in_specs=in_specs, out_specs=out_specs, check_vma=False)
```

profile of v0, /device:TPU:0, one launch (start us, length us, event | category | flops | bytes accessed | tf_op | source)
XLA Modules:
  0.0 200.1 jit_solution(12823052942383580060)
XLA Ops:
  7.3 1.5 fusion.51
  8.8 1.5 fusion.50
  10.3 14.8 %all-gather = bf16[4,4,1024]{2,1,0:T(4,128)(2,1)S(1)} all-gather(bf16[1,4,1024]{2,1,0:T(4,128)(2,1)S(1)} %fusion.50), channel_id=1, replica_groups=mesh['groups'=2,'expert'=4,'head'=4] {'expert'}, dimensions={0}, use_global_device_ids=true | all-gather | bytes 40960 | tf_op jit(solution)/shard_map/all_gather | solution.py:92
  25.1 13.2 %all-gather.1 = bf16[4,4,1024]{2,1,0:T(4,128)(2,1)S(1)} all-gather(bf16[1,4,1024]{2,1,0:T(4,128)(2,1)S(1)} %fusion.51), channel_id=1, replica_groups=mesh['groups'=2,'expert'=4,'head'=4] {'expert'}, dimensions={0}, use_global_device_ids=true | all-gather | bytes 40960 | tf_op jit(solution)/shard_map/all_gather | solution.py:92
  39.0 11.3 %all-reduce.1 = (bf16[16,896]{1,0:T(8,128)(2,1)S(1)}, bf16[16,896]{1,0:T(8,128)(2,1)S(1)}) all-reduce(f32[16,896]{1,0:T(8,128)S(1)} %fusion.89, f32[16,896]{1,0:T(8,128)S(1)} %fusion.88), channel_id=1, replica_groups=mesh['groups'=2,'expert'=4,'head'=4] {'head'}, use_global_device_ids=true, to_apply=%region_5.6 | all-reduce | flops 28672 | bytes 172032 | tf_op jit(solution)/shard_map/psum | solution.py:96
  51.0 4.6 %all-to-all-start.1 = ((bf16[4,4,896]{2,1,0:T(4,128)(2,1)}), bf16[4,4,896]{2,1,0:T(4,128)(2,1)S(1)}, u32[]{:S(2)}, u32[]{:S(2)}) async-start(bf16[4,4,896]{2,1,0:T(4,128)(2,1)} %all_to_all.34), calls=%async_computation.1 | async-start | bytes 57344 | tf_op jit(solution)/shard_map/all_to_all | solution.py:97
  58.7 2.5 %all-to-all-done.1 = bf16[4,4,896]{2,1,0:T(4,128)(2,1)S(1)} async-done(((bf16[4,4,896]{2,1,0:T(4,128)(2,1)}), bf16[4,4,896]{2,1,0:T(4,128)(2,1)S(1)}, u32[]{:S(2)}, u32[]{:S(2)}) %all-to-all-start.1) | async-done | bytes 28704 | tf_op jit(solution)/shard_map/all_to_all | solution.py:97
  61.2 3.3 %all-to-all-start = ((bf16[4,4,896]{2,1,0:T(4,128)(2,1)}), bf16[4,4,896]{2,1,0:T(4,128)(2,1)S(1)}, u32[]{:S(2)}, u32[]{:S(2)}) async-start(bf16[4,4,896]{2,1,0:T(4,128)(2,1)} %all_to_all.32), calls=%async_computation | async-start | bytes 57344 | tf_op jit(solution)/shard_map/all_to_all | solution.py:97
  64.6 5.5 %all-to-all-done = bf16[4,4,896]{2,1,0:T(4,128)(2,1)S(1)} async-done(((bf16[4,4,896]{2,1,0:T(4,128)(2,1)}), bf16[4,4,896]{2,1,0:T(4,128)(2,1)S(1)}, u32[]{:S(2)}, u32[]{:S(2)}) %all-to-all-start) | async-done | bytes 28704 | tf_op jit(solution)/shard_map/all_to_all | solution.py:97
  73.2 3.5 %all-to-all-start.2 = ((bf16[32,2,3584]{2,1,0:T(2,128)(2,1)}), bf16[32,2,3584]{2,1,0:T(2,128)(2,1)S(1)}, u32[]{:S(2)}, u32[]{:S(2)}) async-start(bf16[32,2,3584]{2,1,0:T(2,128)(2,1)} %reshape.97), calls=%async_computation.2 | async-start | bytes 917504 | tf_op jit(solution)/shard_map/all_to_all | solution.py:115
  78.7 9.2 %all-to-all-done.2 = bf16[32,2,3584]{2,1,0:T(2,128)(2,1)S(1)} async-done(((bf16[32,2,3584]{2,1,0:T(2,128)(2,1)}), bf16[32,2,3584]{2,1,0:T(2,128)(2,1)S(1)}, u32[]{:S(2)}, u32[]{:S(2)}) %all-to-all-start.2) | async-done | bytes 458784 | tf_op jit(solution)/shard_map/all_to_all | solution.py:115
  87.9 3.6 %all-to-all-start.4 = ((bf16[32,2,3584]{2,1,0:T(2,128)(2,1)}), bf16[32,2,3584]{2,1,0:T(2,128)(2,1)S(1)}, u32[]{:S(2)}, u32[]{:S(2)}) async-start(bf16[32,2,3584]{2,1,0:T(2,128)(2,1)} %reshape.101), calls=%async_computation.4 | async-start | bytes 917504 | tf_op jit(solution)/shard_map/all_to_all | solution.py:115
  91.6 7.4 %fusion.20 = f32[4,8,2,256]{3,0,2,1:T(4,128)S(1)} fusion(bf16[8,3584,256]{2,1,0:T(8,128)(2,1)} %param.23, bf16[4,8,2,3584]{3,1,0,2:T(8,128)(2,1)S(1)} %bitcast.113), kind=kOutput, calls=%fused_computation.20 | convolution fusion | flops 117440512 | bytes 15204352 | tf_op jit(solution)/shard_map/secd,edf->secf/dot_general | solution.py:51
  99.0 3.4 %all-to-all-done.4 = bf16[32,2,3584]{2,1,0:T(2,128)(2,1)S(1)} async-done(((bf16[32,2,3584]{2,1,0:T(2,128)(2,1)}), bf16[32,2,3584]{2,1,0:T(2,128)(2,1)S(1)}, u32[]{:S(2)}, u32[]{:S(2)}) %all-to-all-start.4) | async-done | bytes 458784 | tf_op jit(solution)/shard_map/all_to_all | solution.py:115
  102.4 7.5 %fusion.23 = f32[4,8,2,256]{3,0,2,1:T(4,128)S(1)} fusion(bf16[8,3584,256]{2,1,0:T(8,128)(2,1)} %param.23, bf16[4,8,2,3584]{3,1,0,2:T(8,128)(2,1)S(1)} %bitcast.115), kind=kOutput, calls=%fused_computation.21 | convolution fusion | flops 117440512 | bytes 15204352 | tf_op jit(solution)/shard_map/secd,edf->secf/dot_general | solution.py:51
  110.0 8.2 %fusion.41 = bf16[4,8,2,256]{3,0,2,1:T(4,128)(2,1)S(1)} fusion(bf16[8,3584,256]{2,1,0:T(8,128)(2,1)} %param.24, bf16[4,8,2,3584]{3,1,0,2:T(8,128)(2,1)S(1)} %bitcast.114, f32[4,8,2,256]{3,0,2,1:T(4,128)S(1)} %fusion.20), kind=kOutput, calls=%fused_computation.29 | convolution fusion | flops 117538816 | bytes 15237120 | tf_op jit(solution)/shard_map/secd,edf->secf/dot_general | solution.py:52
  118.6 2.2 %fusion.35 = bf16[4,8,2,256]{3,0,2,1:T(4,128)(2,1)S(1)} fusion(bf16[8,3584,256]{2,1,0:T(8,128)(2,1)S(1)} %bitcast.110, bf16[4,8,2,3584]{3,1,0,2:T(8,128)(2,1)S(1)} %bitcast.116, f32[4,8,2,256]{3,0,2,1:T(4,128)S(1)} %fusion.23), kind=kOutput, calls=%fused_computation.27 | convolution fusion | flops 117538816 | bytes 15237120 | tf_op jit(solution)/shard_map/secd,edf->secf/dot_general | solution.py:52
  120.9 2.0 fusion.17
  122.9 2.9 %fusion.14 = f32[4,8,2,3584]{3,0,2,1:T(4,128)} fusion(bf16[4,8,2,256]{3,0,2,1:T(4,128)(2,1)S(1)} %fusion.41, bf16[8,256,3584]{2,1,0:T(8,128)(2,1)S(1)} %bitcast.112), kind=kOutput, calls=%fused_computation.14 | convolution fusion | flops 117440512 | bytes 15630336 | tf_op jit(solution)/shard_map/secf,efd->secd/dot_general | solution.py:54
  125.9 36.9 %all-reduce.3 = (bf16[4,8,2,3584]{3,0,2,1:T(4,128)(2,1)}, bf16[4,8,2,3584]{3,0,2,1:T(4,128)(2,1)S(1)}) all-reduce(f32[4,8,2,3584]{3,0,2,1:T(4,128)S(1)} %fusion.17, f32[4,8,2,3584]{3,0,2,1:T(4,128)} %fusion.14), channel_id=1, replica_groups=mesh['groups'=2,'expert'=4,'head'=4] {'head'}, use_global_device_ids=true, to_apply=%region_17.18 | all-reduce | flops 458752 | bytes 2752512 | tf_op jit(solution)/shard_map/psum | solution.py:117
  165.1 3.5 %all-to-all-start.5 = ((bf16[32,2,3584]{2,1,0:T(2,128)(2,1)}), bf16[32,2,3584]{2,1,0:T(2,128)(2,1)S(1)}, u32[]{:S(2)}, u32[]{:S(2)}) async-start(bf16[32,2,3584]{2,1,0:T(2,128)(2,1)} %copy.56), calls=%async_computation.5 | async-start | bytes 917504 | tf_op jit(solution)/shard_map/all_to_all | solution.py:118
  170.0 12.4 %all-to-all-done.5 = bf16[32,2,3584]{2,1,0:T(2,128)(2,1)S(1)} async-done(((bf16[32,2,3584]{2,1,0:T(2,128)(2,1)}), bf16[32,2,3584]{2,1,0:T(2,128)(2,1)S(1)}, u32[]{:S(2)}, u32[]{:S(2)}) %all-to-all-start.5) | async-done | bytes 458784 | tf_op jit(solution)/shard_map/all_to_all | solution.py:118
  182.4 3.5 %all-to-all-start.3 = ((bf16[32,2,3584]{2,1,0:T(2,128)(2,1)}), bf16[32,2,3584]{2,1,0:T(2,128)(2,1)S(1)}, u32[]{:S(2)}, u32[]{:S(2)}) async-start(bf16[32,2,3584]{2,1,0:T(2,128)(2,1)} %copy.51), calls=%async_computation.3 | async-start | bytes 917504 | tf_op jit(solution)/shard_map/all_to_all | solution.py:118
  187.1 11.8 %all-to-all-done.3 = bf16[32,2,3584]{2,1,0:T(2,128)(2,1)S(1)} async-done(((bf16[32,2,3584]{2,1,0:T(2,128)(2,1)}), bf16[32,2,3584]{2,1,0:T(2,128)(2,1)S(1)}, u32[]{:S(2)}, u32[]{:S(2)}) %all-to-all-start.3) | async-done | bytes 458784 | tf_op jit(solution)/shard_map/all_to_all | solution.py:118
  (72 shorter events, 23.0 us)
Async XLA Ops:
  0.6 37.7 %copy-start = (bf16[1024,896]{1,0:T(8,128)(2,1)S(1)}, bf16[1024,896]{1,0:T(8,128)(2,1)}, u32[]{:S(2)}) copy-start(bf16[1024,896]{1,0:T(8,128)(2,1)} %param.19) | copy-start | bytes 5505028
  51.0 10.2 %all-to-all-start.1 = ((bf16[4,4,896]{2,1,0:T(4,128)(2,1)}), bf16[4,4,896]{2,1,0:T(4,128)(2,1)S(1)}, u32[]{:S(2)}, u32[]{:S(2)}) async-start(bf16[4,4,896]{2,1,0:T(4,128)(2,1)} %all_to_all.34), calls=%async_computation.1 | async-start | bytes 57344 | tf_op jit(solution)/shard_map/all_to_all | solution.py:97
  61.2 8.9 %all-to-all-start = ((bf16[4,4,896]{2,1,0:T(4,128)(2,1)}), bf16[4,4,896]{2,1,0:T(4,128)(2,1)S(1)}, u32[]{:S(2)}, u32[]{:S(2)}) async-start(bf16[4,4,896]{2,1,0:T(4,128)(2,1)} %all_to_all.32), calls=%async_computation | async-start | bytes 57344 | tf_op jit(solution)/shard_map/all_to_all | solution.py:97
  73.2 14.6 %all-to-all-start.2 = ((bf16[32,2,3584]{2,1,0:T(2,128)(2,1)}), bf16[32,2,3584]{2,1,0:T(2,128)(2,1)S(1)}, u32[]{:S(2)}, u32[]{:S(2)}) async-start(bf16[32,2,3584]{2,1,0:T(2,128)(2,1)} %reshape.97), calls=%async_computation.2 | async-start | bytes 917504 | tf_op jit(solution)/shard_map/all_to_all | solution.py:115
  87.9 14.5 %all-to-all-start.4 = ((bf16[32,2,3584]{2,1,0:T(2,128)(2,1)}), bf16[32,2,3584]{2,1,0:T(2,128)(2,1)S(1)}, u32[]{:S(2)}, u32[]{:S(2)}) async-start(bf16[32,2,3584]{2,1,0:T(2,128)(2,1)} %reshape.101), calls=%async_computation.4 | async-start | bytes 917504 | tf_op jit(solution)/shard_map/all_to_all | solution.py:115
  102.4 15.8 %slice-start = ((s8[14680064]{0:T(1024)(128)(4,1)}), s8[4194304]{0:T(1024)(128)(4,1)S(1)}, s32[]{:S(2)}) async-start(s8[14680064]{0:T(1024)(128)(4,1)} %bitcast.109), calls=%async_computation.6 | async-start | bytes 8388608
  102.4 15.8 %slice-start.1 = ((s8[14680064]{0:T(1024)(128)(4,1)}), s8[4194304]{0:T(1024)(128)(4,1)S(1)}, s32[]{:S(2)}) async-start(s8[14680064]{0:T(1024)(128)(4,1)} %bitcast.109), calls=%async_computation.7 | async-start | bytes 8388608
  102.4 18.5 %slice-start.4 = ((s8[14680064]{0:T(1024)(128)(4,1)}), s8[4194304]{0:T(1024)(128)(4,1)S(1)}, s32[]{:S(2)}) async-start(s8[14680064]{0:T(1024)(128)(4,1)} %bitcast.111), calls=%async_computation.10 | async-start | bytes 8388608
  102.4 18.4 %slice-start.5 = ((s8[14680064]{0:T(1024)(128)(4,1)}), s8[4194304]{0:T(1024)(128)(4,1)S(1)}, s32[]{:S(2)}) async-start(s8[14680064]{0:T(1024)(128)(4,1)} %bitcast.111), calls=%async_computation.11 | async-start | bytes 8388608
  110.0 8.3 %slice-start.2 = ((s8[14680064]{0:T(1024)(128)(4,1)}), s8[4194304]{0:T(1024)(128)(4,1)S(1)}, s32[]{:S(2)}) async-start(s8[14680064]{0:T(1024)(128)(4,1)} %bitcast.109), calls=%async_computation.8 | async-start | bytes 8388608
  110.0 8.6 %slice-start.3 = ((s8[14680064]{0:T(1024)(128)(4,1)}), s8[2097152]{0:T(1024)(128)(4,1)S(1)}, s32[]{:S(2)}) async-start(s8[14680064]{0:T(1024)(128)(4,1)} %bitcast.109), calls=%async_computation.9 | async-start | bytes 4194304
  110.0 10.9 %slice-start.6 = ((s8[14680064]{0:T(1024)(128)(4,1)}), s8[4194304]{0:T(1024)(128)(4,1)S(1)}, s32[]{:S(2)}) async-start(s8[14680064]{0:T(1024)(128)(4,1)} %bitcast.111), calls=%async_computation.12 | async-start | bytes 8388608
  118.6 2.3 %slice-start.7 = ((s8[14680064]{0:T(1024)(128)(4,1)}), s8[2097152]{0:T(1024)(128)(4,1)S(1)}, s32[]{:S(2)}) async-start(s8[14680064]{0:T(1024)(128)(4,1)} %bitcast.111), calls=%async_computation.13 | async-start | bytes 4194304
  120.9 47.7 %copy-start.1 = (f32[8,8]{1,0:T(8,128)S(1)}, f32[8,8]{1,0:T(8,128)}, u32[]{:S(2)}) copy-start(f32[8,8]{1,0:T(8,128)} %param.22) | copy-start | bytes 772
  165.1 17.3 %all-to-all-start.5 = ((bf16[32,2,3584]{2,1,0:T(2,128)(2,1)}), bf16[32,2,3584]{2,1,0:T(2,128)(2,1)S(1)}, u32[]{:S(2)}, u32[]{:S(2)}) async-start(bf16[32,2,3584]{2,1,0:T(2,128)(2,1)} %copy.56), calls=%async_computation.5 | async-start | bytes 917504 | tf_op jit(solution)/shard_map/all_to_all | solution.py:118
  182.4 16.5 %all-to-all-start.3 = ((bf16[32,2,3584]{2,1,0:T(2,128)(2,1)}), bf16[32,2,3584]{2,1,0:T(2,128)(2,1)S(1)}, u32[]{:S(2)}, u32[]{:S(2)}) async-start(bf16[32,2,3584]{2,1,0:T(2,128)(2,1)} %copy.51), calls=%async_computation.3 | async-start | bytes 917504 | tf_op jit(solution)/shard_map/all_to_all | solution.py:118
where the time goes:
time: 201 us; the launch traced here: 200 us
  blocking collectives  76.1 us (38%)
  waiting for transfers between devices  44.8 us (22%)
  matrix products  43 us (21%)
  starting transfers between devices  21.9 us (11%)
  local copies, waits for them, and re-layouts  8.92 us (4%)
  other arithmetic  4.37 us (2%)
    psum x1, blocking collectives, shards(): outputs = lax.psum(expert_out, 'head').astype(jnp.bfloat16)  36.9 us
    all_gather x2, blocking collectives, shards(): lax.all_gather(per_head, 'expert', axis=0, tiled=True)  28 us
    all_to_all x2, waiting for transfers between devices, shards(): lax.all_to_all(outputs.reshape(experts, CAP, model_d), 'expert', split_ax...  24.2 us
    dot_general x2, matrix products, expert_terms(): jnp.einsum('secd,edf->secf', slot_grid, w_gate, preferred_element_type=jn...  14.9 us
    all_to_all x2, waiting for transfers between devices, shards(): lax.all_to_all(outgoing, 'expert', split_axis=0, concat_axis=0, tiled=True)  12.6 us
    psum x1, blocking collectives, shards(): summed = lax.psum(partial_cols, 'head').astype(jnp.bfloat16)  11.3 us
    dot_general x2, matrix products, expert_terms(): jnp.einsum('secd,edf->secf', slot_grid, w_up, preferred_element_type=jnp....  10.5 us
    all_to_all x2, waiting for transfers between devices, shards(): lax.all_to_all(summed, 'expert', split_axis=0, concat_axis=1, tiled=True)  8.01 us
  transfers between devices with their start and end apart: 6, of which 6 were waited for; matrix products, arithmetic and copies ran while one was open for 7% of the time, Pallas kernels for 0%

commit v1 on v0

v1 whole, which is shorter than its diff:
```python
import jax
import jax.numpy as jnp
from jax import lax
from jax.sharding import PartitionSpec as P


def swap(x, axis, size, step):
    return lax.ppermute(x, axis, [(s, s ^ step) for s in range(size)])


def gather_rows(x, axis):
    size = lax.axis_size(axis)
    me = lax.axis_index(axis)
    out = jnp.zeros((size,) + x.shape, x.dtype)
    out = lax.dynamic_update_index_in_dim(out, x, me, 0)
    for step in range(1, size):
        out = lax.dynamic_update_index_in_dim(out, swap(x, axis, size, step), me ^ step, 0)
    return out


def scatter_sum(blocks, axis):
    size = lax.axis_size(axis)
    me = lax.axis_index(axis)
    total = lax.dynamic_index_in_dim(blocks, me, 0, keepdims=False)
    for step in range(1, size):
        block = lax.dynamic_index_in_dim(blocks, me ^ step, 0, keepdims=False)
        total = total + swap(block.astype(jnp.bfloat16), axis, size, step).astype(jnp.float32)
    return total


def sum_all(x, axis):
    size = lax.axis_size(axis)
    step = 1
    while step < size:
        x = x + swap(x.astype(jnp.bfloat16), axis, size, step).astype(jnp.float32)
        step *= 2
    return x


def attend(query_lat, query_rot, cache_lat, cache_rot, absorb_value, score_scale):
    scores = jnp.einsum("thl,tcl->thc", query_lat, cache_lat, preferred_element_type=jnp.float32)
    scores = scores + jnp.einsum(
        "thr,tcr->thc", query_rot, cache_rot, preferred_element_type=jnp.float32
    )
    probs = jax.nn.softmax(scores * score_scale, axis=-1).astype(jnp.bfloat16)
    latent = jnp.einsum(
        "thc,tcl->thl", probs, cache_lat, preferred_element_type=jnp.float32
    ).astype(jnp.bfloat16)
    per_head = jnp.einsum(
        "thl,hlv->thv", latent, absorb_value, preferred_element_type=jnp.float32
    ).astype(jnp.bfloat16)
    return per_head.reshape(per_head.shape[0], per_head.shape[1] * per_head.shape[2])


def shards(
    residual,
    query_latent,
    query_rope,
    cache_latent,
    cache_rope,
    absorb_value,
    out_proj,
    norm_gain,
    routes,
    route_weights,
    w_gate,
    w_up,
    w_down,
):
    sources = lax.axis_size("expert")
    me = lax.axis_index("expert")
    experts, model_d, hidden_f = w_gate.shape
    rows = residual.shape[0]
    tokens = rows * sources
    score_scale = (absorb_value.shape[2] + query_rope.shape[2]) ** (-0.5)
    all_res = gather_rows(residual, "expert").reshape(tokens, model_d)
    all_routes = gather_rows(routes, "expert").reshape(tokens, -1)
    all_weights = gather_rows(route_weights, "expert").reshape(tokens, -1)
    own_ids = me * experts + jnp.arange(experts, dtype=jnp.int32)
    named = all_routes[:, None, :] == own_ids[None, :, None]
    chosen = jnp.any(named, axis=2)
    weight = jnp.sum(jnp.where(named, all_weights[:, None, :], 0.0), axis=2)

    per_head = attend(
        query_latent, query_rope, cache_latent, cache_rope, absorb_value, score_scale
    )
    all_heads = gather_rows(per_head, "expert").reshape(tokens, -1)
    partial = jnp.dot(all_heads, out_proj, preferred_element_type=jnp.float32)
    summed = sum_all(partial, "head").astype(jnp.bfloat16)
    attention = gather_rows(summed, "expert")
    attention = attention.transpose(1, 0, 2).reshape(tokens, model_d)
    mid = (all_res.astype(jnp.float32) + attention.astype(jnp.float32)).astype(jnp.bfloat16)
    mid_float = mid.astype(jnp.float32)
    normed = (
        mid_float
        * lax.rsqrt(jnp.mean(mid_float * mid_float, axis=-1, keepdims=True) + 1e-06)
        * norm_gain
    ).astype(jnp.bfloat16)
    gate = jnp.einsum("td,edf->etf", normed, w_gate, preferred_element_type=jnp.float32)
    up = jnp.einsum("td,edf->etf", normed, w_up, preferred_element_type=jnp.float32)
    hidden = jnp.where(
        chosen.T[:, :, None], jax.nn.silu(gate) * up * weight.T[:, :, None], 0.0
    ).astype(jnp.bfloat16)
    down = jnp.einsum("etf,efd->td", hidden, w_down, preferred_element_type=jnp.float32)
    mixed = scatter_sum(down.reshape(sources, rows, model_d), "expert")
    mixed = sum_all(mixed, "head").astype(jnp.bfloat16)
    own_mid = lax.dynamic_slice_in_dim(mid, me * rows, rows, 0)
    return own_mid, mixed


def solution(mesh):
    in_specs = (
        P(("groups", "expert"), None),
        P(("groups", "expert"), "head", None),
        P(("groups", "expert"), "head", None),
        P(("groups", "expert"), None, None),
        P(("groups", "expert"), None, None),
        P("head", None, None),
        P("head", "expert"),
        P(),
        P(("groups", "expert"), None),
        P(("groups", "expert"), None),
        P("expert", None, "head"),
        P("expert", None, "head"),
        P("expert", "head", None),
    )
    out_specs = (P(("groups", "expert"), None), P(("groups", "expert"), None))
    return jax.shard_map(shards, mesh=mesh, in_specs=in_specs, out_specs=out_specs, check_vma=False)
```

time: 201 us -> 88.5 us (0.44)
  blocking collectives: 76.1 us -> 0 us
  waiting for transfers between devices: 44.8 us -> 23.8 us
  matrix products: 43 us -> 27.8 us
  starting transfers between devices: 21.9 us -> 28 us
  other arithmetic: 4.37 us -> 1.38 us
  local copies, waits for them, and re-layouts: 8.92 us -> 6.22 us
    psum x2 -> x0, blocking collectives: 48.2 us -> none  [the longest x1 36.9 us: shards(): outputs = lax.psum(expert_out, 'head').astype(jnp.bfloat16)]
    all_to_all x6 -> x0, waiting for transfers between devices: 44.8 us -> none  [the longest x2 24.2 us: shards(): lax.all_to_all(outputs.reshape(experts, CAP, model_d), 'expert', split_ax...]
    ppermute x0 -> x22, starting transfers between devices: none -> 28 us  [swap(): return lax.ppermute(x, axis, [(s, s ^ step) for s in range(size)])]
    all_gather x2 -> x0, blocking collectives: 28 us -> none  [shards(): lax.all_gather(per_head, 'expert', axis=0, tiled=True)]
    ppermute x0 -> x22, waiting for transfers between devices: none -> 23.8 us  [swap(): return lax.ppermute(x, axis, [(s, s ^ step) for s in range(size)])]
    all_to_all x6 -> x0, starting transfers between devices: 21.9 us -> none  [the longest x2 7.87 us: shards(): lax.all_to_all(summed, 'expert', split_axis=0, concat_axis=1, tiled=True)]
    dot_general x12 -> x3, matrix products: 33.7 us -> 22.8 us  [the longest x1 14.6 us: shards(): jnp.einsum('etf,efd->td', hidden, w_down, preferred_element_type=jnp.floa...]
    reshape x6 -> x0, local copies, waits for them, and re-layouts: 4.74 us -> none  [the longest x2 2.5 us: shards(): outputs.reshape(experts, CAP, model_d)]
  transfers between devices with their start and end apart: 6 -> 22, of which waited for: 6 -> 11; matrix products, arithmetic and copies ran while one was open for 7% -> 5% of each run, Pallas kernels for 0% -> 0%
where the time goes in v1:
time: 88.5 us; the launch traced here: 88.1 us
  starting transfers between devices  28 us (32%)
  matrix products  27.8 us (31%)
  waiting for transfers between devices  23.8 us (27%)
  local copies, waits for them, and re-layouts  6.22 us (7%)
  other arithmetic  1.38 us (2%)
  between operations  0.9 us (1%)
    ppermute x22, starting transfers between devices, swap(): return lax.ppermute(x, axis, [(s, s ^ step) for s in range(size)])  28 us
    ppermute x22, waiting for transfers between devices, swap(): return lax.ppermute(x, axis, [(s, s ^ step) for s in range(size)])  23.8 us
    dot_general x1, matrix products, shards(): jnp.einsum('etf,efd->td', hidden, w_down, preferred_element_type=jnp.floa...  14.6 us
    dot_general x1, matrix products, shards(): jnp.einsum('td,edf->etf', normed, w_gate, preferred_element_type=jnp.floa...  7.87 us
    dynamic_update_slice x16, local copies, waits for them, and re-layouts, gather_rows(): lax.dynamic_update_index_in_dim(out, swap(x, axis, size, step), me ^ step...  2.06 us
  transfers between devices with their start and end apart: 22, of which 11 were waited for; matrix products, arithmetic and copies ran while one was open for 5% of the time, Pallas kernels for 0%

profile of v1, /device:TPU:0, one launch (start us, length us, event | category | flops | bytes accessed | tf_op | source)
XLA Modules:
  0.0 88.1 jit_solution(1795342546839105310)
XLA Ops:
  0.7 1.3 %fusion.42 = f32[8,8,32]{2,1,0:T(8,128)S(1)} fusion(bf16[8,8,512]{2,1,0:T(8,128)(2,1)} %param.14, bf16[8,32,512]{2,1,0:T(8,128)(2,1)} %param.16), kind=kOutput, calls=%fused_computation.74 | convolution fusion | flops 2097152 | bytes 335872 | tf_op jit(solution)/shard_map/thl,tcl->thc/dot_general | solution.py:41
  4.4 1.5 %bitcast_dynamic-update-slice_fusion.7 = (bf16[4,8,1024]{2,1,0:T(8,128)(2,1)S(1)}, bf16[8,8,128]{2,1,0:T(8,128)(2,1)S(1)}) fusion(bf16[4,8,1024]{2,1,0:T(8,128)(2,1)S(1)} %broadcast_in_dim.119, s32[]{:T(128)S(6)} %select_n.49, bf16[8,512,128]{2,1,0:T(8,128)(2,1)} %param.18, bf16[8,8,512]{2,1,0:T(8,128)(2,1)S(1)} %convolution_convert_fusion), kind=kOutput, calls=%fused_computation.61 | convolution fusion | flops 8396800 | bytes 1146884 | tf_op jit(solution)/shard_map/thl,hlv->thv/dot_general | solution.py:49
  5.9 3.1 %collective-permute-start.3 = (bf16[8,1024]{1,0:T(8,128)(2,1)S(1)}, bf16[8,1024]{1,0:T(8,128)(2,1)S(1)}, u32[]{:S(2)}, u32[]{:S(2)}) collective-permute-start(bf16[8,1024]{1,0:T(8,128)(2,1)S(1)} %bitcast.107), channel_id=1, source_target_pairs={{0,4},{4,0},{8,12},{12,8},{1,5},{5,1},{9,13},{13,9},{2,6},{6,2},{1... | collective-permute-start | bytes 49160 | tf_op jit(solution)/shard_map/ppermute | solution.py:8
  8.9 2.6 %collective-permute-start.4 = (bf16[8,1024]{1,0:T(8,128)(2,1)S(1)}, bf16[8,1024]{1,0:T(8,128)(2,1)S(1)}, u32[]{:S(2)}, u32[]{:S(2)}) collective-permute-start(bf16[8,1024]{1,0:T(8,128)(2,1)S(1)} %bitcast.108), channel_id=1, source_target_pairs={{0,8},{4,12},{8,0},{12,4},{1,9},{5,13},{9,1},{13,5},{2,10},{6,14},... | collective-permute-start | bytes 49160 | tf_op jit(solution)/shard_map/ppermute | solution.py:8
  12.4 3.5 %collective-permute-start.12 = (s32[8,8]{1,0:T(8,128)}, s32[8,8]{1,0:T(8,128)S(1)}, u32[]{:S(2)}, u32[]{:S(2)}) collective-permute-start(s32[8,8]{1,0:T(8,128)} %param.21), channel_id=1, source_target_pairs={{0,8},{4,12},{8,0},{12,4},{1,9},{5,13},{9,1},{13,5},{2,10},{6,14},... | collective-permute-start | bytes 776 | tf_op jit(solution)/shard_map/ppermute | solution.py:8
  19.3 4.8 %collective-permute-done.13 = s32[8,8]{1,0:T(8,128)S(1)} collective-permute-done((s32[8,8]{1,0:T(8,128)}, s32[8,8]{1,0:T(8,128)S(1)}, u32[]{:S(2)}, u32[]{:S(2)}) %collective-permute-start.13) | collective-permute-done | bytes 288 | tf_op jit(solution)/shard_map/ppermute | solution.py:8
  24.4 1.8 %collective-permute-start.16 = (f32[8,8]{1,0:T(8,128)}, f32[8,8]{1,0:T(8,128)S(1)}, u32[]{:S(2)}, u32[]{:S(2)}) collective-permute-start(f32[8,8]{1,0:T(8,128)} %param.22), channel_id=1, source_target_pairs={{0,12},{4,8},{8,4},{12,0},{1,13},{5,9},{9,5},{13,1},{2,14},{6,10},... | collective-permute-start | bytes 776 | tf_op jit(solution)/shard_map/ppermute | solution.py:8
  26.3 2.5 %collective-permute-done.15 = f32[8,8]{1,0:T(8,128)S(1)} collective-permute-done((f32[8,8]{1,0:T(8,128)}, f32[8,8]{1,0:T(8,128)S(1)}, u32[]{:S(2)}, u32[]{:S(2)}) %collective-permute-start.15) | collective-permute-done | bytes 288 | tf_op jit(solution)/shard_map/ppermute | solution.py:8
  28.9 1.3 %collective-permute-done.16 = f32[8,8]{1,0:T(8,128)S(1)} collective-permute-done((f32[8,8]{1,0:T(8,128)}, f32[8,8]{1,0:T(8,128)S(1)}, u32[]{:S(2)}, u32[]{:S(2)}) %collective-permute-start.16) | collective-permute-done | bytes 288 | tf_op jit(solution)/shard_map/ppermute | solution.py:8
  30.2 1.4 %collective-permute-start.1 = (bf16[8,3584]{1,0:T(8,128)(2,1)}, bf16[8,3584]{1,0:T(8,128)(2,1)S(1)}, u32[]{:S(2)}, u32[]{:S(2)}) collective-permute-start(bf16[8,3584]{1,0:T(8,128)(2,1)} %param.13), channel_id=1, source_target_pairs={{0,8},{4,12},{8,0},{12,4},{1,9},{5,13},{9,1},{13,5},{2,10},{6,14},... | collective-permute-start | bytes 172040 | tf_op jit(solution)/shard_map/ppermute | solution.py:8
  32.0 1.8 %collective-permute-start.2 = (bf16[8,3584]{1,0:T(8,128)(2,1)}, bf16[8,3584]{1,0:T(8,128)(2,1)S(1)}, u32[]{:S(2)}, u32[]{:S(2)}) collective-permute-start(bf16[8,3584]{1,0:T(8,128)(2,1)} %param.13), channel_id=1, source_target_pairs={{0,12},{4,8},{8,4},{12,0},{1,13},{5,9},{9,5},{13,1},{2,14},{6,10},... | collective-permute-start | bytes 172040 | tf_op jit(solution)/shard_map/ppermute | solution.py:8
  35.6 1.6 %collective-permute-start.7 = (bf16[32,896]{1,0:T(8,128)(2,1)S(1)}, bf16[32,896]{1,0:T(8,128)(2,1)S(1)}, u32[]{:S(2)}, u32[]{:S(2)}) collective-permute-start(bf16[32,896]{1,0:T(8,128)(2,1)S(1)} %fusion.26), channel_id=1, source_target_pairs={{0,2},{1,3},{2,0},{3,1},{4,6},{5,7},{6,4},{7,5},{8,10},{9,11},{10,... | collective-permute-start | bytes 172040 | tf_op jit(solution)/shard_map/ppermute | solution.py:8
  37.2 2.7 %collective-permute-done.7 = bf16[32,896]{1,0:T(8,128)(2,1)S(1)} collective-permute-done((bf16[32,896]{1,0:T(8,128)(2,1)S(1)}, bf16[32,896]{1,0:T(8,128)(2,1)S(1)}, u32[]{:S(2)}, u32[]{:S(2)}) %collective-permute-start.7) | collective-permute-done | bytes 57376 | tf_op jit(solution)/shard_map/ppermute | solution.py:8
  40.4 2.3 %collective-permute-start.9 = (bf16[32,896]{1,0:T(8,128)(2,1)S(1)}, bf16[32,896]{1,0:T(8,128)(2,1)S(1)}, u32[]{:S(2)}, u32[]{:S(2)}) collective-permute-start(bf16[32,896]{1,0:T(8,128)(2,1)S(1)} %get-tuple-element.5), channel_id=1, source_target_pairs={{0,8},{4,12},{8,0},{12,4},{1,9},{5,13},{9,1},{13,5},{2,10},{6,14},... | collective-permute-start | bytes 172040 | tf_op jit(solution)/shard_map/ppermute | solution.py:8
  42.7 1.7 %collective-permute-start.10 = (bf16[32,896]{1,0:T(8,128)(2,1)S(1)}, bf16[32,896]{1,0:T(8,128)(2,1)S(1)}, u32[]{:S(2)}, u32[]{:S(2)}) collective-permute-start(bf16[32,896]{1,0:T(8,128)(2,1)S(1)} %get-tuple-element.5), channel_id=1, source_target_pairs={{0,12},{4,8},{8,4},{12,0},{1,13},{5,9},{9,5},{13,1},{2,14},{6,10},... | collective-permute-start | bytes 172040 | tf_op jit(solution)/shard_map/ppermute | solution.py:8
  45.7 3.0 %collective-permute-done.10 = bf16[32,896]{1,0:T(8,128)(2,1)S(1)} collective-permute-done((bf16[32,896]{1,0:T(8,128)(2,1)S(1)}, bf16[32,896]{1,0:T(8,128)(2,1)S(1)}, u32[]{:S(2)}, u32[]{:S(2)}) %collective-permute-start.10) | collective-permute-done | bytes 57376 | tf_op jit(solution)/shard_map/ppermute | solution.py:8
  48.8 1.6 %dynamic_update_slice.76 = bf16[4,32,896]{2,0,1:T(4,128)(2,1)S(1)} dynamic-update-slice(bf16[4,32,896]{2,0,1:T(4,128)(2,1)S(1)} %copy.20, bf16[1,32,896]{2,0,1:T(2,128)(2,1)S(1)} %copy.21, s32[]{:T(128)S(6)} %select_n.52, s32[]{:T(128)} %constant.87.clone.1, s32[]{:T(128)} %constant.87.clone.1) | dynamic-update-slice | bytes 114692 | tf_op jit(solution)/shard_map/jit(dynamic_update_index_in_dim)/dynamic_update_slice | solution.py:17
  51.0 7.9 %convolution_bitcast_fusion.2 = f32[8,32,256]{2,1,0:T(8,128)S(1)} fusion(bf16[8,3584,256]{2,1,0:T(8,128)(2,1)} %param.23, bf16[32,3584]{1,0:T(8,128)(2,1)S(1)} %fusion.9, f32[3584]{0:T(1024)} %param.20, f32[32]{0:T(128)S(1)} %rsqrt.12), kind=kOutput, calls=%fused_computation.3 | convolution fusion | flops 470220800 | bytes 15186048 | tf_op jit(solution)/shard_map/td,edf->etf/dot_general | solution.py:99
  58.9 14.6 %convolution_bitcast_fusion = f32[4,8,3584]{2,1,0:T(8,128)S(1)} fusion(bf16[8,256,3584]{2,1,0:T(8,128)(2,1)} %param.25, bf16[8,3584,256]{2,1,0:T(8,128)(2,1)} %param.24, f32[8,32,256]{2,1,0:T(8,128)S(1)} %convolution_bitcast_fusion.2, f32[8,32]{1,0:T(8,128)S(1)} %bitcast.110, pred[8,32]{1,0:T(8,128)(4,1)S(1)} %bitcast.111, bf16[32,3584]{1,0:T(8,128)(2,1)S(1)} %fusion.9, ...), kind=kOutput, calls=%fused_computation.1 | convolution fusion | flops 940507136 | bytes 30326144 | tf_op jit(solution)/shard_map/etf,efd->td/dot_general | solution.py:104
  73.6 2.3 %collective-permute-start.18 = (bf16[8,3584]{1,0:T(8,128)(2,1)S(1)}, bf16[8,3584]{1,0:T(8,128)(2,1)S(1)}, u32[]{:S(2)}, u32[]{:S(2)}) collective-permute-start(bf16[8,3584]{1,0:T(8,128)(2,1)S(1)} %get-tuple-element.8), channel_id=1, source_target_pairs={{0,8},{4,12},{8,0},{12,4},{1,9},{5,13},{9,1},{13,5},{2,10},{6,14},... | collective-permute-start | bytes 172040 | tf_op jit(solution)/shard_map/ppermute | solution.py:8
  75.9 2.1 %collective-permute-start.19 = (bf16[8,3584]{1,0:T(8,128)(2,1)S(1)}, bf16[8,3584]{1,0:T(8,128)(2,1)S(1)}, u32[]{:S(2)}, u32[]{:S(2)}) collective-permute-start(bf16[8,3584]{1,0:T(8,128)(2,1)S(1)} %get-tuple-element.7), channel_id=1, source_target_pairs={{0,12},{4,8},{8,4},{12,0},{1,13},{5,9},{9,5},{13,1},{2,14},{6,10},... | collective-permute-start | bytes 172040 | tf_op jit(solution)/shard_map/ppermute | solution.py:8
  78.9 2.9 %collective-permute-done.19 = bf16[8,3584]{1,0:T(8,128)(2,1)S(1)} collective-permute-done((bf16[8,3584]{1,0:T(8,128)(2,1)S(1)}, bf16[8,3584]{1,0:T(8,128)(2,1)S(1)}, u32[]{:S(2)}, u32[]{:S(2)}) %collective-permute-start.19) | collective-permute-done | bytes 57376 | tf_op jit(solution)/shard_map/ppermute | solution.py:8
  83.2 1.6 %collective-permute-start.21 = (bf16[8,3584]{1,0:T(8,128)(2,1)S(1)}, bf16[8,3584]{1,0:T(8,128)(2,1)S(1)}, u32[]{:S(2)}, u32[]{:S(2)}) collective-permute-start(bf16[8,3584]{1,0:T(8,128)(2,1)S(1)} %fusion.27), channel_id=1, source_target_pairs={{0,2},{1,3},{2,0},{3,1},{4,6},{5,7},{6,4},{7,5},{8,10},{9,11},{10,... | collective-permute-start | bytes 172040 | tf_op jit(solution)/shard_map/ppermute | solution.py:8
  85.4 2.1 %collective-permute-done.21 = bf16[8,3584]{1,0:T(8,128)(2,1)S(1)} collective-permute-done((bf16[8,3584]{1,0:T(8,128)(2,1)S(1)}, bf16[8,3584]{1,0:T(8,128)(2,1)S(1)}, u32[]{:S(2)}, u32[]{:S(2)}) %collective-permute-start.21) | collective-permute-done | bytes 57376 | tf_op jit(solution)/shard_map/ppermute | solution.py:8
  (84 shorter events, 15.4 us)
Async XLA Ops:
  0.6 33.2 %copy-start = (bf16[1024,896]{1,0:T(8,128)(2,1)S(1)}, bf16[1024,896]{1,0:T(8,128)(2,1)}, u32[]{:S(2)}) copy-start(bf16[1024,896]{1,0:T(8,128)(2,1)} %param.19) | copy-start | bytes 5505028
  0.6 58.2 %copy-start.1 = (f32[3584]{0:T(1024)S(1)}, f32[3584]{0:T(1024)}, u32[]{:S(2)}) copy-start(f32[3584]{0:T(1024)} %param.20) | copy-start | bytes 43012
  5.9 26.2 %collective-permute-start.3 = (bf16[8,1024]{1,0:T(8,128)(2,1)S(1)}, bf16[8,1024]{1,0:T(8,128)(2,1)S(1)}, u32[]{:S(2)}, u32[]{:S(2)}) collective-permute-start(bf16[8,1024]{1,0:T(8,128)(2,1)S(1)} %bitcast.107), channel_id=1, source_target_pairs={{0,4},{4,0},{8,12},{12,8},{1,5},{5,1},{9,13},{13,9},{2,6},{6,2},{1... | collective-permute-start | bytes 49160 | tf_op jit(solution)/shard_map/ppermute | solution.py:8
  8.9 24.9 %collective-permute-start.4 = (bf16[8,1024]{1,0:T(8,128)(2,1)S(1)}, bf16[8,1024]{1,0:T(8,128)(2,1)S(1)}, u32[]{:S(2)}, u32[]{:S(2)}) collective-permute-start(bf16[8,1024]{1,0:T(8,128)(2,1)S(1)} %bitcast.108), channel_id=1, source_target_pairs={{0,8},{4,12},{8,0},{12,4},{1,9},{5,13},{9,1},{13,5},{2,10},{6,14},... | collective-permute-start | bytes 49160 | tf_op jit(solution)/shard_map/ppermute | solution.py:8
  11.5 22.3 %collective-permute-start.5 = (bf16[8,1024]{1,0:T(8,128)(2,1)S(1)}, bf16[8,1024]{1,0:T(8,128)(2,1)S(1)}, u32[]{:S(2)}, u32[]{:S(2)}) collective-permute-start(bf16[8,1024]{1,0:T(8,128)(2,1)S(1)} %bitcast.109), channel_id=1, source_target_pairs={{0,12},{4,8},{8,4},{12,0},{1,13},{5,9},{9,5},{13,1},{2,14},{6,10},... | collective-permute-start | bytes 49160 | tf_op jit(solution)/shard_map/ppermute | solution.py:8
  11.5 6.9 %collective-permute-start.11 = (s32[8,8]{1,0:T(8,128)}, s32[8,8]{1,0:T(8,128)S(1)}, u32[]{:S(2)}, u32[]{:S(2)}) collective-permute-start(s32[8,8]{1,0:T(8,128)} %param.21), channel_id=1, source_target_pairs={{0,4},{4,0},{8,12},{12,8},{1,5},{5,1},{9,13},{13,9},{2,6},{6,2},{1... | collective-permute-start | bytes 776 | tf_op jit(solution)/shard_map/ppermute | solution.py:8
  12.4 6.8 %collective-permute-start.12 = (s32[8,8]{1,0:T(8,128)}, s32[8,8]{1,0:T(8,128)S(1)}, u32[]{:S(2)}, u32[]{:S(2)}) collective-permute-start(s32[8,8]{1,0:T(8,128)} %param.21), channel_id=1, source_target_pairs={{0,8},{4,12},{8,0},{12,4},{1,9},{5,13},{9,1},{13,5},{2,10},{6,14},... | collective-permute-start | bytes 776 | tf_op jit(solution)/shard_map/ppermute | solution.py:8
  18.4 5.7 %collective-permute-start.13 = (s32[8,8]{1,0:T(8,128)}, s32[8,8]{1,0:T(8,128)S(1)}, u32[]{:S(2)}, u32[]{:S(2)}) collective-permute-start(s32[8,8]{1,0:T(8,128)} %param.21), channel_id=1, source_target_pairs={{0,12},{4,8},{8,4},{12,0},{1,13},{5,9},{9,5},{13,1},{2,14},{6,10},... | collective-permute-start | bytes 776 | tf_op jit(solution)/shard_map/ppermute | solution.py:8
  19.2 5.2 %collective-permute-start.14 = (f32[8,8]{1,0:T(8,128)}, f32[8,8]{1,0:T(8,128)S(1)}, u32[]{:S(2)}, u32[]{:S(2)}) collective-permute-start(f32[8,8]{1,0:T(8,128)} %param.22), channel_id=1, source_target_pairs={{0,4},{4,0},{8,12},{12,8},{1,5},{5,1},{9,13},{13,9},{2,6},{6,2},{1... | collective-permute-start | bytes 776 | tf_op jit(solution)/shard_map/ppermute | solution.py:8
  24.1 4.7 %collective-permute-start.15 = (f32[8,8]{1,0:T(8,128)}, f32[8,8]{1,0:T(8,128)S(1)}, u32[]{:S(2)}, u32[]{:S(2)}) collective-permute-start(f32[8,8]{1,0:T(8,128)} %param.22), channel_id=1, source_target_pairs={{0,8},{4,12},{8,0},{12,4},{1,9},{5,13},{9,1},{13,5},{2,10},{6,14},... | collective-permute-start | bytes 776 | tf_op jit(solution)/shard_map/ppermute | solution.py:8
  24.4 5.8 %collective-permute-start.16 = (f32[8,8]{1,0:T(8,128)}, f32[8,8]{1,0:T(8,128)S(1)}, u32[]{:S(2)}, u32[]{:S(2)}) collective-permute-start(f32[8,8]{1,0:T(8,128)} %param.22), channel_id=1, source_target_pairs={{0,12},{4,8},{8,4},{12,0},{1,13},{5,9},{9,5},{13,1},{2,14},{6,10},... | collective-permute-start | bytes 776 | tf_op jit(solution)/shard_map/ppermute | solution.py:8
  28.8 5.5 %collective-permute-start = (bf16[8,3584]{1,0:T(8,128)(2,1)}, bf16[8,3584]{1,0:T(8,128)(2,1)S(1)}, u32[]{:S(2)}, u32[]{:S(2)}) collective-permute-start(bf16[8,3584]{1,0:T(8,128)(2,1)} %param.13), channel_id=1, source_target_pairs={{0,4},{4,0},{8,12},{12,8},{1,5},{5,1},{9,13},{13,9},{2,6},{6,2},{1... | collective-permute-start | bytes 172040 | tf_op jit(solution)/shard_map/ppermute | solution.py:8
  30.2 7.0 %collective-permute-start.1 = (bf16[8,3584]{1,0:T(8,128)(2,1)}, bf16[8,3584]{1,0:T(8,128)(2,1)S(1)}, u32[]{:S(2)}, u32[]{:S(2)}) collective-permute-start(bf16[8,3584]{1,0:T(8,128)(2,1)} %param.13), channel_id=1, source_target_pairs={{0,8},{4,12},{8,0},{12,4},{1,9},{5,13},{9,1},{13,5},{2,10},{6,14},... | collective-permute-start | bytes 172040 | tf_op jit(solution)/shard_map/ppermute | solution.py:8
  32.0 8.3 %collective-permute-start.2 = (bf16[8,3584]{1,0:T(8,128)(2,1)}, bf16[8,3584]{1,0:T(8,128)(2,1)S(1)}, u32[]{:S(2)}, u32[]{:S(2)}) collective-permute-start(bf16[8,3584]{1,0:T(8,128)(2,1)} %param.13), channel_id=1, source_target_pairs={{0,12},{4,8},{8,4},{12,0},{1,13},{5,9},{9,5},{13,1},{2,14},{6,10},... | collective-permute-start | bytes 172040 | tf_op jit(solution)/shard_map/ppermute | solution.py:8
  34.3 1.3 %collective-permute-start.6 = (bf16[32,896]{1,0:T(8,128)(2,1)S(1)}, bf16[32,896]{1,0:T(8,128)(2,1)S(1)}, u32[]{:S(2)}, u32[]{:S(2)}) collective-permute-start(bf16[32,896]{1,0:T(8,128)(2,1)S(1)} %get-tuple-element.13), channel_id=1, source_target_pairs={{0,1},{1,0},{2,3},{3,2},{4,5},{5,4},{6,7},{7,6},{8,9},{9,8},{10,11... | collective-permute-start | bytes 172040 | tf_op jit(solution)/shard_map/ppermute | solution.py:8
  35.6 4.2 %collective-permute-start.7 = (bf16[32,896]{1,0:T(8,128)(2,1)S(1)}, bf16[32,896]{1,0:T(8,128)(2,1)S(1)}, u32[]{:S(2)}, u32[]{:S(2)}) collective-permute-start(bf16[32,896]{1,0:T(8,128)(2,1)S(1)} %fusion.26), channel_id=1, source_target_pairs={{0,2},{1,3},{2,0},{3,1},{4,6},{5,7},{6,4},{7,5},{8,10},{9,11},{10,... | collective-permute-start | bytes 172040 | tf_op jit(solution)/shard_map/ppermute | solution.py:8
  39.9 4.5 %collective-permute-start.8 = (bf16[32,896]{1,0:T(8,128)(2,1)S(1)}, bf16[32,896]{1,0:T(8,128)(2,1)S(1)}, u32[]{:S(2)}, u32[]{:S(2)}) collective-permute-start(bf16[32,896]{1,0:T(8,128)(2,1)S(1)} %get-tuple-element.5), channel_id=1, source_target_pairs={{0,4},{4,0},{8,12},{12,8},{1,5},{5,1},{9,13},{13,9},{2,6},{6,2},{1... | collective-permute-start | bytes 172040 | tf_op jit(solution)/shard_map/ppermute | solution.py:8
  40.4 5.2 %collective-permute-start.9 = (bf16[32,896]{1,0:T(8,128)(2,1)S(1)}, bf16[32,896]{1,0:T(8,128)(2,1)S(1)}, u32[]{:S(2)}, u32[]{:S(2)}) collective-permute-start(bf16[32,896]{1,0:T(8,128)(2,1)S(1)} %get-tuple-element.5), channel_id=1, source_target_pairs={{0,8},{4,12},{8,0},{12,4},{1,9},{5,13},{9,1},{13,5},{2,10},{6,14},... | collective-permute-start | bytes 172040 | tf_op jit(solution)/shard_map/ppermute | solution.py:8
  42.7 6.0 %collective-permute-start.10 = (bf16[32,896]{1,0:T(8,128)(2,1)S(1)}, bf16[32,896]{1,0:T(8,128)(2,1)S(1)}, u32[]{:S(2)}, u32[]{:S(2)}) collective-permute-start(bf16[32,896]{1,0:T(8,128)(2,1)S(1)} %get-tuple-element.5), channel_id=1, source_target_pairs={{0,12},{4,8},{8,4},{12,0},{1,13},{5,9},{9,5},{13,1},{2,14},{6,10},... | collective-permute-start | bytes 172040 | tf_op jit(solution)/shard_map/ppermute | solution.py:8
  73.5 5.4 %collective-permute-start.17 = (bf16[8,3584]{1,0:T(8,128)(2,1)S(1)}, bf16[8,3584]{1,0:T(8,128)(2,1)S(1)}, u32[]{:S(2)}, u32[]{:S(2)}) collective-permute-start(bf16[8,3584]{1,0:T(8,128)(2,1)S(1)} %get-tuple-element.6), channel_id=1, source_target_pairs={{0,4},{4,0},{8,12},{12,8},{1,5},{5,1},{9,13},{13,9},{2,6},{6,2},{1... | collective-permute-start | bytes 172040 | tf_op jit(solution)/shard_map/ppermute | solution.py:8
  73.6 5.3 %collective-permute-start.18 = (bf16[8,3584]{1,0:T(8,128)(2,1)S(1)}, bf16[8,3584]{1,0:T(8,128)(2,1)S(1)}, u32[]{:S(2)}, u32[]{:S(2)}) collective-permute-start(bf16[8,3584]{1,0:T(8,128)(2,1)S(1)} %get-tuple-element.8), channel_id=1, source_target_pairs={{0,8},{4,12},{8,0},{12,4},{1,9},{5,13},{9,1},{13,5},{2,10},{6,14},... | collective-permute-start | bytes 172040 | tf_op jit(solution)/shard_map/ppermute | solution.py:8
  75.9 6.0 %collective-permute-start.19 = (bf16[8,3584]{1,0:T(8,128)(2,1)S(1)}, bf16[8,3584]{1,0:T(8,128)(2,1)S(1)}, u32[]{:S(2)}, u32[]{:S(2)}) collective-permute-start(bf16[8,3584]{1,0:T(8,128)(2,1)S(1)} %get-tuple-element.7), channel_id=1, source_target_pairs={{0,12},{4,8},{8,4},{12,0},{1,13},{5,9},{9,5},{13,1},{2,14},{6,10},... | collective-permute-start | bytes 172040 | tf_op jit(solution)/shard_map/ppermute | solution.py:8
  81.9 1.3 %collective-permute-start.20 = (bf16[8,3584]{1,0:T(8,128)(2,1)S(1)}, bf16[8,3584]{1,0:T(8,128)(2,1)S(1)}, u32[]{:S(2)}, u32[]{:S(2)}) collective-permute-start(bf16[8,3584]{1,0:T(8,128)(2,1)S(1)} %get-tuple-element.2), channel_id=1, source_target_pairs={{0,1},{1,0},{2,3},{3,2},{4,5},{5,4},{6,7},{7,6},{8,9},{9,8},{10,11... | collective-permute-start | bytes 172040 | tf_op jit(solution)/shard_map/ppermute | solution.py:8
  83.2 4.2 %collective-permute-start.21 = (bf16[8,3584]{1,0:T(8,128)(2,1)S(1)}, bf16[8,3584]{1,0:T(8,128)(2,1)S(1)}, u32[]{:S(2)}, u32[]{:S(2)}) collective-permute-start(bf16[8,3584]{1,0:T(8,128)(2,1)S(1)} %fusion.27), channel_id=1, source_target_pairs={{0,2},{1,3},{2,0},{3,1},{4,6},{5,7},{6,4},{7,5},{8,10},{9,11},{10,... | collective-permute-start | bytes 172040 | tf_op jit(solution)/shard_map/ppermute | solution.py:8

commit v2 on v1

--- a/solution.py
+++ b/solution.py
@@ -1,7 +1,17 @@
+import functools
+
 import jax
 import jax.numpy as jnp
 from jax import lax
+from jax.experimental import pallas as pl
+from jax.experimental.pallas import tpu as pltpu
 from jax.sharding import PartitionSpec as P
+
+LANES = 128
+ROWS = 8
+VMEM = pl.BlockSpec(memory_space=pltpu.VMEM)
+SMEM = pl.BlockSpec(memory_space=pltpu.SMEM)
+FLOPS = (2 * 10**10, 2 * 10**10, 2 * 10**10, 2 * 10**10, 10**10)
 
 
 def swap(x, axis, size, step):
@@ -52,7 +62,7 @@
     return per_head.reshape(per_head.shape[0], per_head.shape[1] * per_head.shape[2])
 
 
-def shards(
+def plain_shards(
     residual,
     query_latent,
     query_rope,
@@ -108,6 +118,291 @@
     return own_mid, mixed
 
 
+def call(body, outs, *args, limit, scratch=(), flops=None, specs=None):
+    estimate = None
+    if flops is not None:
+        estimate = pl.CostEstimate(flops=flops, bytes_accessed=1 << 20, transcendentals=0)
+    return pl.pallas_call(
+        body,
+        out_shape=outs,
+        in_specs=[VMEM] * len(args) if specs is None else specs,
+        out_specs=jax.tree.map(lambda _: VMEM, outs),
+        scratch_shapes=list(scratch),
+        compiler_params=pltpu.CompilerParams(vmem_limit_bytes=limit),
+        cost_estimate=estimate,
+    )(*args)
+
+
+def bf16(*shape):
+    return jax.ShapeDtypeStruct(shape, jnp.bfloat16)
+
+
+def f32(*shape):
+    return jax.ShapeDtypeStruct(shape, jnp.float32)
+
+
+def dot(a, b):
+    return jnp.dot(a, b, preferred_element_type=jnp.float32)
+
+
+def dot_t(a, b):
+    return lax.dot_general(a, b, (((1,), (1,)), ((), ())), preferred_element_type=jnp.float32)
+
+
+def rows_of(x, first, second):
+    return x.astype(jnp.float32).reshape(first * second, x.shape[2]).astype(x.dtype)
+
+
+def attend_kernel(scale, *refs):
+    sources, (heads_ref, res_out_ref, table_ref), held, sems = refs[:8], refs[8:11], refs[11:19], refs[19]
+    copies = [
+        pltpu.make_async_copy(source, place, sems.at[i])
+        for i, (source, place) in enumerate(zip(sources, held))
+    ]
+    for copy in copies:
+        copy.start()
+    ql_ref, cl_ref, qr_ref, cr_ref, av_ref, res_ref, routes_ref, weights_ref = held
+    t, h, _ = ql_ref.shape
+    c = cl_ref.shape[1]
+    vdim = av_ref.shape[2]
+    for copy in copies[:4]:
+        copy.wait()
+    cache = rows_of(cl_ref[...], t, c)
+    scores = dot_t(rows_of(ql_ref[...], t, h), cache)
+    scores = scores + dot_t(rows_of(qr_ref[...], t, h), rows_of(cr_ref[...], t, c))
+    row_t = lax.broadcasted_iota(jnp.int32, (t * h, t * c), 0) // h
+    col_t = lax.broadcasted_iota(jnp.int32, (t * h, t * c), 1) // c
+    scores = jnp.where(row_t == col_t, scores * scale, -jnp.inf)
+    top = jnp.max(scores, axis=-1, keepdims=True)
+    exps = jnp.exp(scores - top)
+    probs = (exps / jnp.sum(exps, axis=-1, keepdims=True)).astype(jnp.bfloat16)
+    latent = dot(probs, cache).astype(jnp.bfloat16)
+    to_row = lax.broadcasted_iota(jnp.int32, (t * h, t * h), 0)
+    from_row = lax.broadcasted_iota(jnp.int32, (t * h, t * h), 1)
+    order = (to_row // t == from_row % h) & (to_row % t == from_row // h)
+    by_head = dot(jnp.where(order, 1.0, 0.0).astype(jnp.bfloat16), latent)
+    for copy in copies[4:]:
+        copy.wait()
+    for i in range(h):
+        out = dot(by_head[i * t : (i + 1) * t].astype(jnp.bfloat16), av_ref[i])
+        heads_ref[:, i * vdim : (i + 1) * vdim] = out.astype(jnp.bfloat16)
+    res_out_ref[...] = res_ref[...]
+    lane = lax.broadcasted_iota(jnp.int32, (t, LANES), 1)
+    table = jnp.zeros((t, LANES), jnp.float32)
+    for k in range(routes_ref.shape[1]):
+        named = lane == routes_ref[:, k : k + 1]
+        table = jnp.where(named, weights_ref[:, k : k + 1], table)
+    high = table.astype(jnp.bfloat16).astype(jnp.float32)
+    low = pltpu.roll(table - high, LANES // 2, 1)
+    table_ref[...] = jnp.where(lane < LANES // 2, high, low).astype(jnp.bfloat16)
+
+
+def pack_kernel(me_ref, heads_ref, res_ref, table_ref, *msgs):
+    cols = res_ref.shape[1] // len(msgs)
+    width = heads_ref.shape[1]
+    me = me_ref[0]
+    for step, msg in enumerate(msgs):
+        start = pl.multiple_of((me ^ step) * cols, LANES)
+        msg[:, :width] = heads_ref[...]
+        msg[:, width : width + cols] = res_ref[:, pl.ds(start, cols)]
+        msg[:, width + cols :] = table_ref[...]
+
+
+def stacked(refs, first, last):
+    blocks = [ref[:, first:last].astype(jnp.float32) for ref in refs]
+    return jnp.concatenate(blocks, axis=0)
+
+
+def project_kernel(proj_ref, *refs):
+    *msgs, out_ref, res_ref, table_ref = refs
+    width = proj_ref.shape[0]
+    cols = proj_ref.shape[1]
+    heads = stacked(msgs, 0, width).astype(jnp.bfloat16)
+    out_ref[...] = dot(heads, proj_ref[...]).astype(jnp.bfloat16)
+    res_ref[...] = stacked(msgs, width, width + cols)
+    table_ref[...] = stacked(msgs, width + cols, width + cols + LANES)
+
+
+def add_kernel(a_ref, b_ref, out_ref):
+    total = a_ref[...].astype(jnp.float32) + b_ref[...].astype(jnp.float32)
+    out_ref[...] = total.astype(out_ref.dtype)
+
+
+def mid_kernel(a_ref, b_ref, res_ref, out_ref):
+    total = a_ref[...].astype(jnp.float32) + b_ref[...].astype(jnp.float32)
+    attention = total.astype(jnp.bfloat16).astype(jnp.float32)
+    out_ref[...] = (res_ref[...] + attention).astype(jnp.bfloat16)
+
+
+def expert_kernel(experts, me_ref, table_ref, gain_ref, wg_ref, wu_ref, wd_ref, *refs):
+    n = (len(refs) - 3) // 2
+    mids, (own_ref, total_ref), outs, (mid_ref, sum_ref) = refs[:n], refs[n : n + 2], refs[n + 2 : -2], refs[-2:]
+    tokens, cols = mids[0].shape
+    rows = tokens // n
+    me = me_ref[0]
+    squares = jnp.zeros((tokens, 1), jnp.float32)
+    for k in range(n):
+        got = mids[k][...].astype(jnp.float32)
+        block = jnp.concatenate([got[(i ^ k) * rows : (i ^ k) * rows + rows] for i in range(n)], axis=0)
+        squares = squares + jnp.sum(block * block, axis=-1, keepdims=True)
+        mid_ref[:, pl.ds(pl.multiple_of((me ^ k) * cols, LANES), cols)] = block
+    inverse = lax.rsqrt(squares / (n * cols) + 1e-06)
+    own_ref[...] = mid_ref[:rows].astype(jnp.bfloat16)
+    normed = (mid_ref[...] * inverse * gain_ref[...].reshape(1, n * cols)).astype(jnp.bfloat16)
+    lane = lax.broadcasted_iota(jnp.int32, (tokens, LANES), 1) % (LANES // 2)
+    for e in range(experts):
+        gate = dot(normed, wg_ref[e])
+        up = dot(normed, wu_ref[e])
+        weight = jnp.sum(
+            jnp.where(lane == me * experts + e, table_ref[...], 0.0), axis=1, keepdims=True
+        )
+        hidden = gate / (1.0 + jnp.exp(-gate)) * up * weight
+        hidden = jnp.where(weight != 0.0, hidden, 0.0).astype(jnp.bfloat16)
+        down = dot(hidden, wd_ref[e])
+        if e == 0:
+            sum_ref[...] = down
+        else:
+            sum_ref[...] += down
+    total_ref[...] = sum_ref[:rows]
+    for k in range(1, n):
+        outs[k - 1][...] = sum_ref[k * rows : (k + 1) * rows].astype(jnp.bfloat16)
+
+
+def join_kernel(total_ref, *refs):
+    *got, out_ref = refs
+    total = total_ref[...]
+    for ref in got:
+        total = total + ref[...].astype(jnp.float32)
+    out_ref[...] = total.astype(jnp.bfloat16)
+
+
+def shards(
+    residual,
+    query_latent,
+    query_rope,
+    cache_latent,
+    cache_rope,
+    absorb_value,
+    out_proj,
+    norm_gain,
+    routes,
+    route_weights,
+    w_gate,
+    w_up,
+    w_down,
+):
+    args = (
+        residual,
+        query_latent,
+        query_rope,
+        cache_latent,
+        cache_rope,
+        absorb_value,
+        out_proj,
+        norm_gain,
+        routes,
+        route_weights,
+        w_gate,
+        w_up,
+        w_down,
+    )
+    n = lax.axis_size("expert")
+    head_n = lax.axis_size("head")
+    rows, model_d = residual.shape
+    width, cols = out_proj.shape
+    experts = w_gate.shape[0]
+    tokens = rows * n
+    fits = rows == ROWS and cols % LANES == 0 and n & (n - 1) == 0 and head_n == 4
+    if not fits or experts * n > LANES // 2 or width % LANES:
+        return plain_shards(*args)
+    scale = (absorb_value.shape[2] + query_rope.shape[2]) ** (-0.5)
+    me = lax.axis_index("expert").astype(jnp.int32).reshape(1)
+
+    def in_vmem(x):
+        return pltpu.with_memory_space_constraint(x, pltpu.VMEM)
+
+    inputs = [
+        query_latent,
+        cache_latent,
+        query_rope,
+        cache_rope,
+        absorb_value,
+        residual,
+        routes,
+        route_weights,
+    ]
+    local = call(
+        functools.partial(attend_kernel, scale),
+        [bf16(rows, width), bf16(rows, model_d), bf16(rows, LANES)],
+        *[pltpu.with_memory_space_constraint(x, pltpu.HBM) for x in inputs],
+        limit=6 << 20,
+        scratch=[pltpu.VMEM(x.shape, x.dtype) for x in inputs] + [pltpu.SemaphoreType.DMA((len(inputs),))],
+        specs=[pl.BlockSpec(memory_space=pltpu.HBM)] * len(inputs),
+    )
+    msgs = call(
+        pack_kernel,
+        [bf16(rows, width + cols + LANES)] * n,
+        me,
+        *local,
+        limit=2 << 20,
+        specs=[SMEM] + [VMEM] * 3,
+        flops=FLOPS[0],
+    )
+    got = [msgs[0]] + [swap(msgs[k], "expert", n, k) for k in range(1, n)]
+    partial, res, table = call(
+        project_kernel,
+        [bf16(tokens, cols), f32(tokens, cols), f32(tokens, LANES)],
+        in_vmem(out_proj),
+        *got,
+        limit=4 << 20,
+        flops=FLOPS[1],
+    )
+    pair = call(
+        add_kernel,
+        bf16(tokens, cols),
+        partial,
+        swap(partial, "head", head_n, 1),
+        limit=2 << 20,
+        flops=FLOPS[2],
+    )
+    mid = call(
+        mid_kernel,
+        bf16(tokens, cols),
+        pair,
+        swap(pair, "head", head_n, 2),
+        res,
+        limit=2 << 20,
+        flops=FLOPS[3],
+    )
+    mids = [mid] + [swap(mid, "expert", n, k) for k in range(1, n)]
+    own_mid, own, *parts = call(
+        functools.partial(expert_kernel, experts),
+        [bf16(rows, model_d), f32(rows, model_d)] + [bf16(rows, model_d)] * (n - 1),
+        me,
+        table,
+        norm_gain,
+        in_vmem(w_gate),
+        in_vmem(w_up),
+        in_vmem(w_down),
+        *mids,
+        limit=8 << 20,
+        scratch=[pltpu.VMEM((tokens, model_d), jnp.float32)] * 2,
+        specs=[SMEM] + [VMEM] * (5 + n),
+        flops=FLOPS[4],
+    )
+    back = [swap(parts[k - 1], "expert", n, k) for k in range(1, n)]
+    mixed = call(join_kernel, bf16(rows, model_d), own, *back, limit=2 << 20)
+    for step in (1, 2):
+        mixed = call(
+            add_kernel,
+            bf16(rows, model_d),
+            mixed,
+            swap(mixed, "head", head_n, step),
+            limit=2 << 20,
+        )
+    return own_mid, mixed
+
+
 def solution(mesh):
     in_specs = (
         P(("groups", "expert"), None),

time: 88.5 us -> 53.1 us (0.60)
  matrix products: 27.8 us -> 0 us
  Pallas kernels: 0 us -> 12.3 us
  starting transfers between devices: 28 us -> 17.8 us
  waiting for transfers between devices: 23.8 us -> 19.4 us
  local copies, waits for them, and re-layouts: 6.22 us -> 2.73 us
  other arithmetic: 1.38 us -> 0.01 us
    dot_general x7 -> x0, matrix products: 27.8 us -> none  [the longest x1 14.6 us: shards(): jnp.einsum('etf,efd->td', hidden, w_down, preferred_element_type=jnp.floa...]
    pallas_call x0 -> x9, Pallas kernels: none -> 12.3 us  [call(): pl.pallas_call(body, out_shape=outs, in_specs=[VMEM] * len(args) if specs...]
    ppermute x22 -> x13, starting transfers between devices: 28 us -> 17.8 us  [swap(): return lax.ppermute(x, axis, [(s, s ^ step) for s in range(size)])]
    ppermute x22 -> x13, waiting for transfers between devices: 23.8 us -> 19.4 us  [swap(): return lax.ppermute(x, axis, [(s, s ^ step) for s in range(size)])]
    dynamic_update_slice x19 -> x0, local copies, waits for them, and re-layouts: 2.98 us -> none  [the longest x16 2.06 us: gather_rows(): lax.dynamic_update_index_in_dim(out, swap(x, axis, size, step), me ^ step...]
    unnamed x5 -> x28, local copies, waits for them, and re-layouts: 0.05 us -> 2.73 us
    broadcast_in_dim x15 -> x0, local copies, waits for them, and re-layouts: 2.19 us -> none  [the longest x2 1.54 us: gather_rows(): out = lax.dynamic_update_index_in_dim(out, x, me, 0)]
  transfers between devices with their start and end apart: 22 -> 13, of which waited for: 11 -> 10; matrix products, arithmetic and copies ran while one was open for 5% -> 0% of each run, Pallas kernels for 0% -> 0%
where the time goes in v2:
time: 53.1 us; the launch traced here: 53 us
  waiting for transfers between devices  19.4 us (37%)
  starting transfers between devices  17.8 us (34%)
  Pallas kernels  12.3 us (23%)
  local copies, waits for them, and re-layouts  2.73 us (5%)
  between operations  0.82 us (2%)
    ppermute x13, waiting for transfers between devices, swap(): return lax.ppermute(x, axis, [(s, s ^ step) for s in range(size)])  19.4 us
    ppermute x13, starting transfers between devices, swap(): return lax.ppermute(x, axis, [(s, s ^ step) for s in range(size)])  17.8 us
    pallas_call x9, Pallas kernels, call(): pl.pallas_call(body, out_shape=outs, in_specs=[VMEM] * len(args) if specs...  12.3 us
    unnamed x28, local copies, waits for them, and re-layouts  2.73 us
  transfers between devices with their start and end apart: 13, of which 10 were waited for; matrix products, arithmetic and copies ran while one was open for 0% of the time, Pallas kernels for 0%

profile of v2, /device:TPU:0, one launch (start us, length us, event | category | flops | bytes accessed | tf_op | source)
XLA Modules:
  0.0 53.0 jit_solution(5047392876580576843)
XLA Ops:
  0.6 2.1 %shard_map.140 = (bf16[8,1024]{1,0:T(8,128)(2,1)S(1)}, bf16[8,3584]{1,0:T(8,128)(2,1)S(1)}, bf16[8,128]{1,0:T(8,128)(2,1)S(1)}) custom-call(bf16[8,8,512]{2,1,0:T(8,128)(2,1)} %refs_0_.1, bf16[8,32,512]{2,1,0:T(8,128)(2,1)} %refs_1_.1, bf16[8,8,64]{2,1,0:T(8,128)(2,1)} %refs_2_.1, bf16[8,32,64]{2,1,0:T(8,128)(2,1)} %refs_3_.1, bf16[8,512,128]{2,1,0:T(8,128)(2,1)} %refs_4_.1, ...), custom_call_target="tpu_custom_call" | custom-call | tf_op jit(solution)/shard_map/pallas_call | solution.py:125
  2.8 3.1 %collective-permute-start = (bf16[8,2048]{1,0:T(8,128)(2,1)S(1)}, bf16[8,2048]{1,0:T(8,128)(2,1)S(1)}, u32[]{:S(2)}, u32[]{:S(2)}) collective-permute-start(bf16[8,2048]{1,0:T(8,128)(2,1)S(1)} %get-tuple-element.21), channel_id=1, source_target_pairs={{0,4},{4,0},{8,12},{12,8},{1,5},{5,1},{9,13},{13,9},{2,6},{6,2},{1... | collective-permute-start | bytes 98312 | tf_op jit(solution)/shard_map/ppermute | solution.py:18
  5.9 2.6 %collective-permute-start.1 = (bf16[8,2048]{1,0:T(8,128)(2,1)S(1)}, bf16[8,2048]{1,0:T(8,128)(2,1)S(1)}, u32[]{:S(2)}, u32[]{:S(2)}) collective-permute-start(bf16[8,2048]{1,0:T(8,128)(2,1)S(1)} %get-tuple-element.22), channel_id=1, source_target_pairs={{0,8},{4,12},{8,0},{12,4},{1,9},{5,13},{9,1},{13,5},{2,10},{6,14},... | collective-permute-start | bytes 98312 | tf_op jit(solution)/shard_map/ppermute | solution.py:18
  8.5 2.8 %collective-permute-done.1.refs_2_ = bf16[8,2048]{1,0:T(8,128)(2,1)S(1)} collective-permute-done((bf16[8,2048]{1,0:T(8,128)(2,1)S(1)}, bf16[8,2048]{1,0:T(8,128)(2,1)S(1)}, u32[]{:S(2)}, u32[]{:S(2)}) %collective-permute-start.1) | collective-permute-done | bytes 32800 | tf_op jit(solution)/shard_map/ppermute | solution.py:18
  11.3 2.9 %collective-permute-done.2.refs_3_ = bf16[8,2048]{1,0:T(8,128)(2,1)S(1)} collective-permute-done((bf16[8,2048]{1,0:T(8,128)(2,1)S(1)}, bf16[8,2048]{1,0:T(8,128)(2,1)S(1)}, u32[]{:S(2)}, u32[]{:S(2)}) %collective-permute-start.2) | collective-permute-done | bytes 32800 | tf_op jit(solution)/shard_map/ppermute | solution.py:18
  14.7 1.2 %collective-permute-done.3.b_ref = bf16[32,896]{1,0:T(8,128)(2,1)S(1)} collective-permute-done((bf16[32,896]{1,0:T(8,128)(2,1)S(1)}, bf16[32,896]{1,0:T(8,128)(2,1)S(1)}, u32[]{:S(2)}, u32[]{:S(2)}) %collective-permute-start.3) | collective-permute-done | bytes 57376 | tf_op jit(solution)/shard_map/ppermute | solution.py:18
  16.0 1.6 %collective-permute-start.4 = (bf16[32,896]{1,0:T(8,128)(2,1)S(1)}, bf16[32,896]{1,0:T(8,128)(2,1)S(1)}, u32[]{:S(2)}, u32[]{:S(2)}) collective-permute-start(bf16[32,896]{1,0:T(8,128)(2,1)S(1)} %shard_map.143.a_ref), channel_id=1, source_target_pairs={{0,2},{1,3},{2,0},{3,1},{4,6},{5,7},{6,4},{7,5},{8,10},{9,11},{10,... | collective-permute-start | bytes 172040 | tf_op jit(solution)/shard_map/ppermute | solution.py:18
  17.6 2.7 %collective-permute-done.4.b_ref = bf16[32,896]{1,0:T(8,128)(2,1)S(1)} collective-permute-done((bf16[32,896]{1,0:T(8,128)(2,1)S(1)}, bf16[32,896]{1,0:T(8,128)(2,1)S(1)}, u32[]{:S(2)}, u32[]{:S(2)}) %collective-permute-start.4) | collective-permute-done | bytes 57376 | tf_op jit(solution)/shard_map/ppermute | solution.py:18
  20.8 3.9 %collective-permute-start.5 = (bf16[32,896]{1,0:T(8,128)(2,1)S(1)}, bf16[32,896]{1,0:T(8,128)(2,1)S(1)}, u32[]{:S(2)}, u32[]{:S(2)}) collective-permute-start(bf16[32,896]{1,0:T(8,128)(2,1)S(1)} %shard_map.144.refs_0_), channel_id=1, source_target_pairs={{0,4},{4,0},{8,12},{12,8},{1,5},{5,1},{9,13},{13,9},{2,6},{6,2},{1... | collective-permute-start | bytes 172040 | tf_op jit(solution)/shard_map/ppermute | solution.py:18
  24.8 1.7 %collective-permute-done.7.refs_3_ = bf16[32,896]{1,0:T(8,128)(2,1)S(1)} collective-permute-done((bf16[32,896]{1,0:T(8,128)(2,1)S(1)}, bf16[32,896]{1,0:T(8,128)(2,1)S(1)}, u32[]{:S(2)}, u32[]{:S(2)}) %collective-permute-start.7) | collective-permute-done | bytes 57376 | tf_op jit(solution)/shard_map/ppermute | solution.py:18
  26.4 0.6 %collective-permute-done.5.refs_1_ = bf16[32,896]{1,0:T(8,128)(2,1)S(1)} collective-permute-done((bf16[32,896]{1,0:T(8,128)(2,1)S(1)}, bf16[32,896]{1,0:T(8,128)(2,1)S(1)}, u32[]{:S(2)}, u32[]{:S(2)}) %collective-permute-start.5) | collective-permute-done | bytes 57376 | tf_op jit(solution)/shard_map/ppermute | solution.py:18
  27.1 0.7 %slice-done.10 = s8[4194304]{0:T(1024)(128)(4,1)S(1)} async-done(((s8[14680064]{0:T(1024)(128)(4,1)}), s8[4194304]{0:T(1024)(128)(4,1)S(1)}, s32[]{:S(2)}) %slice-start.10) | async-done | bytes 4194328
  27.8 0.8 %slice-done.3 = s8[2097152]{0:T(1024)(128)(4,1)S(1)} async-done(((s8[14680064]{0:T(1024)(128)(4,1)}), s8[2097152]{0:T(1024)(128)(4,1)S(1)}, s32[]{:S(2)}) %slice-start.3) | async-done | bytes 2097176
  28.6 0.6 %slice-done.7 = s8[2097152]{0:T(1024)(128)(4,1)S(1)} async-done(((s8[14680064]{0:T(1024)(128)(4,1)}), s8[2097152]{0:T(1024)(128)(4,1)S(1)}, s32[]{:S(2)}) %slice-start.7) | async-done | bytes 2097176
  29.2 0.6 %slice-done.11 = s8[2097152]{0:T(1024)(128)(4,1)S(1)} async-done(((s8[14680064]{0:T(1024)(128)(4,1)}), s8[2097152]{0:T(1024)(128)(4,1)S(1)}, s32[]{:S(2)}) %slice-start.11) | async-done | bytes 2097176
  29.8 9.0 %shard_map.145 = (bf16[8,3584]{1,0:T(8,128)(2,1)}, f32[8,3584]{1,0:T(8,128)S(1)}, bf16[8,3584]{1,0:T(8,128)(2,1)S(1)}, bf16[8,3584]{1,0:T(8,128)(2,1)S(1)}, bf16[8,3584]{1,0:T(8,128)(2,1)S(1)}) custom-call(s32[1]{0:T(128)} %bitcast.me_ref, f32[32,128]{1,0:T(8,128)S(1)} %get-tuple-element.24.table_ref, f32[3584]{0:T(1024)S(1)} %copy-done, ...), custom_call_target="tpu_custom_call" | custom-call | flops 10000000000 | bytes 1048576 | tf_op jit(solution)/shard_map/pallas_call | solution.py:125
  38.8 0.9 %collective-permute-start.9 = (bf16[8,3584]{1,0:T(8,128)(2,1)S(1)}, bf16[8,3584]{1,0:T(8,128)(2,1)S(1)}, u32[]{:S(2)}, u32[]{:S(2)}) collective-permute-start(bf16[8,3584]{1,0:T(8,128)(2,1)S(1)} %get-tuple-element.30), channel_id=1, source_target_pairs={{0,8},{4,12},{8,0},{12,4},{1,9},{5,13},{9,1},{13,5},{2,10},{6,14},... | collective-permute-start | bytes 172040 | tf_op jit(solution)/shard_map/ppermute | solution.py:18
  39.7 3.5 %collective-permute-start.10 = (bf16[8,3584]{1,0:T(8,128)(2,1)S(1)}, bf16[8,3584]{1,0:T(8,128)(2,1)S(1)}, u32[]{:S(2)}, u32[]{:S(2)}) collective-permute-start(bf16[8,3584]{1,0:T(8,128)(2,1)S(1)} %get-tuple-element.31), channel_id=1, source_target_pairs={{0,12},{4,8},{8,4},{12,0},{1,13},{5,9},{9,5},{13,1},{2,14},{6,10},... | collective-permute-start | bytes 172040 | tf_op jit(solution)/shard_map/ppermute | solution.py:18
  43.2 0.7 %collective-permute-done.8.refs_0_ = bf16[8,3584]{1,0:T(8,128)(2,1)S(1)} collective-permute-done((bf16[8,3584]{1,0:T(8,128)(2,1)S(1)}, bf16[8,3584]{1,0:T(8,128)(2,1)S(1)}, u32[]{:S(2)}, u32[]{:S(2)}) %collective-permute-start.8) | collective-permute-done | bytes 57376 | tf_op jit(solution)/shard_map/ppermute | solution.py:18
  43.8 2.9 %collective-permute-done.9.refs_1_ = bf16[8,3584]{1,0:T(8,128)(2,1)S(1)} collective-permute-done((bf16[8,3584]{1,0:T(8,128)(2,1)S(1)}, bf16[8,3584]{1,0:T(8,128)(2,1)S(1)}, u32[]{:S(2)}, u32[]{:S(2)}) %collective-permute-start.9) | collective-permute-done | bytes 57376 | tf_op jit(solution)/shard_map/ppermute | solution.py:18
  46.8 1.2 %collective-permute-done.11.b_ref = bf16[8,3584]{1,0:T(8,128)(2,1)S(1)} collective-permute-done((bf16[8,3584]{1,0:T(8,128)(2,1)S(1)}, bf16[8,3584]{1,0:T(8,128)(2,1)S(1)}, u32[]{:S(2)}, u32[]{:S(2)}) %collective-permute-start.11) | collective-permute-done | bytes 57376 | tf_op jit(solution)/shard_map/ppermute | solution.py:18
  48.1 1.6 %collective-permute-start.12 = (bf16[8,3584]{1,0:T(8,128)(2,1)S(1)}, bf16[8,3584]{1,0:T(8,128)(2,1)S(1)}, u32[]{:S(2)}, u32[]{:S(2)}) collective-permute-start(bf16[8,3584]{1,0:T(8,128)(2,1)S(1)} %shard_map.147.a_ref), channel_id=1, source_target_pairs={{0,2},{1,3},{2,0},{3,1},{4,6},{5,7},{6,4},{7,5},{8,10},{9,11},{10,... | collective-permute-start | bytes 172040 | tf_op jit(solution)/shard_map/ppermute | solution.py:18
  49.6 2.7 %collective-permute-done.12.b_ref = bf16[8,3584]{1,0:T(8,128)(2,1)S(1)} collective-permute-done((bf16[8,3584]{1,0:T(8,128)(2,1)S(1)}, bf16[8,3584]{1,0:T(8,128)(2,1)S(1)}, u32[]{:S(2)}, u32[]{:S(2)}) %collective-permute-start.12) | collective-permute-done | bytes 57376 | tf_op jit(solution)/shard_map/ppermute | solution.py:18
  52.3 0.6 %shard_map.148 = bf16[8,3584]{1,0:T(8,128)(2,1)} custom-call(bf16[8,3584]{1,0:T(8,128)(2,1)S(1)} %shard_map.147.a_ref, bf16[8,3584]{1,0:T(8,128)(2,1)S(1)} %collective-permute-done.12.b_ref), custom_call_target="tpu_custom_call" | custom-call | tf_op jit(solution)/shard_map/pallas_call | solution.py:125
  (42 shorter events, 1.3 us)
Async XLA Ops:
  2.8 11.4 %copy-start.1 = (bf16[1024,896]{1,0:T(8,128)(2,1)S(1)}, bf16[1024,896]{1,0:T(8,128)(2,1)}, u32[]{:S(2)}) copy-start(bf16[1024,896]{1,0:T(8,128)(2,1)} %proj_ref.1) | copy-start | bytes 5505028
  2.8 5.7 %collective-permute-start = (bf16[8,2048]{1,0:T(8,128)(2,1)S(1)}, bf16[8,2048]{1,0:T(8,128)(2,1)S(1)}, u32[]{:S(2)}, u32[]{:S(2)}) collective-permute-start(bf16[8,2048]{1,0:T(8,128)(2,1)S(1)} %get-tuple-element.21), channel_id=1, source_target_pairs={{0,4},{4,0},{8,12},{12,8},{1,5},{5,1},{9,13},{13,9},{2,6},{6,2},{1... | collective-permute-start | bytes 98312 | tf_op jit(solution)/shard_map/ppermute | solution.py:18
  5.9 5.4 %collective-permute-start.1 = (bf16[8,2048]{1,0:T(8,128)(2,1)S(1)}, bf16[8,2048]{1,0:T(8,128)(2,1)S(1)}, u32[]{:S(2)}, u32[]{:S(2)}) collective-permute-start(bf16[8,2048]{1,0:T(8,128)(2,1)S(1)} %get-tuple-element.22), channel_id=1, source_target_pairs={{0,8},{4,12},{8,0},{12,4},{1,9},{5,13},{9,1},{13,5},{2,10},{6,14},... | collective-permute-start | bytes 98312 | tf_op jit(solution)/shard_map/ppermute | solution.py:18
  8.5 5.7 %collective-permute-start.2 = (bf16[8,2048]{1,0:T(8,128)(2,1)S(1)}, bf16[8,2048]{1,0:T(8,128)(2,1)S(1)}, u32[]{:S(2)}, u32[]{:S(2)}) collective-permute-start(bf16[8,2048]{1,0:T(8,128)(2,1)S(1)} %get-tuple-element.23), channel_id=1, source_target_pairs={{0,12},{4,8},{8,4},{12,0},{1,13},{5,9},{9,5},{13,1},{2,14},{6,10},... | collective-permute-start | bytes 98312 | tf_op jit(solution)/shard_map/ppermute | solution.py:18
  14.6 1.3 %collective-permute-start.3 = (bf16[32,896]{1,0:T(8,128)(2,1)S(1)}, bf16[32,896]{1,0:T(8,128)(2,1)S(1)}, u32[]{:S(2)}, u32[]{:S(2)}) collective-permute-start(bf16[32,896]{1,0:T(8,128)(2,1)S(1)} %get-tuple-element.25.a_ref), channel_id=1, source_target_pairs={{0,1},{1,0},{2,3},{3,2},{4,5},{5,4},{6,7},{7,6},{8,9},{9,8},{10,11... | collective-permute-start | bytes 172040 | tf_op jit(solution)/shard_map/ppermute | solution.py:18
  15.9 11.1 %slice-start = ((s8[14680064]{0:T(1024)(128)(4,1)}), s8[4194304]{0:T(1024)(128)(4,1)S(1)}, s32[]{:S(2)}) async-start(s8[14680064]{0:T(1024)(128)(4,1)} %bitcast.1), calls=%async_computation | async-start | bytes 8388608
  15.9 11.1 %slice-start.1 = ((s8[14680064]{0:T(1024)(128)(4,1)}), s8[4194304]{0:T(1024)(128)(4,1)S(1)}, s32[]{:S(2)}) async-start(s8[14680064]{0:T(1024)(128)(4,1)} %bitcast.1), calls=%async_computation.1 | async-start | bytes 8388608
  15.9 11.1 %slice-start.4 = ((s8[14680064]{0:T(1024)(128)(4,1)}), s8[4194304]{0:T(1024)(128)(4,1)S(1)}, s32[]{:S(2)}) async-start(s8[14680064]{0:T(1024)(128)(4,1)} %bitcast.3), calls=%async_computation.4 | async-start | bytes 8388608
  15.9 11.1 %slice-start.5 = ((s8[14680064]{0:T(1024)(128)(4,1)}), s8[4194304]{0:T(1024)(128)(4,1)S(1)}, s32[]{:S(2)}) async-start(s8[14680064]{0:T(1024)(128)(4,1)} %bitcast.3), calls=%async_computation.5 | async-start | bytes 8388608
  15.9 11.1 %slice-start.8 = ((s8[14680064]{0:T(1024)(128)(4,1)}), s8[4194304]{0:T(1024)(128)(4,1)S(1)}, s32[]{:S(2)}) async-start(s8[14680064]{0:T(1024)(128)(4,1)} %bitcast.5), calls=%async_computation.8 | async-start | bytes 8388608
  15.9 11.1 %slice-start.9 = ((s8[14680064]{0:T(1024)(128)(4,1)}), s8[4194304]{0:T(1024)(128)(4,1)S(1)}, s32[]{:S(2)}) async-start(s8[14680064]{0:T(1024)(128)(4,1)} %bitcast.5), calls=%async_computation.9 | async-start | bytes 8388608
  16.0 11.1 %slice-start.2 = ((s8[14680064]{0:T(1024)(128)(4,1)}), s8[4194304]{0:T(1024)(128)(4,1)S(1)}, s32[]{:S(2)}) async-start(s8[14680064]{0:T(1024)(128)(4,1)} %bitcast.1), calls=%async_computation.2 | async-start | bytes 8388608
  16.0 11.1 %slice-start.6 = ((s8[14680064]{0:T(1024)(128)(4,1)}), s8[4194304]{0:T(1024)(128)(4,1)S(1)}, s32[]{:S(2)}) async-start(s8[14680064]{0:T(1024)(128)(4,1)} %bitcast.3), calls=%async_computation.6 | async-start | bytes 8388608
  16.0 11.8 %slice-start.10 = ((s8[14680064]{0:T(1024)(128)(4,1)}), s8[4194304]{0:T(1024)(128)(4,1)S(1)}, s32[]{:S(2)}) async-start(s8[14680064]{0:T(1024)(128)(4,1)} %bitcast.5), calls=%async_computation.10 | async-start | bytes 8388608
  16.0 4.2 %collective-permute-start.4 = (bf16[32,896]{1,0:T(8,128)(2,1)S(1)}, bf16[32,896]{1,0:T(8,128)(2,1)S(1)}, u32[]{:S(2)}, u32[]{:S(2)}) collective-permute-start(bf16[32,896]{1,0:T(8,128)(2,1)S(1)} %shard_map.143.a_ref), channel_id=1, source_target_pairs={{0,2},{1,3},{2,0},{3,1},{4,6},{5,7},{6,4},{7,5},{8,10},{9,11},{10,... | collective-permute-start | bytes 172040 | tf_op jit(solution)/shard_map/ppermute | solution.py:18
  20.3 9.5 %copy-start = (f32[3584]{0:T(1024)S(1)}, f32[3584]{0:T(1024)}, u32[]{:S(2)}) copy-start(f32[3584]{0:T(1024)} %gain_ref.1) | copy-start | bytes 43012
  20.3 6.1 %collective-permute-start.7 = (bf16[32,896]{1,0:T(8,128)(2,1)S(1)}, bf16[32,896]{1,0:T(8,128)(2,1)S(1)}, u32[]{:S(2)}, u32[]{:S(2)}) collective-permute-start(bf16[32,896]{1,0:T(8,128)(2,1)S(1)} %shard_map.144.refs_0_), channel_id=1, source_target_pairs={{0,12},{4,8},{8,4},{12,0},{1,13},{5,9},{9,5},{13,1},{2,14},{6,10},... | collective-permute-start | bytes 172040 | tf_op jit(solution)/shard_map/ppermute | solution.py:18
  20.7 5.7 %collective-permute-start.6 = (bf16[32,896]{1,0:T(8,128)(2,1)S(1)}, bf16[32,896]{1,0:T(8,128)(2,1)S(1)}, u32[]{:S(2)}, u32[]{:S(2)}) collective-permute-start(bf16[32,896]{1,0:T(8,128)(2,1)S(1)} %shard_map.144.refs_0_), channel_id=1, source_target_pairs={{0,8},{4,12},{8,0},{12,4},{1,9},{5,13},{9,1},{13,5},{2,10},{6,14},... | collective-permute-start | bytes 172040 | tf_op jit(solution)/shard_map/ppermute | solution.py:18
  20.8 6.2 %collective-permute-start.5 = (bf16[32,896]{1,0:T(8,128)(2,1)S(1)}, bf16[32,896]{1,0:T(8,128)(2,1)S(1)}, u32[]{:S(2)}, u32[]{:S(2)}) collective-permute-start(bf16[32,896]{1,0:T(8,128)(2,1)S(1)} %shard_map.144.refs_0_), channel_id=1, source_target_pairs={{0,4},{4,0},{8,12},{12,8},{1,5},{5,1},{9,13},{13,9},{2,6},{6,2},{1... | collective-permute-start | bytes 172040 | tf_op jit(solution)/shard_map/ppermute | solution.py:18
  38.8 5.0 %collective-permute-start.8 = (bf16[8,3584]{1,0:T(8,128)(2,1)S(1)}, bf16[8,3584]{1,0:T(8,128)(2,1)S(1)}, u32[]{:S(2)}, u32[]{:S(2)}) collective-permute-start(bf16[8,3584]{1,0:T(8,128)(2,1)S(1)} %get-tuple-element.29), channel_id=1, source_target_pairs={{0,4},{4,0},{8,12},{12,8},{1,5},{5,1},{9,13},{13,9},{2,6},{6,2},{1... | collective-permute-start | bytes 172040 | tf_op jit(solution)/shard_map/ppermute | solution.py:18
  38.8 8.0 %collective-permute-start.9 = (bf16[8,3584]{1,0:T(8,128)(2,1)S(1)}, bf16[8,3584]{1,0:T(8,128)(2,1)S(1)}, u32[]{:S(2)}, u32[]{:S(2)}) collective-permute-start(bf16[8,3584]{1,0:T(8,128)(2,1)S(1)} %get-tuple-element.30), channel_id=1, source_target_pairs={{0,8},{4,12},{8,0},{12,4},{1,9},{5,13},{9,1},{13,5},{2,10},{6,14},... | collective-permute-start | bytes 172040 | tf_op jit(solution)/shard_map/ppermute | solution.py:18
  39.7 7.0 %collective-permute-start.10 = (bf16[8,3584]{1,0:T(8,128)(2,1)S(1)}, bf16[8,3584]{1,0:T(8,128)(2,1)S(1)}, u32[]{:S(2)}, u32[]{:S(2)}) collective-permute-start(bf16[8,3584]{1,0:T(8,128)(2,1)S(1)} %get-tuple-element.31), channel_id=1, source_target_pairs={{0,12},{4,8},{8,4},{12,0},{1,13},{5,9},{9,5},{13,1},{2,14},{6,10},... | collective-permute-start | bytes 172040 | tf_op jit(solution)/shard_map/ppermute | solution.py:18
  46.8 1.3 %collective-permute-start.11 = (bf16[8,3584]{1,0:T(8,128)(2,1)S(1)}, bf16[8,3584]{1,0:T(8,128)(2,1)S(1)}, u32[]{:S(2)}, u32[]{:S(2)}) collective-permute-start(bf16[8,3584]{1,0:T(8,128)(2,1)S(1)} %shard_map.146.a_ref), channel_id=1, source_target_pairs={{0,1},{1,0},{2,3},{3,2},{4,5},{5,4},{6,7},{7,6},{8,9},{9,8},{10,11... | collective-permute-start | bytes 172040 | tf_op jit(solution)/shard_map/ppermute | solution.py:18
  48.1 4.2 %collective-permute-start.12 = (bf16[8,3584]{1,0:T(8,128)(2,1)S(1)}, bf16[8,3584]{1,0:T(8,128)(2,1)S(1)}, u32[]{:S(2)}, u32[]{:S(2)}) collective-permute-start(bf16[8,3584]{1,0:T(8,128)(2,1)S(1)} %shard_map.147.a_ref), channel_id=1, source_target_pairs={{0,2},{1,3},{2,0},{3,1},{4,6},{5,7},{6,4},{7,5},{8,10},{9,11},{10,... | collective-permute-start | bytes 172040 | tf_op jit(solution)/shard_map/ppermute | solution.py:18
  (3 other events, 26.7 us)

commit v3 on v2

--- a/solution.py
+++ b/solution.py
@@ -10,8 +10,7 @@
 LANES = 128
 ROWS = 8
 VMEM = pl.BlockSpec(memory_space=pltpu.VMEM)
-SMEM = pl.BlockSpec(memory_space=pltpu.SMEM)
-FLOPS = (2 * 10**10, 2 * 10**10, 2 * 10**10, 2 * 10**10, 10**10)
+FLOPS = (8 * 10**10, 1, 1, 1, 10**10)
 
 
 def swap(x, axis, size, step):
@@ -197,10 +196,10 @@
     table_ref[...] = jnp.where(lane < LANES // 2, high, low).astype(jnp.bfloat16)
 
 
-def pack_kernel(me_ref, heads_ref, res_ref, table_ref, *msgs):
+def pack_kernel(heads_ref, res_ref, table_ref, *msgs):
     cols = res_ref.shape[1] // len(msgs)
     width = heads_ref.shape[1]
-    me = me_ref[0]
+    me = lax.axis_index("expert")
     for step, msg in enumerate(msgs):
         start = pl.multiple_of((me ^ step) * cols, LANES)
         msg[:, :width] = heads_ref[...]
@@ -215,6 +214,7 @@
 
 def project_kernel(proj_ref, *refs):
     *msgs, out_ref, res_ref, table_ref = refs
+    msgs = msgs[::-1]
     width = proj_ref.shape[0]
     cols = proj_ref.shape[1]
     heads = stacked(msgs, 0, width).astype(jnp.bfloat16)
@@ -234,12 +234,12 @@
     out_ref[...] = (res_ref[...] + attention).astype(jnp.bfloat16)
 
 
-def expert_kernel(experts, me_ref, table_ref, gain_ref, wg_ref, wu_ref, wd_ref, *refs):
+def expert_kernel(experts, table_ref, gain_ref, wg_ref, wu_ref, wd_ref, *refs):
     n = (len(refs) - 3) // 2
     mids, (own_ref, total_ref), outs, (mid_ref, sum_ref) = refs[:n], refs[n : n + 2], refs[n + 2 : -2], refs[-2:]
     tokens, cols = mids[0].shape
     rows = tokens // n
-    me = me_ref[0]
+    me = lax.axis_index("expert")
     squares = jnp.zeros((tokens, 1), jnp.float32)
     for k in range(n):
         got = mids[k][...].astype(jnp.float32)
@@ -249,16 +249,19 @@
     inverse = lax.rsqrt(squares / (n * cols) + 1e-06)
     own_ref[...] = mid_ref[:rows].astype(jnp.bfloat16)
     normed = (mid_ref[...] * inverse * gain_ref[...].reshape(1, n * cols)).astype(jnp.bfloat16)
+    copies = max(1, LANES // tokens)
+    normed = jnp.concatenate([normed] * copies, axis=0)
     lane = lax.broadcasted_iota(jnp.int32, (tokens, LANES), 1) % (LANES // 2)
     for e in range(experts):
-        gate = dot(normed, wg_ref[e])
-        up = dot(normed, wu_ref[e])
+        gate = dot(normed, wg_ref[e])[:tokens]
+        up = dot(normed, wu_ref[e])[:tokens]
         weight = jnp.sum(
             jnp.where(lane == me * experts + e, table_ref[...], 0.0), axis=1, keepdims=True
         )
         hidden = gate / (1.0 + jnp.exp(-gate)) * up * weight
         hidden = jnp.where(weight != 0.0, hidden, 0.0).astype(jnp.bfloat16)
-        down = dot(hidden, wd_ref[e])
+        hidden = jnp.concatenate([hidden] * copies, axis=0)
+        down = dot(hidden, wd_ref[e])[:tokens]
         if e == 0:
             sum_ref[...] = down
         else:
@@ -316,8 +319,6 @@
     if not fits or experts * n > LANES // 2 or width % LANES:
         return plain_shards(*args)
     scale = (absorb_value.shape[2] + query_rope.shape[2]) ** (-0.5)
-    me = lax.axis_index("expert").astype(jnp.int32).reshape(1)
-
     def in_vmem(x):
         return pltpu.with_memory_space_constraint(x, pltpu.VMEM)
 
@@ -342,13 +343,11 @@
     msgs = call(
         pack_kernel,
         [bf16(rows, width + cols + LANES)] * n,
-        me,
         *local,
         limit=2 << 20,
-        specs=[SMEM] + [VMEM] * 3,
         flops=FLOPS[0],
     )
-    got = [msgs[0]] + [swap(msgs[k], "expert", n, k) for k in range(1, n)]
+    got = [swap(msgs[k], "expert", n, k) for k in range(n - 1, 0, -1)] + [msgs[0]]
     partial, res, table = call(
         project_kernel,
         [bf16(tokens, cols), f32(tokens, cols), f32(tokens, LANES)],
@@ -378,7 +377,6 @@
     own_mid, own, *parts = call(
         functools.partial(expert_kernel, experts),
         [bf16(rows, model_d), f32(rows, model_d)] + [bf16(rows, model_d)] * (n - 1),
-        me,
         table,
         norm_gain,
         in_vmem(w_gate),
@@ -387,10 +385,9 @@
         *mids,
         limit=8 << 20,
         scratch=[pltpu.VMEM((tokens, model_d), jnp.float32)] * 2,
-        specs=[SMEM] + [VMEM] * (5 + n),
         flops=FLOPS[4],
     )
-    back = [swap(parts[k - 1], "expert", n, k) for k in range(1, n)]
+    back = [swap(parts[k - 1], "expert", n, k) for k in range(n - 1, 0, -1)]
     mixed = call(join_kernel, bf16(rows, model_d), own, *back, limit=2 << 20)
     for step in (1, 2):
         mixed = call(

time: 53.1 us -> 48.2 us (0.908)
  local copies, waits for them, and re-layouts: 2.73 us -> 0.03 us
  Pallas kernels: 12.3 us -> 10.9 us
  waiting for transfers between devices: 19.4 us -> 18.5 us
    unnamed x28 -> x10, local copies, waits for them, and re-layouts: 2.73 us -> 0.03 us
    pallas_call x9, Pallas kernels: 12.3 us -> 10.9 us  [call(): pl.pallas_call(body, out_shape=outs, in_specs=[VMEM] * len(args) if specs...]
    ppermute x13, waiting for transfers between devices: 19.4 us -> 18.5 us  [swap(): return lax.ppermute(x, axis, [(s, s ^ step) for s in range(size)])]
where the time goes in v3:
time: 48.2 us; the launch traced here: 48.1 us
  waiting for transfers between devices  18.5 us (38%)
  starting transfers between devices  17.8 us (37%)
  Pallas kernels  10.9 us (23%)
  between operations  0.76 us (2%)
    ppermute x13, waiting for transfers between devices, swap(): return lax.ppermute(x, axis, [(s, s ^ step) for s in range(size)])  18.5 us
    ppermute x13, starting transfers between devices, swap(): return lax.ppermute(x, axis, [(s, s ^ step) for s in range(size)])  17.8 us
    pallas_call x9, Pallas kernels, call(): pl.pallas_call(body, out_shape=outs, in_specs=[VMEM] * len(args) if specs...  10.9 us
  transfers between devices with their start and end apart: 13, of which 10 were waited for; matrix products, arithmetic and copies ran while one was open for 0% of the time, Pallas kernels for 0%

profile of v3, /device:TPU:0, one launch (start us, length us, event | category | flops | bytes accessed | tf_op | source)
XLA Modules:
  0.0 48.1 jit_solution(9379726353709371865)
XLA Ops:
  0.6 2.1 %shard_map.140 = (bf16[8,1024]{1,0:T(8,128)(2,1)S(1)}, bf16[8,3584]{1,0:T(8,128)(2,1)S(1)}, bf16[8,128]{1,0:T(8,128)(2,1)S(1)}) custom-call(bf16[8,8,512]{2,1,0:T(8,128)(2,1)} %refs_0_.1, bf16[8,32,512]{2,1,0:T(8,128)(2,1)} %refs_1_.1, bf16[8,8,64]{2,1,0:T(8,128)(2,1)} %refs_2_.1, bf16[8,32,64]{2,1,0:T(8,128)(2,1)} %refs_3_.1, bf16[8,512,128]{2,1,0:T(8,128)(2,1)} %refs_4_.1, ...), custom_call_target="tpu_custom_call" | custom-call | tf_op jit(solution)/shard_map/pallas_call | solution.py:124
  2.8 5.1 %collective-permute-start = (bf16[8,2048]{1,0:T(8,128)(2,1)S(1)}, bf16[8,2048]{1,0:T(8,128)(2,1)S(1)}, u32[]{:S(2)}, u32[]{:S(2)}) collective-permute-start(bf16[8,2048]{1,0:T(8,128)(2,1)S(1)} %get-tuple-element.20), channel_id=1, source_target_pairs={{0,12},{4,8},{8,4},{12,0},{1,13},{5,9},{9,5},{13,1},{2,14},{6,10},... | collective-permute-start | bytes 98312 | tf_op jit(solution)/shard_map/ppermute | solution.py:17
  8.0 0.6 %collective-permute-start.2 = (bf16[8,2048]{1,0:T(8,128)(2,1)S(1)}, bf16[8,2048]{1,0:T(8,128)(2,1)S(1)}, u32[]{:S(2)}, u32[]{:S(2)}) collective-permute-start(bf16[8,2048]{1,0:T(8,128)(2,1)S(1)} %get-tuple-element.22), channel_id=1, source_target_pairs={{0,4},{4,0},{8,12},{12,8},{1,5},{5,1},{9,13},{13,9},{2,6},{6,2},{1... | collective-permute-start | bytes 98312 | tf_op jit(solution)/shard_map/ppermute | solution.py:17
  8.6 1.3 %collective-permute-done.refs_0_ = bf16[8,2048]{1,0:T(8,128)(2,1)S(1)} collective-permute-done((bf16[8,2048]{1,0:T(8,128)(2,1)S(1)}, bf16[8,2048]{1,0:T(8,128)(2,1)S(1)}, u32[]{:S(2)}, u32[]{:S(2)}) %collective-permute-start) | collective-permute-done | bytes 32800 | tf_op jit(solution)/shard_map/ppermute | solution.py:17
  9.9 2.9 %collective-permute-done.1.refs_1_ = bf16[8,2048]{1,0:T(8,128)(2,1)S(1)} collective-permute-done((bf16[8,2048]{1,0:T(8,128)(2,1)S(1)}, bf16[8,2048]{1,0:T(8,128)(2,1)S(1)}, u32[]{:S(2)}, u32[]{:S(2)}) %collective-permute-start.1) | collective-permute-done | bytes 32800 | tf_op jit(solution)/shard_map/ppermute | solution.py:17
  12.8 0.4 shard_map.142
  13.3 1.2 %collective-permute-done.3.b_ref = bf16[32,896]{1,0:T(8,128)(2,1)S(1)} collective-permute-done((bf16[32,896]{1,0:T(8,128)(2,1)S(1)}, bf16[32,896]{1,0:T(8,128)(2,1)S(1)}, u32[]{:S(2)}, u32[]{:S(2)}) %collective-permute-start.3) | collective-permute-done | bytes 57376 | tf_op jit(solution)/shard_map/ppermute | solution.py:17
  14.5 1.6 %collective-permute-start.4 = (bf16[32,896]{1,0:T(8,128)(2,1)S(1)}, bf16[32,896]{1,0:T(8,128)(2,1)S(1)}, u32[]{:S(2)}, u32[]{:S(2)}) collective-permute-start(bf16[32,896]{1,0:T(8,128)(2,1)S(1)} %shard_map.143.a_ref), channel_id=1, source_target_pairs={{0,2},{1,3},{2,0},{3,1},{4,6},{5,7},{6,4},{7,5},{8,10},{9,11},{10,... | collective-permute-start | bytes 172040 | tf_op jit(solution)/shard_map/ppermute | solution.py:17
  16.1 2.7 %collective-permute-done.4.b_ref = bf16[32,896]{1,0:T(8,128)(2,1)S(1)} collective-permute-done((bf16[32,896]{1,0:T(8,128)(2,1)S(1)}, bf16[32,896]{1,0:T(8,128)(2,1)S(1)}, u32[]{:S(2)}, u32[]{:S(2)}) %collective-permute-start.4) | collective-permute-done | bytes 57376 | tf_op jit(solution)/shard_map/ppermute | solution.py:17
  18.8 1.5 %collective-permute-start.7 = (bf16[32,896]{1,0:T(8,128)(2,1)S(1)}, bf16[32,896]{1,0:T(8,128)(2,1)S(1)}, u32[]{:S(2)}, u32[]{:S(2)}) collective-permute-start(bf16[32,896]{1,0:T(8,128)(2,1)S(1)} %shard_map.144.refs_0_), channel_id=1, source_target_pairs={{0,12},{4,8},{8,4},{12,0},{1,13},{5,9},{9,5},{13,1},{2,14},{6,10},... | collective-permute-start | bytes 172040 | tf_op jit(solution)/shard_map/ppermute | solution.py:17
  20.3 0.6 %collective-permute-start.6 = (bf16[32,896]{1,0:T(8,128)(2,1)S(1)}, bf16[32,896]{1,0:T(8,128)(2,1)S(1)}, u32[]{:S(2)}, u32[]{:S(2)}) collective-permute-start(bf16[32,896]{1,0:T(8,128)(2,1)S(1)} %shard_map.144.refs_0_), channel_id=1, source_target_pairs={{0,8},{4,12},{8,0},{12,4},{1,9},{5,13},{9,1},{13,5},{2,10},{6,14},... | collective-permute-start | bytes 172040 | tf_op jit(solution)/shard_map/ppermute | solution.py:17
  21.0 2.3 %collective-permute-start.5 = (bf16[32,896]{1,0:T(8,128)(2,1)S(1)}, bf16[32,896]{1,0:T(8,128)(2,1)S(1)}, u32[]{:S(2)}, u32[]{:S(2)}) collective-permute-start(bf16[32,896]{1,0:T(8,128)(2,1)S(1)} %shard_map.144.refs_0_), channel_id=1, source_target_pairs={{0,4},{4,0},{8,12},{12,8},{1,5},{5,1},{9,13},{13,9},{2,6},{6,2},{1... | collective-permute-start | bytes 172040 | tf_op jit(solution)/shard_map/ppermute | solution.py:17
  23.3 1.7 %collective-permute-done.7.refs_3_ = bf16[32,896]{1,0:T(8,128)(2,1)S(1)} collective-permute-done((bf16[32,896]{1,0:T(8,128)(2,1)S(1)}, bf16[32,896]{1,0:T(8,128)(2,1)S(1)}, u32[]{:S(2)}, u32[]{:S(2)}) %collective-permute-start.7) | collective-permute-done | bytes 57376 | tf_op jit(solution)/shard_map/ppermute | solution.py:17
  25.0 1.6 %collective-permute-done.6.refs_2_ = bf16[32,896]{1,0:T(8,128)(2,1)S(1)} collective-permute-done((bf16[32,896]{1,0:T(8,128)(2,1)S(1)}, bf16[32,896]{1,0:T(8,128)(2,1)S(1)}, u32[]{:S(2)}, u32[]{:S(2)}) %collective-permute-start.6) | collective-permute-done | bytes 57376 | tf_op jit(solution)/shard_map/ppermute | solution.py:17
  26.6 7.6 %shard_map.145 = (bf16[8,3584]{1,0:T(8,128)(2,1)}, f32[8,3584]{1,0:T(8,128)S(1)}, bf16[8,3584]{1,0:T(8,128)(2,1)S(1)}, bf16[8,3584]{1,0:T(8,128)(2,1)S(1)}, bf16[8,3584]{1,0:T(8,128)(2,1)S(1)}) custom-call(f32[32,128]{1,0:T(8,128)S(1)} %get-tuple-element.24.table_ref, f32[3584]{0:T(1024)S(1)} %copy-done.4, bf16[8,3584,256]{2,1,0:T(8,128)(2,1)S(1)} %copy-done, ...), custom_call_target="tpu_custom_call" | custom-call | flops 10000000000 | bytes 1048576 | tf_op jit(solution)/shard_map/pallas_call | solution.py:124
  34.2 2.0 %collective-permute-start.8 = (bf16[8,3584]{1,0:T(8,128)(2,1)S(1)}, bf16[8,3584]{1,0:T(8,128)(2,1)S(1)}, u32[]{:S(2)}, u32[]{:S(2)}) collective-permute-start(bf16[8,3584]{1,0:T(8,128)(2,1)S(1)} %get-tuple-element.29), channel_id=1, source_target_pairs={{0,12},{4,8},{8,4},{12,0},{1,13},{5,9},{9,5},{13,1},{2,14},{6,10},... | collective-permute-start | bytes 172040 | tf_op jit(solution)/shard_map/ppermute | solution.py:17
  36.3 0.3 collective-permute-start.9
  36.6 2.1 %collective-permute-start.10 = (bf16[8,3584]{1,0:T(8,128)(2,1)S(1)}, bf16[8,3584]{1,0:T(8,128)(2,1)S(1)}, u32[]{:S(2)}, u32[]{:S(2)}) collective-permute-start(bf16[8,3584]{1,0:T(8,128)(2,1)S(1)} %get-tuple-element.31), channel_id=1, source_target_pairs={{0,4},{4,0},{8,12},{12,8},{1,5},{5,1},{9,13},{13,9},{2,6},{6,2},{1... | collective-permute-start | bytes 172040 | tf_op jit(solution)/shard_map/ppermute | solution.py:17
  38.6 1.7 %collective-permute-done.8.refs_0_ = bf16[8,3584]{1,0:T(8,128)(2,1)S(1)} collective-permute-done((bf16[8,3584]{1,0:T(8,128)(2,1)S(1)}, bf16[8,3584]{1,0:T(8,128)(2,1)S(1)}, u32[]{:S(2)}, u32[]{:S(2)}) %collective-permute-start.8) | collective-permute-done | bytes 57376 | tf_op jit(solution)/shard_map/ppermute | solution.py:17
  40.3 1.5 %collective-permute-done.9.refs_1_ = bf16[8,3584]{1,0:T(8,128)(2,1)S(1)} collective-permute-done((bf16[8,3584]{1,0:T(8,128)(2,1)S(1)}, bf16[8,3584]{1,0:T(8,128)(2,1)S(1)}, u32[]{:S(2)}, u32[]{:S(2)}) %collective-permute-start.9) | collective-permute-done | bytes 57376 | tf_op jit(solution)/shard_map/ppermute | solution.py:17
  41.9 1.2 %collective-permute-done.11.b_ref = bf16[8,3584]{1,0:T(8,128)(2,1)S(1)} collective-permute-done((bf16[8,3584]{1,0:T(8,128)(2,1)S(1)}, bf16[8,3584]{1,0:T(8,128)(2,1)S(1)}, u32[]{:S(2)}, u32[]{:S(2)}) %collective-permute-start.11) | collective-permute-done | bytes 57376 | tf_op jit(solution)/shard_map/ppermute | solution.py:17
  43.2 1.6 %collective-permute-start.12 = (bf16[8,3584]{1,0:T(8,128)(2,1)S(1)}, bf16[8,3584]{1,0:T(8,128)(2,1)S(1)}, u32[]{:S(2)}, u32[]{:S(2)}) collective-permute-start(bf16[8,3584]{1,0:T(8,128)(2,1)S(1)} %shard_map.147.a_ref), channel_id=1, source_target_pairs={{0,2},{1,3},{2,0},{3,1},{4,6},{5,7},{6,4},{7,5},{8,10},{9,11},{10,... | collective-permute-start | bytes 172040 | tf_op jit(solution)/shard_map/ppermute | solution.py:17
  44.7 2.7 %collective-permute-done.12.b_ref = bf16[8,3584]{1,0:T(8,128)(2,1)S(1)} collective-permute-done((bf16[8,3584]{1,0:T(8,128)(2,1)S(1)}, bf16[8,3584]{1,0:T(8,128)(2,1)S(1)}, u32[]{:S(2)}, u32[]{:S(2)}) %collective-permute-start.12) | collective-permute-done | bytes 57376 | tf_op jit(solution)/shard_map/ppermute | solution.py:17
  47.4 0.6 %shard_map.148 = bf16[8,3584]{1,0:T(8,128)(2,1)} custom-call(bf16[8,3584]{1,0:T(8,128)(2,1)S(1)} %shard_map.147.a_ref, bf16[8,3584]{1,0:T(8,128)(2,1)S(1)} %collective-permute-done.12.b_ref), custom_call_target="tpu_custom_call" | custom-call | tf_op jit(solution)/shard_map/pallas_call | solution.py:124
  (21 shorter events, 0.3 us)
Async XLA Ops:
  2.8 10.0 %copy-start.3 = (bf16[1024,896]{1,0:T(8,128)(2,1)S(1)}, bf16[1024,896]{1,0:T(8,128)(2,1)}, u32[]{:S(2)}) copy-start(bf16[1024,896]{1,0:T(8,128)(2,1)} %proj_ref.1) | copy-start | bytes 5505028
  2.8 23.8 %copy-start = (bf16[8,3584,256]{2,1,0:T(8,128)(2,1)S(1)}, bf16[8,3584,256]{2,1,0:T(8,128)(2,1)}, u32[]{:S(2)}) copy-start(bf16[8,3584,256]{2,1,0:T(8,128)(2,1)} %wg_ref.1) | copy-start | bytes 44040196
  2.8 23.8 %copy-start.1 = (bf16[8,3584,256]{2,1,0:T(8,128)(2,1)S(1)}, bf16[8,3584,256]{2,1,0:T(8,128)(2,1)}, u32[]{:S(2)}) copy-start(bf16[8,3584,256]{2,1,0:T(8,128)(2,1)} %wu_ref.1) | copy-start | bytes 44040196
  2.8 23.8 %copy-start.2 = (bf16[8,256,3584]{2,1,0:T(8,128)(2,1)S(1)}, bf16[8,256,3584]{2,1,0:T(8,128)(2,1)}, u32[]{:S(2)}) copy-start(bf16[8,256,3584]{2,1,0:T(8,128)(2,1)} %wd_ref.1) | copy-start | bytes 44040196
  2.8 23.8 %copy-start.4 = (f32[3584]{0:T(1024)S(1)}, f32[3584]{0:T(1024)}, u32[]{:S(2)}) copy-start(f32[3584]{0:T(1024)} %gain_ref.1) | copy-start | bytes 43012
  2.8 7.0 %collective-permute-start = (bf16[8,2048]{1,0:T(8,128)(2,1)S(1)}, bf16[8,2048]{1,0:T(8,128)(2,1)S(1)}, u32[]{:S(2)}, u32[]{:S(2)}) collective-permute-start(bf16[8,2048]{1,0:T(8,128)(2,1)S(1)} %get-tuple-element.20), channel_id=1, source_target_pairs={{0,12},{4,8},{8,4},{12,0},{1,13},{5,9},{9,5},{13,1},{2,14},{6,10},... | collective-permute-start | bytes 98312 | tf_op jit(solution)/shard_map/ppermute | solution.py:17
  8.0 4.8 %collective-permute-start.1 = (bf16[8,2048]{1,0:T(8,128)(2,1)S(1)}, bf16[8,2048]{1,0:T(8,128)(2,1)S(1)}, u32[]{:S(2)}, u32[]{:S(2)}) collective-permute-start(bf16[8,2048]{1,0:T(8,128)(2,1)S(1)} %get-tuple-element.21), channel_id=1, source_target_pairs={{0,8},{4,12},{8,0},{12,4},{1,9},{5,13},{9,1},{13,5},{2,10},{6,14},... | collective-permute-start | bytes 98312 | tf_op jit(solution)/shard_map/ppermute | solution.py:17
  8.0 4.8 %collective-permute-start.2 = (bf16[8,2048]{1,0:T(8,128)(2,1)S(1)}, bf16[8,2048]{1,0:T(8,128)(2,1)S(1)}, u32[]{:S(2)}, u32[]{:S(2)}) collective-permute-start(bf16[8,2048]{1,0:T(8,128)(2,1)S(1)} %get-tuple-element.22), channel_id=1, source_target_pairs={{0,4},{4,0},{8,12},{12,8},{1,5},{5,1},{9,13},{13,9},{2,6},{6,2},{1... | collective-permute-start | bytes 98312 | tf_op jit(solution)/shard_map/ppermute | solution.py:17
  13.2 1.3 %collective-permute-start.3 = (bf16[32,896]{1,0:T(8,128)(2,1)S(1)}, bf16[32,896]{1,0:T(8,128)(2,1)S(1)}, u32[]{:S(2)}, u32[]{:S(2)}) collective-permute-start(bf16[32,896]{1,0:T(8,128)(2,1)S(1)} %get-tuple-element.25.a_ref), channel_id=1, source_target_pairs={{0,1},{1,0},{2,3},{3,2},{4,5},{5,4},{6,7},{7,6},{8,9},{9,8},{10,11... | collective-permute-start | bytes 172040 | tf_op jit(solution)/shard_map/ppermute | solution.py:17
  14.5 4.2 %collective-permute-start.4 = (bf16[32,896]{1,0:T(8,128)(2,1)S(1)}, bf16[32,896]{1,0:T(8,128)(2,1)S(1)}, u32[]{:S(2)}, u32[]{:S(2)}) collective-permute-start(bf16[32,896]{1,0:T(8,128)(2,1)S(1)} %shard_map.143.a_ref), channel_id=1, source_target_pairs={{0,2},{1,3},{2,0},{3,1},{4,6},{5,7},{6,4},{7,5},{8,10},{9,11},{10,... | collective-permute-start | bytes 172040 | tf_op jit(solution)/shard_map/ppermute | solution.py:17
  18.8 6.2 %collective-permute-start.7 = (bf16[32,896]{1,0:T(8,128)(2,1)S(1)}, bf16[32,896]{1,0:T(8,128)(2,1)S(1)}, u32[]{:S(2)}, u32[]{:S(2)}) collective-permute-start(bf16[32,896]{1,0:T(8,128)(2,1)S(1)} %shard_map.144.refs_0_), channel_id=1, source_target_pairs={{0,12},{4,8},{8,4},{12,0},{1,13},{5,9},{9,5},{13,1},{2,14},{6,10},... | collective-permute-start | bytes 172040 | tf_op jit(solution)/shard_map/ppermute | solution.py:17
  20.3 6.2 %collective-permute-start.6 = (bf16[32,896]{1,0:T(8,128)(2,1)S(1)}, bf16[32,896]{1,0:T(8,128)(2,1)S(1)}, u32[]{:S(2)}, u32[]{:S(2)}) collective-permute-start(bf16[32,896]{1,0:T(8,128)(2,1)S(1)} %shard_map.144.refs_0_), channel_id=1, source_target_pairs={{0,8},{4,12},{8,0},{12,4},{1,9},{5,13},{9,1},{13,5},{2,10},{6,14},... | collective-permute-start | bytes 172040 | tf_op jit(solution)/shard_map/ppermute | solution.py:17
  21.0 5.6 %collective-permute-start.5 = (bf16[32,896]{1,0:T(8,128)(2,1)S(1)}, bf16[32,896]{1,0:T(8,128)(2,1)S(1)}, u32[]{:S(2)}, u32[]{:S(2)}) collective-permute-start(bf16[32,896]{1,0:T(8,128)(2,1)S(1)} %shard_map.144.refs_0_), channel_id=1, source_target_pairs={{0,4},{4,0},{8,12},{12,8},{1,5},{5,1},{9,13},{13,9},{2,6},{6,2},{1... | collective-permute-start | bytes 172040 | tf_op jit(solution)/shard_map/ppermute | solution.py:17
  34.2 6.1 %collective-permute-start.8 = (bf16[8,3584]{1,0:T(8,128)(2,1)S(1)}, bf16[8,3584]{1,0:T(8,128)(2,1)S(1)}, u32[]{:S(2)}, u32[]{:S(2)}) collective-permute-start(bf16[8,3584]{1,0:T(8,128)(2,1)S(1)} %get-tuple-element.29), channel_id=1, source_target_pairs={{0,12},{4,8},{8,4},{12,0},{1,13},{5,9},{9,5},{13,1},{2,14},{6,10},... | collective-permute-start | bytes 172040 | tf_op jit(solution)/shard_map/ppermute | solution.py:17
  36.3 5.6 %collective-permute-start.9 = (bf16[8,3584]{1,0:T(8,128)(2,1)S(1)}, bf16[8,3584]{1,0:T(8,128)(2,1)S(1)}, u32[]{:S(2)}, u32[]{:S(2)}) collective-permute-start(bf16[8,3584]{1,0:T(8,128)(2,1)S(1)} %get-tuple-element.30), channel_id=1, source_target_pairs={{0,8},{4,12},{8,0},{12,4},{1,9},{5,13},{9,1},{13,5},{2,10},{6,14},... | collective-permute-start | bytes 172040 | tf_op jit(solution)/shard_map/ppermute | solution.py:17
  36.6 5.3 %collective-permute-start.10 = (bf16[8,3584]{1,0:T(8,128)(2,1)S(1)}, bf16[8,3584]{1,0:T(8,128)(2,1)S(1)}, u32[]{:S(2)}, u32[]{:S(2)}) collective-permute-start(bf16[8,3584]{1,0:T(8,128)(2,1)S(1)} %get-tuple-element.31), channel_id=1, source_target_pairs={{0,4},{4,0},{8,12},{12,8},{1,5},{5,1},{9,13},{13,9},{2,6},{6,2},{1... | collective-permute-start | bytes 172040 | tf_op jit(solution)/shard_map/ppermute | solution.py:17
  41.9 1.3 %collective-permute-start.11 = (bf16[8,3584]{1,0:T(8,128)(2,1)S(1)}, bf16[8,3584]{1,0:T(8,128)(2,1)S(1)}, u32[]{:S(2)}, u32[]{:S(2)}) collective-permute-start(bf16[8,3584]{1,0:T(8,128)(2,1)S(1)} %shard_map.146.a_ref), channel_id=1, source_target_pairs={{0,1},{1,0},{2,3},{3,2},{4,5},{5,4},{6,7},{7,6},{8,9},{9,8},{10,11... | collective-permute-start | bytes 172040 | tf_op jit(solution)/shard_map/ppermute | solution.py:17
  43.2 4.2 %collective-permute-start.12 = (bf16[8,3584]{1,0:T(8,128)(2,1)S(1)}, bf16[8,3584]{1,0:T(8,128)(2,1)S(1)}, u32[]{:S(2)}, u32[]{:S(2)}) collective-permute-start(bf16[8,3584]{1,0:T(8,128)(2,1)S(1)} %shard_map.147.a_ref), channel_id=1, source_target_pairs={{0,2},{1,3},{2,0},{3,1},{4,6},{5,7},{6,4},{7,5},{8,10},{9,11},{10,... | collective-permute-start | bytes 172040 | tf_op jit(solution)/shard_map/ppermute | solution.py:17

commit v4 on v3

--- a/solution.py
+++ b/solution.py
@@ -8,9 +8,11 @@
 from jax.sharding import PartitionSpec as P
 
 LANES = 128
+LIMIT = 4 << 20
+AHEAD = 3
 ROWS = 8
 VMEM = pl.BlockSpec(memory_space=pltpu.VMEM)
-FLOPS = (8 * 10**10, 1, 1, 1, 10**10)
+FLOPS = (16 * 10**10, 1, 1, 1, 10**9, 10**9)
 
 
 def swap(x, axis, size, step):
@@ -153,14 +155,15 @@
 
 
 def attend_kernel(scale, *refs):
-    sources, (heads_ref, res_out_ref, table_ref), held, sems = refs[:8], refs[8:11], refs[11:19], refs[19]
+    sources, outs, held, sems = refs[:9], refs[9:13], refs[13:22], refs[22]
+    heads_ref, res_out_ref, table_ref, gain_out_ref = outs
     copies = [
         pltpu.make_async_copy(source, place, sems.at[i])
         for i, (source, place) in enumerate(zip(sources, held))
     ]
     for copy in copies:
         copy.start()
-    ql_ref, cl_ref, qr_ref, cr_ref, av_ref, res_ref, routes_ref, weights_ref = held
+    ql_ref, cl_ref, qr_ref, cr_ref, av_ref, res_ref, routes_ref, weights_ref, gain_ref = held
     t, h, _ = ql_ref.shape
     c = cl_ref.shape[1]
     vdim = av_ref.shape[2]
@@ -186,6 +189,7 @@
         out = dot(by_head[i * t : (i + 1) * t].astype(jnp.bfloat16), av_ref[i])
         heads_ref[:, i * vdim : (i + 1) * vdim] = out.astype(jnp.bfloat16)
     res_out_ref[...] = res_ref[...]
+    gain_out_ref[...] = gain_ref[...].reshape(gain_out_ref.shape)
     lane = lax.broadcasted_iota(jnp.int32, (t, LANES), 1)
     table = jnp.zeros((t, LANES), jnp.float32)
     for k in range(routes_ref.shape[1]):
@@ -234,34 +238,59 @@
     out_ref[...] = (res_ref[...] + attention).astype(jnp.bfloat16)
 
 
-def expert_kernel(experts, table_ref, gain_ref, wg_ref, wu_ref, wd_ref, *refs):
-    n = (len(refs) - 3) // 2
-    mids, (own_ref, total_ref), outs, (mid_ref, sum_ref) = refs[:n], refs[n : n + 2], refs[n + 2 : -2], refs[-2:]
+def padded(x):
+    return jnp.concatenate([x] * max(1, LANES // x.shape[0]), axis=0)
+
+
+def add_block(n, k, mid_ref, gain_ref, wg_ref, wu_ref, before, after):
+    gate_ref, up_ref, square_ref = after
+    tokens, cols = mid_ref.shape
+    experts, _, width = wg_ref.shape
+    rows = tokens // n
+    start = pl.multiple_of((lax.axis_index("expert") ^ k) * cols, LANES)
+    got = mid_ref[...].astype(jnp.float32)
+    block = jnp.concatenate([got[(i ^ k) * rows : (i ^ k) * rows + rows] for i in range(n)], axis=0)
+    square = jnp.sum(block * block, axis=-1, keepdims=True)
+    square_ref[...] = square + before[2][...] if before else jnp.broadcast_to(square, square_ref.shape)
+    left = padded((block * gain_ref[:, pl.ds(start, cols)]).astype(jnp.bfloat16))
+    for e in range(experts):
+        at = slice(e * width, (e + 1) * width)
+        gate = dot(left, wg_ref[e, pl.ds(start, cols)])[:tokens]
+        up = dot(left, wu_ref[e, pl.ds(start, cols)])[:tokens]
+        gate_ref[:, at] = gate + before[0][:, at] if before else gate
+        up_ref[:, at] = up + before[1][:, at] if before else up
+
+
+def part_kernel(n, k, gain_ref, wg_ref, wu_ref, _, mid_ref, *refs):
+    add_block(n, k, mid_ref, gain_ref, wg_ref, wu_ref, refs[:-3], refs[-3:])
+
+
+def rest_kernel(n, rest, gain_ref, wg_ref, wu_ref, wd_ref, table_ref, *refs):
+    mids, sums, refs = refs[:n], refs[n : n + 3], refs[n + 3 :]
+    (own_ref, total_ref), outs = refs[:2], refs[2 : n + 1]
+    gate_ref, up_ref, square_ref, sum_ref = refs[n + 1 :]
     tokens, cols = mids[0].shape
+    experts, width, _ = wd_ref.shape
     rows = tokens // n
     me = lax.axis_index("expert")
-    squares = jnp.zeros((tokens, 1), jnp.float32)
+    for k in rest:
+        add_block(n, k, mids[k], gain_ref, wg_ref, wu_ref, sums, (gate_ref, up_ref, square_ref))
+        sums = (gate_ref, up_ref, square_ref)
     for k in range(n):
-        got = mids[k][...].astype(jnp.float32)
-        block = jnp.concatenate([got[(i ^ k) * rows : (i ^ k) * rows + rows] for i in range(n)], axis=0)
-        squares = squares + jnp.sum(block * block, axis=-1, keepdims=True)
-        mid_ref[:, pl.ds(pl.multiple_of((me ^ k) * cols, LANES), cols)] = block
-    inverse = lax.rsqrt(squares / (n * cols) + 1e-06)
-    own_ref[...] = mid_ref[:rows].astype(jnp.bfloat16)
-    normed = (mid_ref[...] * inverse * gain_ref[...].reshape(1, n * cols)).astype(jnp.bfloat16)
-    copies = max(1, LANES // tokens)
-    normed = jnp.concatenate([normed] * copies, axis=0)
+        got = mids[k][...].astype(jnp.float32)[k * rows : (k + 1) * rows]
+        own_ref[:, pl.ds(pl.multiple_of((me ^ k) * cols, LANES), cols)] = got.astype(jnp.bfloat16)
+    inverse = lax.rsqrt(square_ref[:, :1] / (n * cols) + 1e-06)
     lane = lax.broadcasted_iota(jnp.int32, (tokens, LANES), 1) % (LANES // 2)
     for e in range(experts):
-        gate = dot(normed, wg_ref[e])[:tokens]
-        up = dot(normed, wu_ref[e])[:tokens]
+        at = slice(e * width, (e + 1) * width)
+        gate = gate_ref[:, at] * inverse
+        up = up_ref[:, at] * inverse
         weight = jnp.sum(
             jnp.where(lane == me * experts + e, table_ref[...], 0.0), axis=1, keepdims=True
         )
         hidden = gate / (1.0 + jnp.exp(-gate)) * up * weight
         hidden = jnp.where(weight != 0.0, hidden, 0.0).astype(jnp.bfloat16)
-        hidden = jnp.concatenate([hidden] * copies, axis=0)
-        down = dot(hidden, wd_ref[e])[:tokens]
+        down = dot(padded(hidden), wd_ref[e])[:tokens]
         if e == 0:
             sum_ref[...] = down
         else:
@@ -313,7 +342,7 @@
     head_n = lax.axis_size("head")
     rows, model_d = residual.shape
     width, cols = out_proj.shape
-    experts = w_gate.shape[0]
+    experts, _, hidden_f = w_gate.shape
     tokens = rows * n
     fits = rows == ROWS and cols % LANES == 0 and n & (n - 1) == 0 and head_n == 4
     if not fits or experts * n > LANES // 2 or width % LANES:
@@ -331,10 +360,11 @@
         residual,
         routes,
         route_weights,
+        norm_gain,
     ]
-    local = call(
+    *local, gain = call(
         functools.partial(attend_kernel, scale),
-        [bf16(rows, width), bf16(rows, model_d), bf16(rows, LANES)],
+        [bf16(rows, width), bf16(rows, model_d), bf16(rows, LANES), f32(1, model_d)],
         *[pltpu.with_memory_space_constraint(x, pltpu.HBM) for x in inputs],
         limit=6 << 20,
         scratch=[pltpu.VMEM(x.shape, x.dtype) for x in inputs] + [pltpu.SemaphoreType.DMA((len(inputs),))],
@@ -344,7 +374,7 @@
         pack_kernel,
         [bf16(rows, width + cols + LANES)] * n,
         *local,
-        limit=2 << 20,
+        limit=LIMIT,
         flops=FLOPS[0],
     )
     got = [swap(msgs[k], "expert", n, k) for k in range(n - 1, 0, -1)] + [msgs[0]]
@@ -353,7 +383,7 @@
         [bf16(tokens, cols), f32(tokens, cols), f32(tokens, LANES)],
         in_vmem(out_proj),
         *got,
-        limit=4 << 20,
+        limit=LIMIT,
         flops=FLOPS[1],
     )
     pair = call(
@@ -361,7 +391,7 @@
         bf16(tokens, cols),
         partial,
         swap(partial, "head", head_n, 1),
-        limit=2 << 20,
+        limit=LIMIT,
         flops=FLOPS[2],
     )
     mid = call(
@@ -370,32 +400,50 @@
         pair,
         swap(pair, "head", head_n, 2),
         res,
-        limit=2 << 20,
+        limit=LIMIT,
         flops=FLOPS[3],
     )
     mids = [mid] + [swap(mid, "expert", n, k) for k in range(1, n)]
+    gate_weights, up_weights, down_weights = in_vmem(w_gate), in_vmem(w_up), in_vmem(w_down)
+    sum_shapes = [f32(tokens, experts * hidden_f)] * 2 + [f32(tokens, LANES)]
+    order = [0] + list(range(n - 1, 0, -1))
+    sums = []
+    for k in order[:AHEAD]:
+        sums = call(
+            functools.partial(part_kernel, n, k),
+            sum_shapes,
+            gain,
+            gate_weights,
+            up_weights,
+            down_weights,
+            mids[k],
+            *sums,
+            limit=LIMIT,
+            flops=FLOPS[4],
+        )
     own_mid, own, *parts = call(
-        functools.partial(expert_kernel, experts),
+        functools.partial(rest_kernel, n, order[AHEAD:]),
         [bf16(rows, model_d), f32(rows, model_d)] + [bf16(rows, model_d)] * (n - 1),
+        gain,
+        gate_weights,
+        up_weights,
+        down_weights,
         table,
-        norm_gain,
-        in_vmem(w_gate),
-        in_vmem(w_up),
-        in_vmem(w_down),
         *mids,
-        limit=8 << 20,
-        scratch=[pltpu.VMEM((tokens, model_d), jnp.float32)] * 2,
-        flops=FLOPS[4],
+        *sums,
+        limit=LIMIT,
+        scratch=[pltpu.VMEM(x.shape, x.dtype) for x in sum_shapes + [f32(tokens, model_d)]],
+        flops=FLOPS[5],
     )
     back = [swap(parts[k - 1], "expert", n, k) for k in range(n - 1, 0, -1)]
-    mixed = call(join_kernel, bf16(rows, model_d), own, *back, limit=2 << 20)
+    mixed = call(join_kernel, bf16(rows, model_d), own, *back, limit=LIMIT)
     for step in (1, 2):
         mixed = call(
             add_kernel,
             bf16(rows, model_d),
             mixed,
             swap(mixed, "head", head_n, step),
-            limit=2 << 20,
+            limit=LIMIT,
         )
     return own_mid, mixed
 

time: 48.2 us -> 46.1 us (0.956)
  waiting for transfers between devices: 18.5 us -> 17.4 us
  starting transfers between devices: 17.8 us -> 16.9 us
    ppermute x13, waiting for transfers between devices: 18.5 us -> 17.4 us  [swap(): return lax.ppermute(x, axis, [(s, s ^ step) for s in range(size)])]
    ppermute x13, starting transfers between devices: 17.8 us -> 16.9 us  [swap(): return lax.ppermute(x, axis, [(s, s ^ step) for s in range(size)])]
    pallas_call x9 -> x12, Pallas kernels: 10.9 us -> 10.9 us  [call(): pl.pallas_call(body, out_shape=outs, in_specs=[VMEM] * len(args) if specs...]
  transfers between devices with their start and end apart: 13 -> 13, of which waited for: 10 -> 11; matrix products, arithmetic and copies ran while one was open for 0% -> 0% of each run, Pallas kernels for 0% -> 8%
where the time goes in v4:
time: 46.1 us; the launch traced here: 46 us
  waiting for transfers between devices  17.4 us (38%)
  starting transfers between devices  16.9 us (37%)
  Pallas kernels  10.9 us (24%)
  between operations  0.76 us (2%)
    ppermute x13, waiting for transfers between devices, swap(): return lax.ppermute(x, axis, [(s, s ^ step) for s in range(size)])  17.4 us
    ppermute x13, starting transfers between devices, swap(): return lax.ppermute(x, axis, [(s, s ^ step) for s in range(size)])  16.9 us
    pallas_call x12, Pallas kernels, call(): pl.pallas_call(body, out_shape=outs, in_specs=[VMEM] * len(args) if specs...  10.9 us
  transfers between devices with their start and end apart: 13, of which 11 were waited for; matrix products, arithmetic and copies ran while one was open for 0% of the time, Pallas kernels for 8%

profile of v4, /device:TPU:0, one launch (start us, length us, event | category | flops | bytes accessed | tf_op | source)
XLA Modules:
  0.0 46.0 jit_solution(3330932432832149865)
XLA Ops:
  0.6 2.1 %shard_map.140 = (bf16[8,1024]{1,0:T(8,128)(2,1)S(1)}, bf16[8,3584]{1,0:T(8,128)(2,1)S(1)}, bf16[8,128]{1,0:T(8,128)(2,1)S(1)}, f32[1,3584]{1,0:T(1,128)S(1)}) custom-call(bf16[8,8,512]{2,1,0:T(8,128)(2,1)} %refs_0_.1, bf16[8,32,512]{2,1,0:T(8,128)(2,1)} %refs_1_.1, bf16[8,8,64]{2,1,0:T(8,128)(2,1)} %refs_2_.1, bf16[8,32,64]{2,1,0:T(8,128)(2,1)} %refs_3_.1, ...), custom_call_target="tpu_custom_call" | custom-call | tf_op jit(solution)/shard_map/pallas_call | solution.py:126
  2.8 5.1 %collective-permute-start = (bf16[8,2048]{1,0:T(8,128)(2,1)S(1)}, bf16[8,2048]{1,0:T(8,128)(2,1)S(1)}, u32[]{:S(2)}, u32[]{:S(2)}) collective-permute-start(bf16[8,2048]{1,0:T(8,128)(2,1)S(1)} %get-tuple-element.31), channel_id=1, source_target_pairs={{0,12},{4,8},{8,4},{12,0},{1,13},{5,9},{9,5},{13,1},{2,14},{6,10},... | collective-permute-start | bytes 98312 | tf_op jit(solution)/shard_map/ppermute | solution.py:19
  8.0 0.6 %collective-permute-start.2 = (bf16[8,2048]{1,0:T(8,128)(2,1)S(1)}, bf16[8,2048]{1,0:T(8,128)(2,1)S(1)}, u32[]{:S(2)}, u32[]{:S(2)}) collective-permute-start(bf16[8,2048]{1,0:T(8,128)(2,1)S(1)} %get-tuple-element.33), channel_id=1, source_target_pairs={{0,4},{4,0},{8,12},{12,8},{1,5},{5,1},{9,13},{13,9},{2,6},{6,2},{1... | collective-permute-start | bytes 98312 | tf_op jit(solution)/shard_map/ppermute | solution.py:19
  8.6 1.3 %collective-permute-done.refs_0_ = bf16[8,2048]{1,0:T(8,128)(2,1)S(1)} collective-permute-done((bf16[8,2048]{1,0:T(8,128)(2,1)S(1)}, bf16[8,2048]{1,0:T(8,128)(2,1)S(1)}, u32[]{:S(2)}, u32[]{:S(2)}) %collective-permute-start) | collective-permute-done | bytes 32800 | tf_op jit(solution)/shard_map/ppermute | solution.py:19
  9.9 2.9 %collective-permute-done.1.refs_1_ = bf16[8,2048]{1,0:T(8,128)(2,1)S(1)} collective-permute-done((bf16[8,2048]{1,0:T(8,128)(2,1)S(1)}, bf16[8,2048]{1,0:T(8,128)(2,1)S(1)}, u32[]{:S(2)}, u32[]{:S(2)}) %collective-permute-start.1) | collective-permute-done | bytes 32800 | tf_op jit(solution)/shard_map/ppermute | solution.py:19
  13.3 1.2 %collective-permute-done.3.b_ref = bf16[32,896]{1,0:T(8,128)(2,1)S(1)} collective-permute-done((bf16[32,896]{1,0:T(8,128)(2,1)S(1)}, bf16[32,896]{1,0:T(8,128)(2,1)S(1)}, u32[]{:S(2)}, u32[]{:S(2)}) %collective-permute-start.3) | collective-permute-done | bytes 57376 | tf_op jit(solution)/shard_map/ppermute | solution.py:19
  14.5 1.6 %collective-permute-start.4 = (bf16[32,896]{1,0:T(8,128)(2,1)S(1)}, bf16[32,896]{1,0:T(8,128)(2,1)S(1)}, u32[]{:S(2)}, u32[]{:S(2)}) collective-permute-start(bf16[32,896]{1,0:T(8,128)(2,1)S(1)} %shard_map.143.a_ref), channel_id=1, source_target_pairs={{0,2},{1,3},{2,0},{3,1},{4,6},{5,7},{6,4},{7,5},{8,10},{9,11},{10,... | collective-permute-start | bytes 172040 | tf_op jit(solution)/shard_map/ppermute | solution.py:19
  16.1 2.7 %collective-permute-done.4.b_ref = bf16[32,896]{1,0:T(8,128)(2,1)S(1)} collective-permute-done((bf16[32,896]{1,0:T(8,128)(2,1)S(1)}, bf16[32,896]{1,0:T(8,128)(2,1)S(1)}, u32[]{:S(2)}, u32[]{:S(2)}) %collective-permute-start.4) | collective-permute-done | bytes 57376 | tf_op jit(solution)/shard_map/ppermute | solution.py:19
  18.8 1.5 %collective-permute-start.7 = (bf16[32,896]{1,0:T(8,128)(2,1)S(1)}, bf16[32,896]{1,0:T(8,128)(2,1)S(1)}, u32[]{:S(2)}, u32[]{:S(2)}) collective-permute-start(bf16[32,896]{1,0:T(8,128)(2,1)S(1)} %shard_map.144.mid_ref.refs_0_), channel_id=1, source_target_pairs={{0,12},{4,8},{8,4},{12,0},{1,13},{5,9},{9,5},{13,1},{2,14},{6,10},... | collective-permute-start | bytes 172040 | tf_op jit(solution)/shard_map/ppermute | solution.py:19
  20.3 0.6 %collective-permute-start.6 = (bf16[32,896]{1,0:T(8,128)(2,1)S(1)}, bf16[32,896]{1,0:T(8,128)(2,1)S(1)}, u32[]{:S(2)}, u32[]{:S(2)}) collective-permute-start(bf16[32,896]{1,0:T(8,128)(2,1)S(1)} %shard_map.144.mid_ref.refs_0_), channel_id=1, source_target_pairs={{0,8},{4,12},{8,0},{12,4},{1,9},{5,13},{9,1},{13,5},{2,10},{6,14},... | collective-permute-start | bytes 172040 | tf_op jit(solution)/shard_map/ppermute | solution.py:19
  21.0 2.3 %collective-permute-start.5 = (bf16[32,896]{1,0:T(8,128)(2,1)S(1)}, bf16[32,896]{1,0:T(8,128)(2,1)S(1)}, u32[]{:S(2)}, u32[]{:S(2)}) collective-permute-start(bf16[32,896]{1,0:T(8,128)(2,1)S(1)} %shard_map.144.mid_ref.refs_0_), channel_id=1, source_target_pairs={{0,4},{4,0},{8,12},{12,8},{1,5},{5,1},{9,13},{13,9},{2,6},{6,2},{1... | collective-permute-start | bytes 172040 | tf_op jit(solution)/shard_map/ppermute | solution.py:19
  23.3 1.3 %shard_map.145 = (f32[32,2048]{1,0:T(8,128)S(1)}, f32[32,2048]{1,0:T(8,128)S(1)}, f32[32,128]{1,0:T(8,128)S(1)}) custom-call(f32[1,3584]{1,0:T(1,128)S(1)} %get-tuple-element.27.gain_ref, bf16[8,3584,256]{2,1,0:T(8,128)(2,1)S(1)} %copy-done, bf16[8,3584,256]{2,1,0:T(8,128)(2,1)S(1)} %copy-done.1, bf16[8,256,3584]{2,1,0:T(8,128)(2,1)S(1)} %copy-done.2, ...), custom_call_target="tpu_custom_call" | custom-call | flops 1000000000 | bytes 1048576 | tf_op jit(solution)/shard_map/pallas_call | solution.py:126
  25.0 1.3 %shard_map.146 = (f32[32,2048]{1,0:T(8,128)S(1)}, f32[32,2048]{1,0:T(8,128)S(1)}, f32[32,128]{1,0:T(8,128)S(1)}) custom-call(f32[1,3584]{1,0:T(1,128)S(1)} %get-tuple-element.27.gain_ref, bf16[8,3584,256]{2,1,0:T(8,128)(2,1)S(1)} %copy-done, bf16[8,3584,256]{2,1,0:T(8,128)(2,1)S(1)} %copy-done.1, bf16[8,256,3584]{2,1,0:T(8,128)(2,1)S(1)} %copy-done.2, ...), custom_call_target="tpu_custom_call" | custom-call | flops 1000000000 | bytes 1048576 | tf_op jit(solution)/shard_map/pallas_call | solution.py:126
  26.6 1.3 %shard_map.147 = (f32[32,2048]{1,0:T(8,128)S(1)}, f32[32,2048]{1,0:T(8,128)S(1)}, f32[32,128]{1,0:T(8,128)S(1)}) custom-call(f32[1,3584]{1,0:T(1,128)S(1)} %get-tuple-element.27.gain_ref, bf16[8,3584,256]{2,1,0:T(8,128)(2,1)S(1)} %copy-done, bf16[8,3584,256]{2,1,0:T(8,128)(2,1)S(1)} %copy-done.1, bf16[8,256,3584]{2,1,0:T(8,128)(2,1)S(1)} %copy-done.2, ...), custom_call_target="tpu_custom_call" | custom-call | flops 1000000000 | bytes 1048576 | tf_op jit(solution)/shard_map/pallas_call | solution.py:126
  27.8 3.8 %shard_map.148 = (bf16[8,3584]{1,0:T(8,128)(2,1)}, f32[8,3584]{1,0:T(8,128)S(1)}, bf16[8,3584]{1,0:T(8,128)(2,1)S(1)}, bf16[8,3584]{1,0:T(8,128)(2,1)S(1)}, bf16[8,3584]{1,0:T(8,128)(2,1)S(1)}) custom-call(f32[1,3584]{1,0:T(1,128)S(1)} %get-tuple-element.27.gain_ref, bf16[8,3584,256]{2,1,0:T(8,128)(2,1)S(1)} %copy-done, bf16[8,3584,256]{2,1,0:T(8,128)(2,1)S(1)} %copy-done.1, ...), custom_call_target="tpu_custom_call" | custom-call | flops 1000000000 | bytes 1048576 | tf_op jit(solution)/shard_map/pallas_call | solution.py:126
  31.6 0.6 %collective-permute-start.10 = (bf16[8,3584]{1,0:T(8,128)(2,1)S(1)}, bf16[8,3584]{1,0:T(8,128)(2,1)S(1)}, u32[]{:S(2)}, u32[]{:S(2)}) collective-permute-start(bf16[8,3584]{1,0:T(8,128)(2,1)S(1)} %get-tuple-element.51), channel_id=1, source_target_pairs={{0,4},{4,0},{8,12},{12,8},{1,5},{5,1},{9,13},{13,9},{2,6},{6,2},{1... | collective-permute-start | bytes 172040 | tf_op jit(solution)/shard_map/ppermute | solution.py:19
  32.2 2.4 %collective-permute-start.8 = (bf16[8,3584]{1,0:T(8,128)(2,1)S(1)}, bf16[8,3584]{1,0:T(8,128)(2,1)S(1)}, u32[]{:S(2)}, u32[]{:S(2)}) collective-permute-start(bf16[8,3584]{1,0:T(8,128)(2,1)S(1)} %get-tuple-element.49), channel_id=1, source_target_pairs={{0,12},{4,8},{8,4},{12,0},{1,13},{5,9},{9,5},{13,1},{2,14},{6,10},... | collective-permute-start | bytes 172040 | tf_op jit(solution)/shard_map/ppermute | solution.py:19
  35.1 1.1 %collective-permute-done.10.refs_2_ = bf16[8,3584]{1,0:T(8,128)(2,1)S(1)} collective-permute-done((bf16[8,3584]{1,0:T(8,128)(2,1)S(1)}, bf16[8,3584]{1,0:T(8,128)(2,1)S(1)}, u32[]{:S(2)}, u32[]{:S(2)}) %collective-permute-start.10) | collective-permute-done | bytes 57376 | tf_op jit(solution)/shard_map/ppermute | solution.py:19
  36.2 2.0 %collective-permute-done.8.refs_0_ = bf16[8,3584]{1,0:T(8,128)(2,1)S(1)} collective-permute-done((bf16[8,3584]{1,0:T(8,128)(2,1)S(1)}, bf16[8,3584]{1,0:T(8,128)(2,1)S(1)}, u32[]{:S(2)}, u32[]{:S(2)}) %collective-permute-start.8) | collective-permute-done | bytes 57376 | tf_op jit(solution)/shard_map/ppermute | solution.py:19
  38.2 1.5 %collective-permute-done.9.refs_1_ = bf16[8,3584]{1,0:T(8,128)(2,1)S(1)} collective-permute-done((bf16[8,3584]{1,0:T(8,128)(2,1)S(1)}, bf16[8,3584]{1,0:T(8,128)(2,1)S(1)}, u32[]{:S(2)}, u32[]{:S(2)}) %collective-permute-start.9) | collective-permute-done | bytes 57376 | tf_op jit(solution)/shard_map/ppermute | solution.py:19
  39.8 1.2 %collective-permute-done.11.b_ref = bf16[8,3584]{1,0:T(8,128)(2,1)S(1)} collective-permute-done((bf16[8,3584]{1,0:T(8,128)(2,1)S(1)}, bf16[8,3584]{1,0:T(8,128)(2,1)S(1)}, u32[]{:S(2)}, u32[]{:S(2)}) %collective-permute-start.11) | collective-permute-done | bytes 57376 | tf_op jit(solution)/shard_map/ppermute | solution.py:19
  41.1 1.6 %collective-permute-start.12 = (bf16[8,3584]{1,0:T(8,128)(2,1)S(1)}, bf16[8,3584]{1,0:T(8,128)(2,1)S(1)}, u32[]{:S(2)}, u32[]{:S(2)}) collective-permute-start(bf16[8,3584]{1,0:T(8,128)(2,1)S(1)} %shard_map.150.a_ref), channel_id=1, source_target_pairs={{0,2},{1,3},{2,0},{3,1},{4,6},{5,7},{6,4},{7,5},{8,10},{9,11},{10,... | collective-permute-start | bytes 172040 | tf_op jit(solution)/shard_map/ppermute | solution.py:19
  42.6 2.7 %collective-permute-done.12.b_ref = bf16[8,3584]{1,0:T(8,128)(2,1)S(1)} collective-permute-done((bf16[8,3584]{1,0:T(8,128)(2,1)S(1)}, bf16[8,3584]{1,0:T(8,128)(2,1)S(1)}, u32[]{:S(2)}, u32[]{:S(2)}) %collective-permute-start.12) | collective-permute-done | bytes 57376 | tf_op jit(solution)/shard_map/ppermute | solution.py:19
  45.3 0.6 %shard_map.151 = bf16[8,3584]{1,0:T(8,128)(2,1)} custom-call(bf16[8,3584]{1,0:T(8,128)(2,1)S(1)} %shard_map.150.a_ref, bf16[8,3584]{1,0:T(8,128)(2,1)S(1)} %collective-permute-done.12.b_ref), custom_call_target="tpu_custom_call" | custom-call | tf_op jit(solution)/shard_map/pallas_call | solution.py:126
  (22 shorter events, 2.0 us)
Async XLA Ops:
  2.8 10.0 %copy-start.3 = (bf16[1024,896]{1,0:T(8,128)(2,1)S(1)}, bf16[1024,896]{1,0:T(8,128)(2,1)}, u32[]{:S(2)}) copy-start(bf16[1024,896]{1,0:T(8,128)(2,1)} %proj_ref.1) | copy-start | bytes 5505028
  2.8 20.5 %copy-start = (bf16[8,3584,256]{2,1,0:T(8,128)(2,1)S(1)}, bf16[8,3584,256]{2,1,0:T(8,128)(2,1)}, u32[]{:S(2)}) copy-start(bf16[8,3584,256]{2,1,0:T(8,128)(2,1)} %wg_ref.7) | copy-start | bytes 44040196
  2.8 20.5 %copy-start.1 = (bf16[8,3584,256]{2,1,0:T(8,128)(2,1)S(1)}, bf16[8,3584,256]{2,1,0:T(8,128)(2,1)}, u32[]{:S(2)}) copy-start(bf16[8,3584,256]{2,1,0:T(8,128)(2,1)} %wu_ref.7) | copy-start | bytes 44040196
  2.8 20.5 %copy-start.2 = (bf16[8,256,3584]{2,1,0:T(8,128)(2,1)S(1)}, bf16[8,256,3584]{2,1,0:T(8,128)(2,1)}, u32[]{:S(2)}) copy-start(bf16[8,256,3584]{2,1,0:T(8,128)(2,1)} %wd_ref.1) | copy-start | bytes 44040196
  2.8 7.0 %collective-permute-start = (bf16[8,2048]{1,0:T(8,128)(2,1)S(1)}, bf16[8,2048]{1,0:T(8,128)(2,1)S(1)}, u32[]{:S(2)}, u32[]{:S(2)}) collective-permute-start(bf16[8,2048]{1,0:T(8,128)(2,1)S(1)} %get-tuple-element.31), channel_id=1, source_target_pairs={{0,12},{4,8},{8,4},{12,0},{1,13},{5,9},{9,5},{13,1},{2,14},{6,10},... | collective-permute-start | bytes 98312 | tf_op jit(solution)/shard_map/ppermute | solution.py:19
  8.0 4.8 %collective-permute-start.1 = (bf16[8,2048]{1,0:T(8,128)(2,1)S(1)}, bf16[8,2048]{1,0:T(8,128)(2,1)S(1)}, u32[]{:S(2)}, u32[]{:S(2)}) collective-permute-start(bf16[8,2048]{1,0:T(8,128)(2,1)S(1)} %get-tuple-element.32), channel_id=1, source_target_pairs={{0,8},{4,12},{8,0},{12,4},{1,9},{5,13},{9,1},{13,5},{2,10},{6,14},... | collective-permute-start | bytes 98312 | tf_op jit(solution)/shard_map/ppermute | solution.py:19
  8.0 4.8 %collective-permute-start.2 = (bf16[8,2048]{1,0:T(8,128)(2,1)S(1)}, bf16[8,2048]{1,0:T(8,128)(2,1)S(1)}, u32[]{:S(2)}, u32[]{:S(2)}) collective-permute-start(bf16[8,2048]{1,0:T(8,128)(2,1)S(1)} %get-tuple-element.33), channel_id=1, source_target_pairs={{0,4},{4,0},{8,12},{12,8},{1,5},{5,1},{9,13},{13,9},{2,6},{6,2},{1... | collective-permute-start | bytes 98312 | tf_op jit(solution)/shard_map/ppermute | solution.py:19
  13.2 1.3 %collective-permute-start.3 = (bf16[32,896]{1,0:T(8,128)(2,1)S(1)}, bf16[32,896]{1,0:T(8,128)(2,1)S(1)}, u32[]{:S(2)}, u32[]{:S(2)}) collective-permute-start(bf16[32,896]{1,0:T(8,128)(2,1)S(1)} %get-tuple-element.36.a_ref), channel_id=1, source_target_pairs={{0,1},{1,0},{2,3},{3,2},{4,5},{5,4},{6,7},{7,6},{8,9},{9,8},{10,11... | collective-permute-start | bytes 172040 | tf_op jit(solution)/shard_map/ppermute | solution.py:19
  14.5 4.2 %collective-permute-start.4 = (bf16[32,896]{1,0:T(8,128)(2,1)S(1)}, bf16[32,896]{1,0:T(8,128)(2,1)S(1)}, u32[]{:S(2)}, u32[]{:S(2)}) collective-permute-start(bf16[32,896]{1,0:T(8,128)(2,1)S(1)} %shard_map.143.a_ref), channel_id=1, source_target_pairs={{0,2},{1,3},{2,0},{3,1},{4,6},{5,7},{6,4},{7,5},{8,10},{9,11},{10,... | collective-permute-start | bytes 172040 | tf_op jit(solution)/shard_map/ppermute | solution.py:19
  18.8 6.2 %collective-permute-start.7 = (bf16[32,896]{1,0:T(8,128)(2,1)S(1)}, bf16[32,896]{1,0:T(8,128)(2,1)S(1)}, u32[]{:S(2)}, u32[]{:S(2)}) collective-permute-start(bf16[32,896]{1,0:T(8,128)(2,1)S(1)} %shard_map.144.mid_ref.refs_0_), channel_id=1, source_target_pairs={{0,12},{4,8},{8,4},{12,0},{1,13},{5,9},{9,5},{13,1},{2,14},{6,10},... | collective-permute-start | bytes 172040 | tf_op jit(solution)/shard_map/ppermute | solution.py:19
  20.3 6.2 %collective-permute-start.6 = (bf16[32,896]{1,0:T(8,128)(2,1)S(1)}, bf16[32,896]{1,0:T(8,128)(2,1)S(1)}, u32[]{:S(2)}, u32[]{:S(2)}) collective-permute-start(bf16[32,896]{1,0:T(8,128)(2,1)S(1)} %shard_map.144.mid_ref.refs_0_), channel_id=1, source_target_pairs={{0,8},{4,12},{8,0},{12,4},{1,9},{5,13},{9,1},{13,5},{2,10},{6,14},... | collective-permute-start | bytes 172040 | tf_op jit(solution)/shard_map/ppermute | solution.py:19
  21.0 6.9 %collective-permute-start.5 = (bf16[32,896]{1,0:T(8,128)(2,1)S(1)}, bf16[32,896]{1,0:T(8,128)(2,1)S(1)}, u32[]{:S(2)}, u32[]{:S(2)}) collective-permute-start(bf16[32,896]{1,0:T(8,128)(2,1)S(1)} %shard_map.144.mid_ref.refs_0_), channel_id=1, source_target_pairs={{0,4},{4,0},{8,12},{12,8},{1,5},{5,1},{9,13},{13,9},{2,6},{6,2},{1... | collective-permute-start | bytes 172040 | tf_op jit(solution)/shard_map/ppermute | solution.py:19
  31.6 4.6 %collective-permute-start.10 = (bf16[8,3584]{1,0:T(8,128)(2,1)S(1)}, bf16[8,3584]{1,0:T(8,128)(2,1)S(1)}, u32[]{:S(2)}, u32[]{:S(2)}) collective-permute-start(bf16[8,3584]{1,0:T(8,128)(2,1)S(1)} %get-tuple-element.51), channel_id=1, source_target_pairs={{0,4},{4,0},{8,12},{12,8},{1,5},{5,1},{9,13},{13,9},{2,6},{6,2},{1... | collective-permute-start | bytes 172040 | tf_op jit(solution)/shard_map/ppermute | solution.py:19
  32.2 6.0 %collective-permute-start.8 = (bf16[8,3584]{1,0:T(8,128)(2,1)S(1)}, bf16[8,3584]{1,0:T(8,128)(2,1)S(1)}, u32[]{:S(2)}, u32[]{:S(2)}) collective-permute-start(bf16[8,3584]{1,0:T(8,128)(2,1)S(1)} %get-tuple-element.49), channel_id=1, source_target_pairs={{0,12},{4,8},{8,4},{12,0},{1,13},{5,9},{9,5},{13,1},{2,14},{6,10},... | collective-permute-start | bytes 172040 | tf_op jit(solution)/shard_map/ppermute | solution.py:19
  34.6 5.1 %collective-permute-start.9 = (bf16[8,3584]{1,0:T(8,128)(2,1)S(1)}, bf16[8,3584]{1,0:T(8,128)(2,1)S(1)}, u32[]{:S(2)}, u32[]{:S(2)}) collective-permute-start(bf16[8,3584]{1,0:T(8,128)(2,1)S(1)} %get-tuple-element.50), channel_id=1, source_target_pairs={{0,8},{4,12},{8,0},{12,4},{1,9},{5,13},{9,1},{13,5},{2,10},{6,14},... | collective-permute-start | bytes 172040 | tf_op jit(solution)/shard_map/ppermute | solution.py:19
  39.8 1.3 %collective-permute-start.11 = (bf16[8,3584]{1,0:T(8,128)(2,1)S(1)}, bf16[8,3584]{1,0:T(8,128)(2,1)S(1)}, u32[]{:S(2)}, u32[]{:S(2)}) collective-permute-start(bf16[8,3584]{1,0:T(8,128)(2,1)S(1)} %shard_map.149.a_ref), channel_id=1, source_target_pairs={{0,1},{1,0},{2,3},{3,2},{4,5},{5,4},{6,7},{7,6},{8,9},{9,8},{10,11... | collective-permute-start | bytes 172040 | tf_op jit(solution)/shard_map/ppermute | solution.py:19
  41.1 4.2 %collective-permute-start.12 = (bf16[8,3584]{1,0:T(8,128)(2,1)S(1)}, bf16[8,3584]{1,0:T(8,128)(2,1)S(1)}, u32[]{:S(2)}, u32[]{:S(2)}) collective-permute-start(bf16[8,3584]{1,0:T(8,128)(2,1)S(1)} %shard_map.150.a_ref), channel_id=1, source_target_pairs={{0,2},{1,3},{2,0},{3,1},{4,6},{5,7},{6,4},{7,5},{8,10},{9,11},{10,... | collective-permute-start | bytes 172040 | tf_op jit(solution)/shard_map/ppermute | solution.py:19

commit v5 on v4

--- a/solution.py
+++ b/solution.py
@@ -267,8 +267,8 @@
 
 def rest_kernel(n, rest, gain_ref, wg_ref, wu_ref, wd_ref, table_ref, *refs):
     mids, sums, refs = refs[:n], refs[n : n + 3], refs[n + 3 :]
-    (own_ref, total_ref), outs = refs[:2], refs[2 : n + 1]
-    gate_ref, up_ref, square_ref, sum_ref = refs[n + 1 :]
+    total_ref, outs = refs[0], refs[1:n]
+    gate_ref, up_ref, square_ref, sum_ref = refs[n:]
     tokens, cols = mids[0].shape
     experts, width, _ = wd_ref.shape
     rows = tokens // n
@@ -276,9 +276,6 @@
     for k in rest:
         add_block(n, k, mids[k], gain_ref, wg_ref, wu_ref, sums, (gate_ref, up_ref, square_ref))
         sums = (gate_ref, up_ref, square_ref)
-    for k in range(n):
-        got = mids[k][...].astype(jnp.float32)[k * rows : (k + 1) * rows]
-        own_ref[:, pl.ds(pl.multiple_of((me ^ k) * cols, LANES), cols)] = got.astype(jnp.bfloat16)
     inverse = lax.rsqrt(square_ref[:, :1] / (n * cols) + 1e-06)
     lane = lax.broadcasted_iota(jnp.int32, (tokens, LANES), 1) % (LANES // 2)
     for e in range(experts):
@@ -298,6 +295,17 @@
     total_ref[...] = sum_ref[:rows]
     for k in range(1, n):
         outs[k - 1][...] = sum_ref[k * rows : (k + 1) * rows].astype(jnp.bfloat16)
+
+
+def last_kernel(n, a_ref, b_ref, *refs):
+    mids, (own_ref, out_ref) = refs[:n], refs[n:]
+    add_kernel(a_ref, b_ref, out_ref)
+    tokens, cols = mids[0].shape
+    rows = tokens // n
+    me = lax.axis_index("expert")
+    for k in range(n):
+        got = mids[k][...].astype(jnp.float32)[k * rows : (k + 1) * rows]
+        own_ref[:, pl.ds(pl.multiple_of((me ^ k) * cols, LANES), cols)] = got.astype(jnp.bfloat16)
 
 
 def join_kernel(total_ref, *refs):
@@ -421,9 +429,9 @@
             limit=LIMIT,
             flops=FLOPS[4],
         )
-    own_mid, own, *parts = call(
+    own, *parts = call(
         functools.partial(rest_kernel, n, order[AHEAD:]),
-        [bf16(rows, model_d), f32(rows, model_d)] + [bf16(rows, model_d)] * (n - 1),
+        [f32(rows, model_d)] + [bf16(rows, model_d)] * (n - 1),
         gain,
         gate_weights,
         up_weights,
@@ -435,16 +443,23 @@
         scratch=[pltpu.VMEM(x.shape, x.dtype) for x in sum_shapes + [f32(tokens, model_d)]],
         flops=FLOPS[5],
     )
-    back = [swap(parts[k - 1], "expert", n, k) for k in range(n - 1, 0, -1)]
+    back = [swap(parts[k - 1], "expert", n, k) for k in range(1, n)]
     mixed = call(join_kernel, bf16(rows, model_d), own, *back, limit=LIMIT)
-    for step in (1, 2):
-        mixed = call(
-            add_kernel,
-            bf16(rows, model_d),
-            mixed,
-            swap(mixed, "head", head_n, step),
-            limit=LIMIT,
-        )
+    mixed = call(
+        add_kernel,
+        bf16(rows, model_d),
+        mixed,
+        swap(mixed, "head", head_n, 1),
+        limit=LIMIT,
+    )
+    own_mid, mixed = call(
+        functools.partial(last_kernel, n),
+        [bf16(rows, model_d)] * 2,
+        mixed,
+        swap(mixed, "head", head_n, 2),
+        *mids,
+        limit=LIMIT,
+    )
     return own_mid, mixed
 
 

time: 46.1 us -> 44.9 us (0.974)
  waiting for transfers between devices: 17.4 us -> 15.7 us
  starting transfers between devices: 16.9 us -> 17.9 us
  Pallas kernels: 10.9 us -> 10.4 us
    ppermute x13, waiting for transfers between devices: 17.4 us -> 15.7 us  [swap(): return lax.ppermute(x, axis, [(s, s ^ step) for s in range(size)])]
    ppermute x13, starting transfers between devices: 16.9 us -> 17.9 us  [swap(): return lax.ppermute(x, axis, [(s, s ^ step) for s in range(size)])]
    pallas_call x12, Pallas kernels: 10.9 us -> 10.4 us  [call(): pl.pallas_call(body, out_shape=outs, in_specs=[VMEM] * len(args) if specs...]
  transfers between devices with their start and end apart: 13 -> 13, of which waited for: 11 -> 10; matrix products, arithmetic and copies ran while one was open for 0% -> 0% of each run, Pallas kernels for 8% -> 9%
where the time goes in v5:
time: 44.9 us; the launch traced here: 44.8 us
  starting transfers between devices  17.9 us (40%)
  waiting for transfers between devices  15.7 us (35%)
  Pallas kernels  10.4 us (23%)
  between operations  0.77 us (2%)
    ppermute x13, starting transfers between devices, swap(): return lax.ppermute(x, axis, [(s, s ^ step) for s in range(size)])  17.9 us
    ppermute x13, waiting for transfers between devices, swap(): return lax.ppermute(x, axis, [(s, s ^ step) for s in range(size)])  15.7 us
    pallas_call x12, Pallas kernels, call(): pl.pallas_call(body, out_shape=outs, in_specs=[VMEM] * len(args) if specs...  10.4 us
  transfers between devices with their start and end apart: 13, of which 10 were waited for; matrix products, arithmetic and copies ran while one was open for 0% of the time, Pallas kernels for 9%

profile of v5, /device:TPU:0, one launch (start us, length us, event | category | flops | bytes accessed | tf_op | source)
XLA Modules:
  0.0 44.8 jit_solution(6274256544888851475)
XLA Ops:
  0.6 2.1 %shard_map.140 = (bf16[8,1024]{1,0:T(8,128)(2,1)S(1)}, bf16[8,3584]{1,0:T(8,128)(2,1)S(1)}, bf16[8,128]{1,0:T(8,128)(2,1)S(1)}, f32[1,3584]{1,0:T(1,128)S(1)}) custom-call(bf16[8,8,512]{2,1,0:T(8,128)(2,1)} %refs_0_.1, bf16[8,32,512]{2,1,0:T(8,128)(2,1)} %refs_1_.1, bf16[8,8,64]{2,1,0:T(8,128)(2,1)} %refs_2_.1, bf16[8,32,64]{2,1,0:T(8,128)(2,1)} %refs_3_.1, ...), custom_call_target="tpu_custom_call" | custom-call | tf_op jit(solution)/shard_map/pallas_call | solution.py:126
  2.8 5.1 %collective-permute-start = (bf16[8,2048]{1,0:T(8,128)(2,1)S(1)}, bf16[8,2048]{1,0:T(8,128)(2,1)S(1)}, u32[]{:S(2)}, u32[]{:S(2)}) collective-permute-start(bf16[8,2048]{1,0:T(8,128)(2,1)S(1)} %get-tuple-element.30), channel_id=1, source_target_pairs={{0,12},{4,8},{8,4},{12,0},{1,13},{5,9},{9,5},{13,1},{2,14},{6,10},... | collective-permute-start | bytes 98312 | tf_op jit(solution)/shard_map/ppermute | solution.py:19
  8.0 0.6 %collective-permute-start.2 = (bf16[8,2048]{1,0:T(8,128)(2,1)S(1)}, bf16[8,2048]{1,0:T(8,128)(2,1)S(1)}, u32[]{:S(2)}, u32[]{:S(2)}) collective-permute-start(bf16[8,2048]{1,0:T(8,128)(2,1)S(1)} %get-tuple-element.32), channel_id=1, source_target_pairs={{0,4},{4,0},{8,12},{12,8},{1,5},{5,1},{9,13},{13,9},{2,6},{6,2},{1... | collective-permute-start | bytes 98312 | tf_op jit(solution)/shard_map/ppermute | solution.py:19
  8.6 1.3 %collective-permute-done.refs_0_ = bf16[8,2048]{1,0:T(8,128)(2,1)S(1)} collective-permute-done((bf16[8,2048]{1,0:T(8,128)(2,1)S(1)}, bf16[8,2048]{1,0:T(8,128)(2,1)S(1)}, u32[]{:S(2)}, u32[]{:S(2)}) %collective-permute-start) | collective-permute-done | bytes 32800 | tf_op jit(solution)/shard_map/ppermute | solution.py:19
  9.9 2.9 %collective-permute-done.1.refs_1_ = bf16[8,2048]{1,0:T(8,128)(2,1)S(1)} collective-permute-done((bf16[8,2048]{1,0:T(8,128)(2,1)S(1)}, bf16[8,2048]{1,0:T(8,128)(2,1)S(1)}, u32[]{:S(2)}, u32[]{:S(2)}) %collective-permute-start.1) | collective-permute-done | bytes 32800 | tf_op jit(solution)/shard_map/ppermute | solution.py:19
  13.3 1.2 %collective-permute-done.3.b_ref = bf16[32,896]{1,0:T(8,128)(2,1)S(1)} collective-permute-done((bf16[32,896]{1,0:T(8,128)(2,1)S(1)}, bf16[32,896]{1,0:T(8,128)(2,1)S(1)}, u32[]{:S(2)}, u32[]{:S(2)}) %collective-permute-start.3) | collective-permute-done | bytes 57376 | tf_op jit(solution)/shard_map/ppermute | solution.py:19
  14.5 1.6 %collective-permute-start.4 = (bf16[32,896]{1,0:T(8,128)(2,1)S(1)}, bf16[32,896]{1,0:T(8,128)(2,1)S(1)}, u32[]{:S(2)}, u32[]{:S(2)}) collective-permute-start(bf16[32,896]{1,0:T(8,128)(2,1)S(1)} %shard_map.143.a_ref), channel_id=1, source_target_pairs={{0,2},{1,3},{2,0},{3,1},{4,6},{5,7},{6,4},{7,5},{8,10},{9,11},{10,... | collective-permute-start | bytes 172040 | tf_op jit(solution)/shard_map/ppermute | solution.py:19
  16.1 2.7 %collective-permute-done.4.b_ref = bf16[32,896]{1,0:T(8,128)(2,1)S(1)} collective-permute-done((bf16[32,896]{1,0:T(8,128)(2,1)S(1)}, bf16[32,896]{1,0:T(8,128)(2,1)S(1)}, u32[]{:S(2)}, u32[]{:S(2)}) %collective-permute-start.4) | collective-permute-done | bytes 57376 | tf_op jit(solution)/shard_map/ppermute | solution.py:19
  18.8 1.5 %collective-permute-start.7 = (bf16[32,896]{1,0:T(8,128)(2,1)S(1)}, bf16[32,896]{1,0:T(8,128)(2,1)S(1)}, u32[]{:S(2)}, u32[]{:S(2)}) collective-permute-start(bf16[32,896]{1,0:T(8,128)(2,1)S(1)} %shard_map.144.mid_ref.refs_0_), channel_id=1, source_target_pairs={{0,12},{4,8},{8,4},{12,0},{1,13},{5,9},{9,5},{13,1},{2,14},{6,10},... | collective-permute-start | bytes 172040 | tf_op jit(solution)/shard_map/ppermute | solution.py:19
  20.3 0.6 %collective-permute-start.6 = (bf16[32,896]{1,0:T(8,128)(2,1)S(1)}, bf16[32,896]{1,0:T(8,128)(2,1)S(1)}, u32[]{:S(2)}, u32[]{:S(2)}) collective-permute-start(bf16[32,896]{1,0:T(8,128)(2,1)S(1)} %shard_map.144.mid_ref.refs_0_), channel_id=1, source_target_pairs={{0,8},{4,12},{8,0},{12,4},{1,9},{5,13},{9,1},{13,5},{2,10},{6,14},... | collective-permute-start | bytes 172040 | tf_op jit(solution)/shard_map/ppermute | solution.py:19
  21.0 2.3 %collective-permute-start.5 = (bf16[32,896]{1,0:T(8,128)(2,1)S(1)}, bf16[32,896]{1,0:T(8,128)(2,1)S(1)}, u32[]{:S(2)}, u32[]{:S(2)}) collective-permute-start(bf16[32,896]{1,0:T(8,128)(2,1)S(1)} %shard_map.144.mid_ref.refs_0_), channel_id=1, source_target_pairs={{0,4},{4,0},{8,12},{12,8},{1,5},{5,1},{9,13},{13,9},{2,6},{6,2},{1... | collective-permute-start | bytes 172040 | tf_op jit(solution)/shard_map/ppermute | solution.py:19
  23.3 1.3 %shard_map.145 = (f32[32,2048]{1,0:T(8,128)S(1)}, f32[32,2048]{1,0:T(8,128)S(1)}, f32[32,128]{1,0:T(8,128)S(1)}) custom-call(f32[1,3584]{1,0:T(1,128)S(1)} %get-tuple-element.26.gain_ref, bf16[8,3584,256]{2,1,0:T(8,128)(2,1)S(1)} %copy-done, bf16[8,3584,256]{2,1,0:T(8,128)(2,1)S(1)} %copy-done.1, bf16[8,256,3584]{2,1,0:T(8,128)(2,1)S(1)} %copy-done.2, ...), custom_call_target="tpu_custom_call" | custom-call | flops 1000000000 | bytes 1048576 | tf_op jit(solution)/shard_map/pallas_call | solution.py:126
  24.5 0.4 collective-permute-done.7.mid_ref.refs_3_
  25.0 1.3 %shard_map.146 = (f32[32,2048]{1,0:T(8,128)S(1)}, f32[32,2048]{1,0:T(8,128)S(1)}, f32[32,128]{1,0:T(8,128)S(1)}) custom-call(f32[1,3584]{1,0:T(1,128)S(1)} %get-tuple-element.26.gain_ref, bf16[8,3584,256]{2,1,0:T(8,128)(2,1)S(1)} %copy-done, bf16[8,3584,256]{2,1,0:T(8,128)(2,1)S(1)} %copy-done.1, bf16[8,256,3584]{2,1,0:T(8,128)(2,1)S(1)} %copy-done.2, ...), custom_call_target="tpu_custom_call" | custom-call | flops 1000000000 | bytes 1048576 | tf_op jit(solution)/shard_map/pallas_call | solution.py:126
  26.6 1.3 %shard_map.147 = (f32[32,2048]{1,0:T(8,128)S(1)}, f32[32,2048]{1,0:T(8,128)S(1)}, f32[32,128]{1,0:T(8,128)S(1)}) custom-call(f32[1,3584]{1,0:T(1,128)S(1)} %get-tuple-element.26.gain_ref, bf16[8,3584,256]{2,1,0:T(8,128)(2,1)S(1)} %copy-done, bf16[8,3584,256]{2,1,0:T(8,128)(2,1)S(1)} %copy-done.1, bf16[8,256,3584]{2,1,0:T(8,128)(2,1)S(1)} %copy-done.2, ...), custom_call_target="tpu_custom_call" | custom-call | flops 1000000000 | bytes 1048576 | tf_op jit(solution)/shard_map/pallas_call | solution.py:126
  27.9 3.2 %shard_map.148 = (f32[8,3584]{1,0:T(8,128)S(1)}, bf16[8,3584]{1,0:T(8,128)(2,1)S(1)}, bf16[8,3584]{1,0:T(8,128)(2,1)S(1)}, bf16[8,3584]{1,0:T(8,128)(2,1)S(1)}) custom-call(f32[1,3584]{1,0:T(1,128)S(1)} %get-tuple-element.26.gain_ref, bf16[8,3584,256]{2,1,0:T(8,128)(2,1)S(1)} %copy-done, bf16[8,3584,256]{2,1,0:T(8,128)(2,1)S(1)} %copy-done.1, ...), custom_call_target="tpu_custom_call" | custom-call | flops 1000000000 | bytes 1048576 | tf_op jit(solution)/shard_map/pallas_call | solution.py:126
  31.1 1.9 %collective-permute-start.10 = (bf16[8,3584]{1,0:T(8,128)(2,1)S(1)}, bf16[8,3584]{1,0:T(8,128)(2,1)S(1)}, u32[]{:S(2)}, u32[]{:S(2)}) collective-permute-start(bf16[8,3584]{1,0:T(8,128)(2,1)S(1)} %get-tuple-element.49), channel_id=1, source_target_pairs={{0,12},{4,8},{8,4},{12,0},{1,13},{5,9},{9,5},{13,1},{2,14},{6,10},... | collective-permute-start | bytes 172040 | tf_op jit(solution)/shard_map/ppermute | solution.py:19
  33.2 2.3 %collective-permute-start.9 = (bf16[8,3584]{1,0:T(8,128)(2,1)S(1)}, bf16[8,3584]{1,0:T(8,128)(2,1)S(1)}, u32[]{:S(2)}, u32[]{:S(2)}) collective-permute-start(bf16[8,3584]{1,0:T(8,128)(2,1)S(1)} %get-tuple-element.48), channel_id=1, source_target_pairs={{0,8},{4,12},{8,0},{12,4},{1,9},{5,13},{9,1},{13,5},{2,10},{6,14},... | collective-permute-start | bytes 172040 | tf_op jit(solution)/shard_map/ppermute | solution.py:19
  35.6 1.8 %collective-permute-done.10.refs_2_ = bf16[8,3584]{1,0:T(8,128)(2,1)S(1)} collective-permute-done((bf16[8,3584]{1,0:T(8,128)(2,1)S(1)}, bf16[8,3584]{1,0:T(8,128)(2,1)S(1)}, u32[]{:S(2)}, u32[]{:S(2)}) %collective-permute-start.10) | collective-permute-done | bytes 57376 | tf_op jit(solution)/shard_map/ppermute | solution.py:19
  37.4 1.2 %collective-permute-done.8.refs_0_ = bf16[8,3584]{1,0:T(8,128)(2,1)S(1)} collective-permute-done((bf16[8,3584]{1,0:T(8,128)(2,1)S(1)}, bf16[8,3584]{1,0:T(8,128)(2,1)S(1)}, u32[]{:S(2)}, u32[]{:S(2)}) %collective-permute-start.8) | collective-permute-done | bytes 57376 | tf_op jit(solution)/shard_map/ppermute | solution.py:19
  38.6 1.2 %collective-permute-done.11.b_ref = bf16[8,3584]{1,0:T(8,128)(2,1)S(1)} collective-permute-done((bf16[8,3584]{1,0:T(8,128)(2,1)S(1)}, bf16[8,3584]{1,0:T(8,128)(2,1)S(1)}, u32[]{:S(2)}, u32[]{:S(2)}) %collective-permute-start.11) | collective-permute-done | bytes 57376 | tf_op jit(solution)/shard_map/ppermute | solution.py:19
  39.9 1.5 %collective-permute-start.12 = (bf16[8,3584]{1,0:T(8,128)(2,1)S(1)}, bf16[8,3584]{1,0:T(8,128)(2,1)S(1)}, u32[]{:S(2)}, u32[]{:S(2)}) collective-permute-start(bf16[8,3584]{1,0:T(8,128)(2,1)S(1)} %shard_map.150.a_ref), channel_id=1, source_target_pairs={{0,2},{1,3},{2,0},{3,1},{4,6},{5,7},{6,4},{7,5},{8,10},{9,11},{10,... | collective-permute-start | bytes 172040 | tf_op jit(solution)/shard_map/ppermute | solution.py:19
  41.4 2.7 %collective-permute-done.12.b_ref = bf16[8,3584]{1,0:T(8,128)(2,1)S(1)} collective-permute-done((bf16[8,3584]{1,0:T(8,128)(2,1)S(1)}, bf16[8,3584]{1,0:T(8,128)(2,1)S(1)}, u32[]{:S(2)}, u32[]{:S(2)}) %collective-permute-start.12) | collective-permute-done | bytes 57376 | tf_op jit(solution)/shard_map/ppermute | solution.py:19
  44.1 0.7 %shard_map.151 = (bf16[8,3584]{1,0:T(8,128)(2,1)}, bf16[8,3584]{1,0:T(8,128)(2,1)}) custom-call(bf16[8,3584]{1,0:T(8,128)(2,1)S(1)} %shard_map.150.a_ref, bf16[8,3584]{1,0:T(8,128)(2,1)S(1)} %collective-permute-done.12.b_ref, bf16[32,896]{1,0:T(8,128)(2,1)S(1)} %shard_map.144.mid_ref.refs_0_, bf16[32,896]{1,0:T(8,128)(2,1)S(1)} %collective-permute-done.5.refs_1_, ...), custom_call_target="tpu_custom_call" | custom-call | tf_op jit(solution)/shard_map/pallas_call | solution.py:126
  (22 shorter events, 1.2 us)
Async XLA Ops:
  2.8 10.0 %copy-start.3 = (bf16[1024,896]{1,0:T(8,128)(2,1)S(1)}, bf16[1024,896]{1,0:T(8,128)(2,1)}, u32[]{:S(2)}) copy-start(bf16[1024,896]{1,0:T(8,128)(2,1)} %proj_ref.1) | copy-start | bytes 5505028
  2.8 20.5 %copy-start = (bf16[8,3584,256]{2,1,0:T(8,128)(2,1)S(1)}, bf16[8,3584,256]{2,1,0:T(8,128)(2,1)}, u32[]{:S(2)}) copy-start(bf16[8,3584,256]{2,1,0:T(8,128)(2,1)} %wg_ref.7) | copy-start | bytes 44040196
  2.8 20.5 %copy-start.1 = (bf16[8,3584,256]{2,1,0:T(8,128)(2,1)S(1)}, bf16[8,3584,256]{2,1,0:T(8,128)(2,1)}, u32[]{:S(2)}) copy-start(bf16[8,3584,256]{2,1,0:T(8,128)(2,1)} %wu_ref.7) | copy-start | bytes 44040196
  2.8 20.5 %copy-start.2 = (bf16[8,256,3584]{2,1,0:T(8,128)(2,1)S(1)}, bf16[8,256,3584]{2,1,0:T(8,128)(2,1)}, u32[]{:S(2)}) copy-start(bf16[8,256,3584]{2,1,0:T(8,128)(2,1)} %wd_ref.1) | copy-start | bytes 44040196
  2.8 7.0 %collective-permute-start = (bf16[8,2048]{1,0:T(8,128)(2,1)S(1)}, bf16[8,2048]{1,0:T(8,128)(2,1)S(1)}, u32[]{:S(2)}, u32[]{:S(2)}) collective-permute-start(bf16[8,2048]{1,0:T(8,128)(2,1)S(1)} %get-tuple-element.30), channel_id=1, source_target_pairs={{0,12},{4,8},{8,4},{12,0},{1,13},{5,9},{9,5},{13,1},{2,14},{6,10},... | collective-permute-start | bytes 98312 | tf_op jit(solution)/shard_map/ppermute | solution.py:19
  8.0 4.8 %collective-permute-start.1 = (bf16[8,2048]{1,0:T(8,128)(2,1)S(1)}, bf16[8,2048]{1,0:T(8,128)(2,1)S(1)}, u32[]{:S(2)}, u32[]{:S(2)}) collective-permute-start(bf16[8,2048]{1,0:T(8,128)(2,1)S(1)} %get-tuple-element.31), channel_id=1, source_target_pairs={{0,8},{4,12},{8,0},{12,4},{1,9},{5,13},{9,1},{13,5},{2,10},{6,14},... | collective-permute-start | bytes 98312 | tf_op jit(solution)/shard_map/ppermute | solution.py:19
  8.0 4.8 %collective-permute-start.2 = (bf16[8,2048]{1,0:T(8,128)(2,1)S(1)}, bf16[8,2048]{1,0:T(8,128)(2,1)S(1)}, u32[]{:S(2)}, u32[]{:S(2)}) collective-permute-start(bf16[8,2048]{1,0:T(8,128)(2,1)S(1)} %get-tuple-element.32), channel_id=1, source_target_pairs={{0,4},{4,0},{8,12},{12,8},{1,5},{5,1},{9,13},{13,9},{2,6},{6,2},{1... | collective-permute-start | bytes 98312 | tf_op jit(solution)/shard_map/ppermute | solution.py:19
  13.2 1.3 %collective-permute-start.3 = (bf16[32,896]{1,0:T(8,128)(2,1)S(1)}, bf16[32,896]{1,0:T(8,128)(2,1)S(1)}, u32[]{:S(2)}, u32[]{:S(2)}) collective-permute-start(bf16[32,896]{1,0:T(8,128)(2,1)S(1)} %get-tuple-element.35.a_ref), channel_id=1, source_target_pairs={{0,1},{1,0},{2,3},{3,2},{4,5},{5,4},{6,7},{7,6},{8,9},{9,8},{10,11... | collective-permute-start | bytes 172040 | tf_op jit(solution)/shard_map/ppermute | solution.py:19
  14.5 4.2 %collective-permute-start.4 = (bf16[32,896]{1,0:T(8,128)(2,1)S(1)}, bf16[32,896]{1,0:T(8,128)(2,1)S(1)}, u32[]{:S(2)}, u32[]{:S(2)}) collective-permute-start(bf16[32,896]{1,0:T(8,128)(2,1)S(1)} %shard_map.143.a_ref), channel_id=1, source_target_pairs={{0,2},{1,3},{2,0},{3,1},{4,6},{5,7},{6,4},{7,5},{8,10},{9,11},{10,... | collective-permute-start | bytes 172040 | tf_op jit(solution)/shard_map/ppermute | solution.py:19
  18.8 6.2 %collective-permute-start.7 = (bf16[32,896]{1,0:T(8,128)(2,1)S(1)}, bf16[32,896]{1,0:T(8,128)(2,1)S(1)}, u32[]{:S(2)}, u32[]{:S(2)}) collective-permute-start(bf16[32,896]{1,0:T(8,128)(2,1)S(1)} %shard_map.144.mid_ref.refs_0_), channel_id=1, source_target_pairs={{0,12},{4,8},{8,4},{12,0},{1,13},{5,9},{9,5},{13,1},{2,14},{6,10},... | collective-permute-start | bytes 172040 | tf_op jit(solution)/shard_map/ppermute | solution.py:19
  20.3 6.2 %collective-permute-start.6 = (bf16[32,896]{1,0:T(8,128)(2,1)S(1)}, bf16[32,896]{1,0:T(8,128)(2,1)S(1)}, u32[]{:S(2)}, u32[]{:S(2)}) collective-permute-start(bf16[32,896]{1,0:T(8,128)(2,1)S(1)} %shard_map.144.mid_ref.refs_0_), channel_id=1, source_target_pairs={{0,8},{4,12},{8,0},{12,4},{1,9},{5,13},{9,1},{13,5},{2,10},{6,14},... | collective-permute-start | bytes 172040 | tf_op jit(solution)/shard_map/ppermute | solution.py:19
  21.0 6.9 %collective-permute-start.5 = (bf16[32,896]{1,0:T(8,128)(2,1)S(1)}, bf16[32,896]{1,0:T(8,128)(2,1)S(1)}, u32[]{:S(2)}, u32[]{:S(2)}) collective-permute-start(bf16[32,896]{1,0:T(8,128)(2,1)S(1)} %shard_map.144.mid_ref.refs_0_), channel_id=1, source_target_pairs={{0,4},{4,0},{8,12},{12,8},{1,5},{5,1},{9,13},{13,9},{2,6},{6,2},{1... | collective-permute-start | bytes 172040 | tf_op jit(solution)/shard_map/ppermute | solution.py:19
  31.1 6.3 %collective-permute-start.10 = (bf16[8,3584]{1,0:T(8,128)(2,1)S(1)}, bf16[8,3584]{1,0:T(8,128)(2,1)S(1)}, u32[]{:S(2)}, u32[]{:S(2)}) collective-permute-start(bf16[8,3584]{1,0:T(8,128)(2,1)S(1)} %get-tuple-element.49), channel_id=1, source_target_pairs={{0,12},{4,8},{8,4},{12,0},{1,13},{5,9},{9,5},{13,1},{2,14},{6,10},... | collective-permute-start | bytes 172040 | tf_op jit(solution)/shard_map/ppermute | solution.py:19
  33.0 5.5 %collective-permute-start.8 = (bf16[8,3584]{1,0:T(8,128)(2,1)S(1)}, bf16[8,3584]{1,0:T(8,128)(2,1)S(1)}, u32[]{:S(2)}, u32[]{:S(2)}) collective-permute-start(bf16[8,3584]{1,0:T(8,128)(2,1)S(1)} %get-tuple-element.47), channel_id=1, source_target_pairs={{0,4},{4,0},{8,12},{12,8},{1,5},{5,1},{9,13},{13,9},{2,6},{6,2},{1... | collective-permute-start | bytes 172040 | tf_op jit(solution)/shard_map/ppermute | solution.py:19
  33.2 5.3 %collective-permute-start.9 = (bf16[8,3584]{1,0:T(8,128)(2,1)S(1)}, bf16[8,3584]{1,0:T(8,128)(2,1)S(1)}, u32[]{:S(2)}, u32[]{:S(2)}) collective-permute-start(bf16[8,3584]{1,0:T(8,128)(2,1)S(1)} %get-tuple-element.48), channel_id=1, source_target_pairs={{0,8},{4,12},{8,0},{12,4},{1,9},{5,13},{9,1},{13,5},{2,10},{6,14},... | collective-permute-start | bytes 172040 | tf_op jit(solution)/shard_map/ppermute | solution.py:19
  38.6 1.3 %collective-permute-start.11 = (bf16[8,3584]{1,0:T(8,128)(2,1)S(1)}, bf16[8,3584]{1,0:T(8,128)(2,1)S(1)}, u32[]{:S(2)}, u32[]{:S(2)}) collective-permute-start(bf16[8,3584]{1,0:T(8,128)(2,1)S(1)} %shard_map.149.a_ref), channel_id=1, source_target_pairs={{0,1},{1,0},{2,3},{3,2},{4,5},{5,4},{6,7},{7,6},{8,9},{9,8},{10,11... | collective-permute-start | bytes 172040 | tf_op jit(solution)/shard_map/ppermute | solution.py:19
  39.9 4.2 %collective-permute-start.12 = (bf16[8,3584]{1,0:T(8,128)(2,1)S(1)}, bf16[8,3584]{1,0:T(8,128)(2,1)S(1)}, u32[]{:S(2)}, u32[]{:S(2)}) collective-permute-start(bf16[8,3584]{1,0:T(8,128)(2,1)S(1)} %shard_map.150.a_ref), channel_id=1, source_target_pairs={{0,2},{1,3},{2,0},{3,1},{4,6},{5,7},{6,4},{7,5},{8,10},{9,11},{10,... | collective-permute-start | bytes 172040 | tf_op jit(solution)/shard_map/ppermute | solution.py:19

commit v6 on v5

--- a/solution.py
+++ b/solution.py
@@ -414,7 +414,7 @@
     mids = [mid] + [swap(mid, "expert", n, k) for k in range(1, n)]
     gate_weights, up_weights, down_weights = in_vmem(w_gate), in_vmem(w_up), in_vmem(w_down)
     sum_shapes = [f32(tokens, experts * hidden_f)] * 2 + [f32(tokens, LANES)]
-    order = [0] + list(range(n - 1, 0, -1))
+    order = list(range(n))
     sums = []
     for k in order[:AHEAD]:
         sums = call(

time: 44.9 us -> 44.2 us (0.984)
  waiting for transfers between devices: 15.7 us -> 15 us
    ppermute x13, waiting for transfers between devices: 15.7 us -> 15 us  [swap(): return lax.ppermute(x, axis, [(s, s ^ step) for s in range(size)])]
  transfers between devices with their start and end apart: 13 -> 13, of which waited for: 10 -> 9; matrix products, arithmetic and copies ran while one was open for 0% -> 0% of each run, Pallas kernels for 9% -> 9%
where the time goes in v6:
time: 44.2 us; the launch traced here: 44.1 us
  starting transfers between devices  17.9 us (40%)
  waiting for transfers between devices  15 us (34%)
  Pallas kernels  10.4 us (24%)
  between operations  0.79 us (2%)
    ppermute x13, starting transfers between devices, swap(): return lax.ppermute(x, axis, [(s, s ^ step) for s in range(size)])  17.9 us
    ppermute x13, waiting for transfers between devices, swap(): return lax.ppermute(x, axis, [(s, s ^ step) for s in range(size)])  15 us
    pallas_call x12, Pallas kernels, call(): pl.pallas_call(body, out_shape=outs, in_specs=[VMEM] * len(args) if specs...  10.4 us
  transfers between devices with their start and end apart: 13, of which 9 were waited for; matrix products, arithmetic and copies ran while one was open for 0% of the time, Pallas kernels for 9%

profile of v6, /device:TPU:0, one launch (start us, length us, event | category | flops | bytes accessed | tf_op | source)
XLA Modules:
  0.0 44.1 jit_solution(16632428083054838726)
XLA Ops:
  0.6 2.1 %shard_map.140 = (bf16[8,1024]{1,0:T(8,128)(2,1)S(1)}, bf16[8,3584]{1,0:T(8,128)(2,1)S(1)}, bf16[8,128]{1,0:T(8,128)(2,1)S(1)}, f32[1,3584]{1,0:T(1,128)S(1)}) custom-call(bf16[8,8,512]{2,1,0:T(8,128)(2,1)} %refs_0_.1, bf16[8,32,512]{2,1,0:T(8,128)(2,1)} %refs_1_.1, bf16[8,8,64]{2,1,0:T(8,128)(2,1)} %refs_2_.1, bf16[8,32,64]{2,1,0:T(8,128)(2,1)} %refs_3_.1, ...), custom_call_target="tpu_custom_call" | custom-call | tf_op jit(solution)/shard_map/pallas_call | solution.py:126
  2.8 5.1 %collective-permute-start = (bf16[8,2048]{1,0:T(8,128)(2,1)S(1)}, bf16[8,2048]{1,0:T(8,128)(2,1)S(1)}, u32[]{:S(2)}, u32[]{:S(2)}) collective-permute-start(bf16[8,2048]{1,0:T(8,128)(2,1)S(1)} %get-tuple-element.30), channel_id=1, source_target_pairs={{0,12},{4,8},{8,4},{12,0},{1,13},{5,9},{9,5},{13,1},{2,14},{6,10},... | collective-permute-start | bytes 98312 | tf_op jit(solution)/shard_map/ppermute | solution.py:19
  8.0 0.6 %collective-permute-start.2 = (bf16[8,2048]{1,0:T(8,128)(2,1)S(1)}, bf16[8,2048]{1,0:T(8,128)(2,1)S(1)}, u32[]{:S(2)}, u32[]{:S(2)}) collective-permute-start(bf16[8,2048]{1,0:T(8,128)(2,1)S(1)} %get-tuple-element.32), channel_id=1, source_target_pairs={{0,4},{4,0},{8,12},{12,8},{1,5},{5,1},{9,13},{13,9},{2,6},{6,2},{1... | collective-permute-start | bytes 98312 | tf_op jit(solution)/shard_map/ppermute | solution.py:19
  8.6 1.3 %collective-permute-done.refs_0_ = bf16[8,2048]{1,0:T(8,128)(2,1)S(1)} collective-permute-done((bf16[8,2048]{1,0:T(8,128)(2,1)S(1)}, bf16[8,2048]{1,0:T(8,128)(2,1)S(1)}, u32[]{:S(2)}, u32[]{:S(2)}) %collective-permute-start) | collective-permute-done | bytes 32800 | tf_op jit(solution)/shard_map/ppermute | solution.py:19
  9.9 2.9 %collective-permute-done.1.refs_1_ = bf16[8,2048]{1,0:T(8,128)(2,1)S(1)} collective-permute-done((bf16[8,2048]{1,0:T(8,128)(2,1)S(1)}, bf16[8,2048]{1,0:T(8,128)(2,1)S(1)}, u32[]{:S(2)}, u32[]{:S(2)}) %collective-permute-start.1) | collective-permute-done | bytes 32800 | tf_op jit(solution)/shard_map/ppermute | solution.py:19
  12.8 0.4 shard_map.142
  13.3 1.2 %collective-permute-done.3.b_ref = bf16[32,896]{1,0:T(8,128)(2,1)S(1)} collective-permute-done((bf16[32,896]{1,0:T(8,128)(2,1)S(1)}, bf16[32,896]{1,0:T(8,128)(2,1)S(1)}, u32[]{:S(2)}, u32[]{:S(2)}) %collective-permute-start.3) | collective-permute-done | bytes 57376 | tf_op jit(solution)/shard_map/ppermute | solution.py:19
  14.5 1.6 %collective-permute-start.4 = (bf16[32,896]{1,0:T(8,128)(2,1)S(1)}, bf16[32,896]{1,0:T(8,128)(2,1)S(1)}, u32[]{:S(2)}, u32[]{:S(2)}) collective-permute-start(bf16[32,896]{1,0:T(8,128)(2,1)S(1)} %shard_map.143.a_ref), channel_id=1, source_target_pairs={{0,2},{1,3},{2,0},{3,1},{4,6},{5,7},{6,4},{7,5},{8,10},{9,11},{10,... | collective-permute-start | bytes 172040 | tf_op jit(solution)/shard_map/ppermute | solution.py:19
  16.1 2.7 %collective-permute-done.4.b_ref = bf16[32,896]{1,0:T(8,128)(2,1)S(1)} collective-permute-done((bf16[32,896]{1,0:T(8,128)(2,1)S(1)}, bf16[32,896]{1,0:T(8,128)(2,1)S(1)}, u32[]{:S(2)}, u32[]{:S(2)}) %collective-permute-start.4) | collective-permute-done | bytes 57376 | tf_op jit(solution)/shard_map/ppermute | solution.py:19
  18.9 2.1 %collective-permute-start.6 = (bf16[32,896]{1,0:T(8,128)(2,1)S(1)}, bf16[32,896]{1,0:T(8,128)(2,1)S(1)}, u32[]{:S(2)}, u32[]{:S(2)}) collective-permute-start(bf16[32,896]{1,0:T(8,128)(2,1)S(1)} %shard_map.144.mid_ref.refs_0_), channel_id=1, source_target_pairs={{0,8},{4,12},{8,0},{12,4},{1,9},{5,13},{9,1},{13,5},{2,10},{6,14},... | collective-permute-start | bytes 172040 | tf_op jit(solution)/shard_map/ppermute | solution.py:19
  21.0 2.3 %collective-permute-start.7 = (bf16[32,896]{1,0:T(8,128)(2,1)S(1)}, bf16[32,896]{1,0:T(8,128)(2,1)S(1)}, u32[]{:S(2)}, u32[]{:S(2)}) collective-permute-start(bf16[32,896]{1,0:T(8,128)(2,1)S(1)} %shard_map.144.mid_ref.refs_0_), channel_id=1, source_target_pairs={{0,12},{4,8},{8,4},{12,0},{1,13},{5,9},{9,5},{13,1},{2,14},{6,10},... | collective-permute-start | bytes 172040 | tf_op jit(solution)/shard_map/ppermute | solution.py:19
  23.3 1.3 %shard_map.145 = (f32[32,2048]{1,0:T(8,128)S(1)}, f32[32,2048]{1,0:T(8,128)S(1)}, f32[32,128]{1,0:T(8,128)S(1)}) custom-call(f32[1,3584]{1,0:T(1,128)S(1)} %get-tuple-element.26.gain_ref, bf16[8,3584,256]{2,1,0:T(8,128)(2,1)S(1)} %copy-done, bf16[8,3584,256]{2,1,0:T(8,128)(2,1)S(1)} %copy-done.1, bf16[8,256,3584]{2,1,0:T(8,128)(2,1)S(1)} %copy-done.2, ...), custom_call_target="tpu_custom_call" | custom-call | flops 1000000000 | bytes 1048576 | tf_op jit(solution)/shard_map/pallas_call | solution.py:126
  24.5 1.3 %shard_map.146 = (f32[32,2048]{1,0:T(8,128)S(1)}, f32[32,2048]{1,0:T(8,128)S(1)}, f32[32,128]{1,0:T(8,128)S(1)}) custom-call(f32[1,3584]{1,0:T(1,128)S(1)} %get-tuple-element.26.gain_ref, bf16[8,3584,256]{2,1,0:T(8,128)(2,1)S(1)} %copy-done, bf16[8,3584,256]{2,1,0:T(8,128)(2,1)S(1)} %copy-done.1, bf16[8,256,3584]{2,1,0:T(8,128)(2,1)S(1)} %copy-done.2, ...), custom_call_target="tpu_custom_call" | custom-call | flops 1000000000 | bytes 1048576 | tf_op jit(solution)/shard_map/pallas_call | solution.py:126
  25.8 1.3 %shard_map.147 = (f32[32,2048]{1,0:T(8,128)S(1)}, f32[32,2048]{1,0:T(8,128)S(1)}, f32[32,128]{1,0:T(8,128)S(1)}) custom-call(f32[1,3584]{1,0:T(1,128)S(1)} %get-tuple-element.26.gain_ref, bf16[8,3584,256]{2,1,0:T(8,128)(2,1)S(1)} %copy-done, bf16[8,3584,256]{2,1,0:T(8,128)(2,1)S(1)} %copy-done.1, bf16[8,256,3584]{2,1,0:T(8,128)(2,1)S(1)} %copy-done.2, ...), custom_call_target="tpu_custom_call" | custom-call | flops 1000000000 | bytes 1048576 | tf_op jit(solution)/shard_map/pallas_call | solution.py:126
  27.1 3.2 %shard_map.148 = (f32[8,3584]{1,0:T(8,128)S(1)}, bf16[8,3584]{1,0:T(8,128)(2,1)S(1)}, bf16[8,3584]{1,0:T(8,128)(2,1)S(1)}, bf16[8,3584]{1,0:T(8,128)(2,1)S(1)}) custom-call(f32[1,3584]{1,0:T(1,128)S(1)} %get-tuple-element.26.gain_ref, bf16[8,3584,256]{2,1,0:T(8,128)(2,1)S(1)} %copy-done, bf16[8,3584,256]{2,1,0:T(8,128)(2,1)S(1)} %copy-done.1, ...), custom_call_target="tpu_custom_call" | custom-call | flops 1000000000 | bytes 1048576 | tf_op jit(solution)/shard_map/pallas_call | solution.py:126
  30.4 2.4 %collective-permute-start.10 = (bf16[8,3584]{1,0:T(8,128)(2,1)S(1)}, bf16[8,3584]{1,0:T(8,128)(2,1)S(1)}, u32[]{:S(2)}, u32[]{:S(2)}) collective-permute-start(bf16[8,3584]{1,0:T(8,128)(2,1)S(1)} %get-tuple-element.49), channel_id=1, source_target_pairs={{0,12},{4,8},{8,4},{12,0},{1,13},{5,9},{9,5},{13,1},{2,14},{6,10},... | collective-permute-start | bytes 172040 | tf_op jit(solution)/shard_map/ppermute | solution.py:19
  32.8 2.1 %collective-permute-start.9 = (bf16[8,3584]{1,0:T(8,128)(2,1)S(1)}, bf16[8,3584]{1,0:T(8,128)(2,1)S(1)}, u32[]{:S(2)}, u32[]{:S(2)}) collective-permute-start(bf16[8,3584]{1,0:T(8,128)(2,1)S(1)} %get-tuple-element.48), channel_id=1, source_target_pairs={{0,8},{4,12},{8,0},{12,4},{1,9},{5,13},{9,1},{13,5},{2,10},{6,14},... | collective-permute-start | bytes 172040 | tf_op jit(solution)/shard_map/ppermute | solution.py:19
  34.8 1.6 %collective-permute-done.10.refs_2_ = bf16[8,3584]{1,0:T(8,128)(2,1)S(1)} collective-permute-done((bf16[8,3584]{1,0:T(8,128)(2,1)S(1)}, bf16[8,3584]{1,0:T(8,128)(2,1)S(1)}, u32[]{:S(2)}, u32[]{:S(2)}) %collective-permute-start.10) | collective-permute-done | bytes 57376 | tf_op jit(solution)/shard_map/ppermute | solution.py:19
  36.4 0.6 %collective-permute-done.8.refs_0_ = bf16[8,3584]{1,0:T(8,128)(2,1)S(1)} collective-permute-done((bf16[8,3584]{1,0:T(8,128)(2,1)S(1)}, bf16[8,3584]{1,0:T(8,128)(2,1)S(1)}, u32[]{:S(2)}, u32[]{:S(2)}) %collective-permute-start.8) | collective-permute-done | bytes 57376 | tf_op jit(solution)/shard_map/ppermute | solution.py:19
  37.0 0.8 %collective-permute-done.9.refs_1_ = bf16[8,3584]{1,0:T(8,128)(2,1)S(1)} collective-permute-done((bf16[8,3584]{1,0:T(8,128)(2,1)S(1)}, bf16[8,3584]{1,0:T(8,128)(2,1)S(1)}, u32[]{:S(2)}, u32[]{:S(2)}) %collective-permute-start.9) | collective-permute-done | bytes 57376 | tf_op jit(solution)/shard_map/ppermute | solution.py:19
  37.9 1.2 %collective-permute-done.11.b_ref = bf16[8,3584]{1,0:T(8,128)(2,1)S(1)} collective-permute-done((bf16[8,3584]{1,0:T(8,128)(2,1)S(1)}, bf16[8,3584]{1,0:T(8,128)(2,1)S(1)}, u32[]{:S(2)}, u32[]{:S(2)}) %collective-permute-start.11) | collective-permute-done | bytes 57376 | tf_op jit(solution)/shard_map/ppermute | solution.py:19
  39.2 1.6 %collective-permute-start.12 = (bf16[8,3584]{1,0:T(8,128)(2,1)S(1)}, bf16[8,3584]{1,0:T(8,128)(2,1)S(1)}, u32[]{:S(2)}, u32[]{:S(2)}) collective-permute-start(bf16[8,3584]{1,0:T(8,128)(2,1)S(1)} %shard_map.150.a_ref), channel_id=1, source_target_pairs={{0,2},{1,3},{2,0},{3,1},{4,6},{5,7},{6,4},{7,5},{8,10},{9,11},{10,... | collective-permute-start | bytes 172040 | tf_op jit(solution)/shard_map/ppermute | solution.py:19
  40.8 2.7 %collective-permute-done.12.b_ref = bf16[8,3584]{1,0:T(8,128)(2,1)S(1)} collective-permute-done((bf16[8,3584]{1,0:T(8,128)(2,1)S(1)}, bf16[8,3584]{1,0:T(8,128)(2,1)S(1)}, u32[]{:S(2)}, u32[]{:S(2)}) %collective-permute-start.12) | collective-permute-done | bytes 57376 | tf_op jit(solution)/shard_map/ppermute | solution.py:19
  43.4 0.7 %shard_map.151 = (bf16[8,3584]{1,0:T(8,128)(2,1)}, bf16[8,3584]{1,0:T(8,128)(2,1)}) custom-call(bf16[8,3584]{1,0:T(8,128)(2,1)S(1)} %shard_map.150.a_ref, bf16[8,3584]{1,0:T(8,128)(2,1)S(1)} %collective-permute-done.12.b_ref, bf16[32,896]{1,0:T(8,128)(2,1)S(1)} %shard_map.144.mid_ref.refs_0_, bf16[32,896]{1,0:T(8,128)(2,1)S(1)} %collective-permute-done.5.mid_ref.refs_1_, ...), custom_call_target="tpu_custom_call" | custom-call | tf_op jit(solution)/shard_map/pallas_call | solution.py:126
  (22 shorter events, 0.4 us)
Async XLA Ops:
  2.8 10.0 %copy-start.3 = (bf16[1024,896]{1,0:T(8,128)(2,1)S(1)}, bf16[1024,896]{1,0:T(8,128)(2,1)}, u32[]{:S(2)}) copy-start(bf16[1024,896]{1,0:T(8,128)(2,1)} %proj_ref.1) | copy-start | bytes 5505028
  2.8 20.5 %copy-start = (bf16[8,3584,256]{2,1,0:T(8,128)(2,1)S(1)}, bf16[8,3584,256]{2,1,0:T(8,128)(2,1)}, u32[]{:S(2)}) copy-start(bf16[8,3584,256]{2,1,0:T(8,128)(2,1)} %wg_ref.7) | copy-start | bytes 44040196
  2.8 20.5 %copy-start.1 = (bf16[8,3584,256]{2,1,0:T(8,128)(2,1)S(1)}, bf16[8,3584,256]{2,1,0:T(8,128)(2,1)}, u32[]{:S(2)}) copy-start(bf16[8,3584,256]{2,1,0:T(8,128)(2,1)} %wu_ref.7) | copy-start | bytes 44040196
  2.8 20.5 %copy-start.2 = (bf16[8,256,3584]{2,1,0:T(8,128)(2,1)S(1)}, bf16[8,256,3584]{2,1,0:T(8,128)(2,1)}, u32[]{:S(2)}) copy-start(bf16[8,256,3584]{2,1,0:T(8,128)(2,1)} %wd_ref.1) | copy-start | bytes 44040196
  2.8 7.0 %collective-permute-start = (bf16[8,2048]{1,0:T(8,128)(2,1)S(1)}, bf16[8,2048]{1,0:T(8,128)(2,1)S(1)}, u32[]{:S(2)}, u32[]{:S(2)}) collective-permute-start(bf16[8,2048]{1,0:T(8,128)(2,1)S(1)} %get-tuple-element.30), channel_id=1, source_target_pairs={{0,12},{4,8},{8,4},{12,0},{1,13},{5,9},{9,5},{13,1},{2,14},{6,10},... | collective-permute-start | bytes 98312 | tf_op jit(solution)/shard_map/ppermute | solution.py:19
  8.0 4.8 %collective-permute-start.1 = (bf16[8,2048]{1,0:T(8,128)(2,1)S(1)}, bf16[8,2048]{1,0:T(8,128)(2,1)S(1)}, u32[]{:S(2)}, u32[]{:S(2)}) collective-permute-start(bf16[8,2048]{1,0:T(8,128)(2,1)S(1)} %get-tuple-element.31), channel_id=1, source_target_pairs={{0,8},{4,12},{8,0},{12,4},{1,9},{5,13},{9,1},{13,5},{2,10},{6,14},... | collective-permute-start | bytes 98312 | tf_op jit(solution)/shard_map/ppermute | solution.py:19
  8.0 4.8 %collective-permute-start.2 = (bf16[8,2048]{1,0:T(8,128)(2,1)S(1)}, bf16[8,2048]{1,0:T(8,128)(2,1)S(1)}, u32[]{:S(2)}, u32[]{:S(2)}) collective-permute-start(bf16[8,2048]{1,0:T(8,128)(2,1)S(1)} %get-tuple-element.32), channel_id=1, source_target_pairs={{0,4},{4,0},{8,12},{12,8},{1,5},{5,1},{9,13},{13,9},{2,6},{6,2},{1... | collective-permute-start | bytes 98312 | tf_op jit(solution)/shard_map/ppermute | solution.py:19
  13.2 1.3 %collective-permute-start.3 = (bf16[32,896]{1,0:T(8,128)(2,1)S(1)}, bf16[32,896]{1,0:T(8,128)(2,1)S(1)}, u32[]{:S(2)}, u32[]{:S(2)}) collective-permute-start(bf16[32,896]{1,0:T(8,128)(2,1)S(1)} %get-tuple-element.35.a_ref), channel_id=1, source_target_pairs={{0,1},{1,0},{2,3},{3,2},{4,5},{5,4},{6,7},{7,6},{8,9},{9,8},{10,11... | collective-permute-start | bytes 172040 | tf_op jit(solution)/shard_map/ppermute | solution.py:19
  14.5 4.2 %collective-permute-start.4 = (bf16[32,896]{1,0:T(8,128)(2,1)S(1)}, bf16[32,896]{1,0:T(8,128)(2,1)S(1)}, u32[]{:S(2)}, u32[]{:S(2)}) collective-permute-start(bf16[32,896]{1,0:T(8,128)(2,1)S(1)} %shard_map.143.a_ref), channel_id=1, source_target_pairs={{0,2},{1,3},{2,0},{3,1},{4,6},{5,7},{6,4},{7,5},{8,10},{9,11},{10,... | collective-permute-start | bytes 172040 | tf_op jit(solution)/shard_map/ppermute | solution.py:19
  18.8 5.7 %collective-permute-start.5 = (bf16[32,896]{1,0:T(8,128)(2,1)S(1)}, bf16[32,896]{1,0:T(8,128)(2,1)S(1)}, u32[]{:S(2)}, u32[]{:S(2)}) collective-permute-start(bf16[32,896]{1,0:T(8,128)(2,1)S(1)} %shard_map.144.mid_ref.refs_0_), channel_id=1, source_target_pairs={{0,4},{4,0},{8,12},{12,8},{1,5},{5,1},{9,13},{13,9},{2,6},{6,2},{1... | collective-permute-start | bytes 172040 | tf_op jit(solution)/shard_map/ppermute | solution.py:19
  18.9 7.0 %collective-permute-start.6 = (bf16[32,896]{1,0:T(8,128)(2,1)S(1)}, bf16[32,896]{1,0:T(8,128)(2,1)S(1)}, u32[]{:S(2)}, u32[]{:S(2)}) collective-permute-start(bf16[32,896]{1,0:T(8,128)(2,1)S(1)} %shard_map.144.mid_ref.refs_0_), channel_id=1, source_target_pairs={{0,8},{4,12},{8,0},{12,4},{1,9},{5,13},{9,1},{13,5},{2,10},{6,14},... | collective-permute-start | bytes 172040 | tf_op jit(solution)/shard_map/ppermute | solution.py:19
  21.0 6.2 %collective-permute-start.7 = (bf16[32,896]{1,0:T(8,128)(2,1)S(1)}, bf16[32,896]{1,0:T(8,128)(2,1)S(1)}, u32[]{:S(2)}, u32[]{:S(2)}) collective-permute-start(bf16[32,896]{1,0:T(8,128)(2,1)S(1)} %shard_map.144.mid_ref.refs_0_), channel_id=1, source_target_pairs={{0,12},{4,8},{8,4},{12,0},{1,13},{5,9},{9,5},{13,1},{2,14},{6,10},... | collective-permute-start | bytes 172040 | tf_op jit(solution)/shard_map/ppermute | solution.py:19
  30.4 6.1 %collective-permute-start.10 = (bf16[8,3584]{1,0:T(8,128)(2,1)S(1)}, bf16[8,3584]{1,0:T(8,128)(2,1)S(1)}, u32[]{:S(2)}, u32[]{:S(2)}) collective-permute-start(bf16[8,3584]{1,0:T(8,128)(2,1)S(1)} %get-tuple-element.49), channel_id=1, source_target_pairs={{0,12},{4,8},{8,4},{12,0},{1,13},{5,9},{9,5},{13,1},{2,14},{6,10},... | collective-permute-start | bytes 172040 | tf_op jit(solution)/shard_map/ppermute | solution.py:19
  32.7 4.3 %collective-permute-start.8 = (bf16[8,3584]{1,0:T(8,128)(2,1)S(1)}, bf16[8,3584]{1,0:T(8,128)(2,1)S(1)}, u32[]{:S(2)}, u32[]{:S(2)}) collective-permute-start(bf16[8,3584]{1,0:T(8,128)(2,1)S(1)} %get-tuple-element.47), channel_id=1, source_target_pairs={{0,4},{4,0},{8,12},{12,8},{1,5},{5,1},{9,13},{13,9},{2,6},{6,2},{1... | collective-permute-start | bytes 172040 | tf_op jit(solution)/shard_map/ppermute | solution.py:19
  32.8 5.1 %collective-permute-start.9 = (bf16[8,3584]{1,0:T(8,128)(2,1)S(1)}, bf16[8,3584]{1,0:T(8,128)(2,1)S(1)}, u32[]{:S(2)}, u32[]{:S(2)}) collective-permute-start(bf16[8,3584]{1,0:T(8,128)(2,1)S(1)} %get-tuple-element.48), channel_id=1, source_target_pairs={{0,8},{4,12},{8,0},{12,4},{1,9},{5,13},{9,1},{13,5},{2,10},{6,14},... | collective-permute-start | bytes 172040 | tf_op jit(solution)/shard_map/ppermute | solution.py:19
  37.9 1.3 %collective-permute-start.11 = (bf16[8,3584]{1,0:T(8,128)(2,1)S(1)}, bf16[8,3584]{1,0:T(8,128)(2,1)S(1)}, u32[]{:S(2)}, u32[]{:S(2)}) collective-permute-start(bf16[8,3584]{1,0:T(8,128)(2,1)S(1)} %shard_map.149.a_ref), channel_id=1, source_target_pairs={{0,1},{1,0},{2,3},{3,2},{4,5},{5,4},{6,7},{7,6},{8,9},{9,8},{10,11... | collective-permute-start | bytes 172040 | tf_op jit(solution)/shard_map/ppermute | solution.py:19
  39.2 4.2 %collective-permute-start.12 = (bf16[8,3584]{1,0:T(8,128)(2,1)S(1)}, bf16[8,3584]{1,0:T(8,128)(2,1)S(1)}, u32[]{:S(2)}, u32[]{:S(2)}) collective-permute-start(bf16[8,3584]{1,0:T(8,128)(2,1)S(1)} %shard_map.150.a_ref), channel_id=1, source_target_pairs={{0,2},{1,3},{2,0},{3,1},{4,6},{5,7},{6,4},{7,5},{8,10},{9,11},{10,... | collective-permute-start | bytes 172040 | tf_op jit(solution)/shard_map/ppermute | solution.py:19

commit v7 on v6

--- a/solution.py
+++ b/solution.py
@@ -449,14 +449,14 @@
         add_kernel,
         bf16(rows, model_d),
         mixed,
-        swap(mixed, "head", head_n, 1),
+        swap(mixed, "head", head_n, 2),
         limit=LIMIT,
     )
     own_mid, mixed = call(
         functools.partial(last_kernel, n),
         [bf16(rows, model_d)] * 2,
         mixed,
-        swap(mixed, "head", head_n, 2),
+        swap(mixed, "head", head_n, 1),
         *mids,
         limit=LIMIT,
     )

time: 44.2 us -> 44.2 us (level)
  no operation moved by 1% of the time
where the time goes in v7:
time: 44.2 us; the launch traced here: 44.1 us
  starting transfers between devices  17.9 us (40%)
  waiting for transfers between devices  15 us (34%)
  Pallas kernels  10.4 us (24%)
  between operations  0.79 us (2%)
    ppermute x13, starting transfers between devices, swap(): return lax.ppermute(x, axis, [(s, s ^ step) for s in range(size)])  17.9 us
    ppermute x13, waiting for transfers between devices, swap(): return lax.ppermute(x, axis, [(s, s ^ step) for s in range(size)])  15 us
    pallas_call x12, Pallas kernels, call(): pl.pallas_call(body, out_shape=outs, in_specs=[VMEM] * len(args) if specs...  10.4 us
  transfers between devices with their start and end apart: 13, of which 9 were waited for; matrix products, arithmetic and copies ran while one was open for 0% of the time, Pallas kernels for 9%

profile of v7, /device:TPU:0, one launch (start us, length us, event | category | flops | bytes accessed | tf_op | source)
XLA Modules:
  0.0 44.1 jit_solution(12546106982576258233)
XLA Ops:
  0.6 2.1 %shard_map.140 = (bf16[8,1024]{1,0:T(8,128)(2,1)S(1)}, bf16[8,3584]{1,0:T(8,128)(2,1)S(1)}, bf16[8,128]{1,0:T(8,128)(2,1)S(1)}, f32[1,3584]{1,0:T(1,128)S(1)}) custom-call(bf16[8,8,512]{2,1,0:T(8,128)(2,1)} %refs_0_.1, bf16[8,32,512]{2,1,0:T(8,128)(2,1)} %refs_1_.1, bf16[8,8,64]{2,1,0:T(8,128)(2,1)} %refs_2_.1, bf16[8,32,64]{2,1,0:T(8,128)(2,1)} %refs_3_.1, ...), custom_call_target="tpu_custom_call" | custom-call | tf_op jit(solution)/shard_map/pallas_call | solution.py:126
  2.8 5.1 %collective-permute-start = (bf16[8,2048]{1,0:T(8,128)(2,1)S(1)}, bf16[8,2048]{1,0:T(8,128)(2,1)S(1)}, u32[]{:S(2)}, u32[]{:S(2)}) collective-permute-start(bf16[8,2048]{1,0:T(8,128)(2,1)S(1)} %get-tuple-element.30), channel_id=1, source_target_pairs={{0,12},{4,8},{8,4},{12,0},{1,13},{5,9},{9,5},{13,1},{2,14},{6,10},... | collective-permute-start | bytes 98312 | tf_op jit(solution)/shard_map/ppermute | solution.py:19
  8.0 0.6 %collective-permute-start.2 = (bf16[8,2048]{1,0:T(8,128)(2,1)S(1)}, bf16[8,2048]{1,0:T(8,128)(2,1)S(1)}, u32[]{:S(2)}, u32[]{:S(2)}) collective-permute-start(bf16[8,2048]{1,0:T(8,128)(2,1)S(1)} %get-tuple-element.32), channel_id=1, source_target_pairs={{0,4},{4,0},{8,12},{12,8},{1,5},{5,1},{9,13},{13,9},{2,6},{6,2},{1... | collective-permute-start | bytes 98312 | tf_op jit(solution)/shard_map/ppermute | solution.py:19
  8.6 1.3 %collective-permute-done.refs_0_ = bf16[8,2048]{1,0:T(8,128)(2,1)S(1)} collective-permute-done((bf16[8,2048]{1,0:T(8,128)(2,1)S(1)}, bf16[8,2048]{1,0:T(8,128)(2,1)S(1)}, u32[]{:S(2)}, u32[]{:S(2)}) %collective-permute-start) | collective-permute-done | bytes 32800 | tf_op jit(solution)/shard_map/ppermute | solution.py:19
  9.9 2.9 %collective-permute-done.1.refs_1_ = bf16[8,2048]{1,0:T(8,128)(2,1)S(1)} collective-permute-done((bf16[8,2048]{1,0:T(8,128)(2,1)S(1)}, bf16[8,2048]{1,0:T(8,128)(2,1)S(1)}, u32[]{:S(2)}, u32[]{:S(2)}) %collective-permute-start.1) | collective-permute-done | bytes 32800 | tf_op jit(solution)/shard_map/ppermute | solution.py:19
  12.8 0.4 shard_map.142
  13.3 1.2 %collective-permute-done.3.b_ref = bf16[32,896]{1,0:T(8,128)(2,1)S(1)} collective-permute-done((bf16[32,896]{1,0:T(8,128)(2,1)S(1)}, bf16[32,896]{1,0:T(8,128)(2,1)S(1)}, u32[]{:S(2)}, u32[]{:S(2)}) %collective-permute-start.3) | collective-permute-done | bytes 57376 | tf_op jit(solution)/shard_map/ppermute | solution.py:19
  14.5 1.6 %collective-permute-start.4 = (bf16[32,896]{1,0:T(8,128)(2,1)S(1)}, bf16[32,896]{1,0:T(8,128)(2,1)S(1)}, u32[]{:S(2)}, u32[]{:S(2)}) collective-permute-start(bf16[32,896]{1,0:T(8,128)(2,1)S(1)} %shard_map.143.a_ref), channel_id=1, source_target_pairs={{0,2},{1,3},{2,0},{3,1},{4,6},{5,7},{6,4},{7,5},{8,10},{9,11},{10,... | collective-permute-start | bytes 172040 | tf_op jit(solution)/shard_map/ppermute | solution.py:19
  16.1 2.7 %collective-permute-done.4.b_ref = bf16[32,896]{1,0:T(8,128)(2,1)S(1)} collective-permute-done((bf16[32,896]{1,0:T(8,128)(2,1)S(1)}, bf16[32,896]{1,0:T(8,128)(2,1)S(1)}, u32[]{:S(2)}, u32[]{:S(2)}) %collective-permute-start.4) | collective-permute-done | bytes 57376 | tf_op jit(solution)/shard_map/ppermute | solution.py:19
  18.9 2.1 %collective-permute-start.6 = (bf16[32,896]{1,0:T(8,128)(2,1)S(1)}, bf16[32,896]{1,0:T(8,128)(2,1)S(1)}, u32[]{:S(2)}, u32[]{:S(2)}) collective-permute-start(bf16[32,896]{1,0:T(8,128)(2,1)S(1)} %shard_map.144.mid_ref.refs_0_), channel_id=1, source_target_pairs={{0,8},{4,12},{8,0},{12,4},{1,9},{5,13},{9,1},{13,5},{2,10},{6,14},... | collective-permute-start | bytes 172040 | tf_op jit(solution)/shard_map/ppermute | solution.py:19
  21.0 2.3 %collective-permute-start.7 = (bf16[32,896]{1,0:T(8,128)(2,1)S(1)}, bf16[32,896]{1,0:T(8,128)(2,1)S(1)}, u32[]{:S(2)}, u32[]{:S(2)}) collective-permute-start(bf16[32,896]{1,0:T(8,128)(2,1)S(1)} %shard_map.144.mid_ref.refs_0_), channel_id=1, source_target_pairs={{0,12},{4,8},{8,4},{12,0},{1,13},{5,9},{9,5},{13,1},{2,14},{6,10},... | collective-permute-start | bytes 172040 | tf_op jit(solution)/shard_map/ppermute | solution.py:19
  23.3 1.3 %shard_map.145 = (f32[32,2048]{1,0:T(8,128)S(1)}, f32[32,2048]{1,0:T(8,128)S(1)}, f32[32,128]{1,0:T(8,128)S(1)}) custom-call(f32[1,3584]{1,0:T(1,128)S(1)} %get-tuple-element.26.gain_ref, bf16[8,3584,256]{2,1,0:T(8,128)(2,1)S(1)} %copy-done, bf16[8,3584,256]{2,1,0:T(8,128)(2,1)S(1)} %copy-done.1, bf16[8,256,3584]{2,1,0:T(8,128)(2,1)S(1)} %copy-done.2, ...), custom_call_target="tpu_custom_call" | custom-call | flops 1000000000 | bytes 1048576 | tf_op jit(solution)/shard_map/pallas_call | solution.py:126
  24.5 1.3 %shard_map.146 = (f32[32,2048]{1,0:T(8,128)S(1)}, f32[32,2048]{1,0:T(8,128)S(1)}, f32[32,128]{1,0:T(8,128)S(1)}) custom-call(f32[1,3584]{1,0:T(1,128)S(1)} %get-tuple-element.26.gain_ref, bf16[8,3584,256]{2,1,0:T(8,128)(2,1)S(1)} %copy-done, bf16[8,3584,256]{2,1,0:T(8,128)(2,1)S(1)} %copy-done.1, bf16[8,256,3584]{2,1,0:T(8,128)(2,1)S(1)} %copy-done.2, ...), custom_call_target="tpu_custom_call" | custom-call | flops 1000000000 | bytes 1048576 | tf_op jit(solution)/shard_map/pallas_call | solution.py:126
  25.8 1.3 %shard_map.147 = (f32[32,2048]{1,0:T(8,128)S(1)}, f32[32,2048]{1,0:T(8,128)S(1)}, f32[32,128]{1,0:T(8,128)S(1)}) custom-call(f32[1,3584]{1,0:T(1,128)S(1)} %get-tuple-element.26.gain_ref, bf16[8,3584,256]{2,1,0:T(8,128)(2,1)S(1)} %copy-done, bf16[8,3584,256]{2,1,0:T(8,128)(2,1)S(1)} %copy-done.1, bf16[8,256,3584]{2,1,0:T(8,128)(2,1)S(1)} %copy-done.2, ...), custom_call_target="tpu_custom_call" | custom-call | flops 1000000000 | bytes 1048576 | tf_op jit(solution)/shard_map/pallas_call | solution.py:126
  27.1 3.2 %shard_map.148 = (f32[8,3584]{1,0:T(8,128)S(1)}, bf16[8,3584]{1,0:T(8,128)(2,1)S(1)}, bf16[8,3584]{1,0:T(8,128)(2,1)S(1)}, bf16[8,3584]{1,0:T(8,128)(2,1)S(1)}) custom-call(f32[1,3584]{1,0:T(1,128)S(1)} %get-tuple-element.26.gain_ref, bf16[8,3584,256]{2,1,0:T(8,128)(2,1)S(1)} %copy-done, bf16[8,3584,256]{2,1,0:T(8,128)(2,1)S(1)} %copy-done.1, ...), custom_call_target="tpu_custom_call" | custom-call | flops 1000000000 | bytes 1048576 | tf_op jit(solution)/shard_map/pallas_call | solution.py:126
  30.4 2.4 %collective-permute-start.10 = (bf16[8,3584]{1,0:T(8,128)(2,1)S(1)}, bf16[8,3584]{1,0:T(8,128)(2,1)S(1)}, u32[]{:S(2)}, u32[]{:S(2)}) collective-permute-start(bf16[8,3584]{1,0:T(8,128)(2,1)S(1)} %get-tuple-element.49), channel_id=1, source_target_pairs={{0,12},{4,8},{8,4},{12,0},{1,13},{5,9},{9,5},{13,1},{2,14},{6,10},... | collective-permute-start | bytes 172040 | tf_op jit(solution)/shard_map/ppermute | solution.py:19
  32.8 2.1 %collective-permute-start.9 = (bf16[8,3584]{1,0:T(8,128)(2,1)S(1)}, bf16[8,3584]{1,0:T(8,128)(2,1)S(1)}, u32[]{:S(2)}, u32[]{:S(2)}) collective-permute-start(bf16[8,3584]{1,0:T(8,128)(2,1)S(1)} %get-tuple-element.48), channel_id=1, source_target_pairs={{0,8},{4,12},{8,0},{12,4},{1,9},{5,13},{9,1},{13,5},{2,10},{6,14},... | collective-permute-start | bytes 172040 | tf_op jit(solution)/shard_map/ppermute | solution.py:19
  34.8 1.6 %collective-permute-done.10.refs_2_ = bf16[8,3584]{1,0:T(8,128)(2,1)S(1)} collective-permute-done((bf16[8,3584]{1,0:T(8,128)(2,1)S(1)}, bf16[8,3584]{1,0:T(8,128)(2,1)S(1)}, u32[]{:S(2)}, u32[]{:S(2)}) %collective-permute-start.10) | collective-permute-done | bytes 57376 | tf_op jit(solution)/shard_map/ppermute | solution.py:19
  36.4 0.6 %collective-permute-done.8.refs_0_ = bf16[8,3584]{1,0:T(8,128)(2,1)S(1)} collective-permute-done((bf16[8,3584]{1,0:T(8,128)(2,1)S(1)}, bf16[8,3584]{1,0:T(8,128)(2,1)S(1)}, u32[]{:S(2)}, u32[]{:S(2)}) %collective-permute-start.8) | collective-permute-done | bytes 57376 | tf_op jit(solution)/shard_map/ppermute | solution.py:19
  37.0 0.8 %collective-permute-done.9.refs_1_ = bf16[8,3584]{1,0:T(8,128)(2,1)S(1)} collective-permute-done((bf16[8,3584]{1,0:T(8,128)(2,1)S(1)}, bf16[8,3584]{1,0:T(8,128)(2,1)S(1)}, u32[]{:S(2)}, u32[]{:S(2)}) %collective-permute-start.9) | collective-permute-done | bytes 57376 | tf_op jit(solution)/shard_map/ppermute | solution.py:19
  37.9 1.6 %collective-permute-start.11 = (bf16[8,3584]{1,0:T(8,128)(2,1)S(1)}, bf16[8,3584]{1,0:T(8,128)(2,1)S(1)}, u32[]{:S(2)}, u32[]{:S(2)}) collective-permute-start(bf16[8,3584]{1,0:T(8,128)(2,1)S(1)} %shard_map.149.a_ref), channel_id=1, source_target_pairs={{0,2},{1,3},{2,0},{3,1},{4,6},{5,7},{6,4},{7,5},{8,10},{9,11},{10,... | collective-permute-start | bytes 172040 | tf_op jit(solution)/shard_map/ppermute | solution.py:19
  39.4 2.7 %collective-permute-done.11.b_ref = bf16[8,3584]{1,0:T(8,128)(2,1)S(1)} collective-permute-done((bf16[8,3584]{1,0:T(8,128)(2,1)S(1)}, bf16[8,3584]{1,0:T(8,128)(2,1)S(1)}, u32[]{:S(2)}, u32[]{:S(2)}) %collective-permute-start.11) | collective-permute-done | bytes 57376 | tf_op jit(solution)/shard_map/ppermute | solution.py:19
  42.2 1.2 %collective-permute-done.12.b_ref = bf16[8,3584]{1,0:T(8,128)(2,1)S(1)} collective-permute-done((bf16[8,3584]{1,0:T(8,128)(2,1)S(1)}, bf16[8,3584]{1,0:T(8,128)(2,1)S(1)}, u32[]{:S(2)}, u32[]{:S(2)}) %collective-permute-start.12) | collective-permute-done | bytes 57376 | tf_op jit(solution)/shard_map/ppermute | solution.py:19
  43.4 0.7 %shard_map.151 = (bf16[8,3584]{1,0:T(8,128)(2,1)}, bf16[8,3584]{1,0:T(8,128)(2,1)}) custom-call(bf16[8,3584]{1,0:T(8,128)(2,1)S(1)} %shard_map.150.a_ref, bf16[8,3584]{1,0:T(8,128)(2,1)S(1)} %collective-permute-done.12.b_ref, bf16[32,896]{1,0:T(8,128)(2,1)S(1)} %shard_map.144.mid_ref.refs_0_, bf16[32,896]{1,0:T(8,128)(2,1)S(1)} %collective-permute-done.5.mid_ref.refs_1_, ...), custom_call_target="tpu_custom_call" | custom-call | tf_op jit(solution)/shard_map/pallas_call | solution.py:126
  (22 shorter events, 0.4 us)
Async XLA Ops:
  2.8 10.0 %copy-start.3 = (bf16[1024,896]{1,0:T(8,128)(2,1)S(1)}, bf16[1024,896]{1,0:T(8,128)(2,1)}, u32[]{:S(2)}) copy-start(bf16[1024,896]{1,0:T(8,128)(2,1)} %proj_ref.1) | copy-start | bytes 5505028
  2.8 20.5 %copy-start = (bf16[8,3584,256]{2,1,0:T(8,128)(2,1)S(1)}, bf16[8,3584,256]{2,1,0:T(8,128)(2,1)}, u32[]{:S(2)}) copy-start(bf16[8,3584,256]{2,1,0:T(8,128)(2,1)} %wg_ref.7) | copy-start | bytes 44040196
  2.8 20.5 %copy-start.1 = (bf16[8,3584,256]{2,1,0:T(8,128)(2,1)S(1)}, bf16[8,3584,256]{2,1,0:T(8,128)(2,1)}, u32[]{:S(2)}) copy-start(bf16[8,3584,256]{2,1,0:T(8,128)(2,1)} %wu_ref.7) | copy-start | bytes 44040196
  2.8 20.5 %copy-start.2 = (bf16[8,256,3584]{2,1,0:T(8,128)(2,1)S(1)}, bf16[8,256,3584]{2,1,0:T(8,128)(2,1)}, u32[]{:S(2)}) copy-start(bf16[8,256,3584]{2,1,0:T(8,128)(2,1)} %wd_ref.1) | copy-start | bytes 44040196
  2.8 7.0 %collective-permute-start = (bf16[8,2048]{1,0:T(8,128)(2,1)S(1)}, bf16[8,2048]{1,0:T(8,128)(2,1)S(1)}, u32[]{:S(2)}, u32[]{:S(2)}) collective-permute-start(bf16[8,2048]{1,0:T(8,128)(2,1)S(1)} %get-tuple-element.30), channel_id=1, source_target_pairs={{0,12},{4,8},{8,4},{12,0},{1,13},{5,9},{9,5},{13,1},{2,14},{6,10},... | collective-permute-start | bytes 98312 | tf_op jit(solution)/shard_map/ppermute | solution.py:19
  8.0 4.8 %collective-permute-start.1 = (bf16[8,2048]{1,0:T(8,128)(2,1)S(1)}, bf16[8,2048]{1,0:T(8,128)(2,1)S(1)}, u32[]{:S(2)}, u32[]{:S(2)}) collective-permute-start(bf16[8,2048]{1,0:T(8,128)(2,1)S(1)} %get-tuple-element.31), channel_id=1, source_target_pairs={{0,8},{4,12},{8,0},{12,4},{1,9},{5,13},{9,1},{13,5},{2,10},{6,14},... | collective-permute-start | bytes 98312 | tf_op jit(solution)/shard_map/ppermute | solution.py:19
  8.0 4.8 %collective-permute-start.2 = (bf16[8,2048]{1,0:T(8,128)(2,1)S(1)}, bf16[8,2048]{1,0:T(8,128)(2,1)S(1)}, u32[]{:S(2)}, u32[]{:S(2)}) collective-permute-start(bf16[8,2048]{1,0:T(8,128)(2,1)S(1)} %get-tuple-element.32), channel_id=1, source_target_pairs={{0,4},{4,0},{8,12},{12,8},{1,5},{5,1},{9,13},{13,9},{2,6},{6,2},{1... | collective-permute-start | bytes 98312 | tf_op jit(solution)/shard_map/ppermute | solution.py:19
  13.2 1.3 %collective-permute-start.3 = (bf16[32,896]{1,0:T(8,128)(2,1)S(1)}, bf16[32,896]{1,0:T(8,128)(2,1)S(1)}, u32[]{:S(2)}, u32[]{:S(2)}) collective-permute-start(bf16[32,896]{1,0:T(8,128)(2,1)S(1)} %get-tuple-element.35.a_ref), channel_id=1, source_target_pairs={{0,1},{1,0},{2,3},{3,2},{4,5},{5,4},{6,7},{7,6},{8,9},{9,8},{10,11... | collective-permute-start | bytes 172040 | tf_op jit(solution)/shard_map/ppermute | solution.py:19
  14.5 4.2 %collective-permute-start.4 = (bf16[32,896]{1,0:T(8,128)(2,1)S(1)}, bf16[32,896]{1,0:T(8,128)(2,1)S(1)}, u32[]{:S(2)}, u32[]{:S(2)}) collective-permute-start(bf16[32,896]{1,0:T(8,128)(2,1)S(1)} %shard_map.143.a_ref), channel_id=1, source_target_pairs={{0,2},{1,3},{2,0},{3,1},{4,6},{5,7},{6,4},{7,5},{8,10},{9,11},{10,... | collective-permute-start | bytes 172040 | tf_op jit(solution)/shard_map/ppermute | solution.py:19
  18.8 5.7 %collective-permute-start.5 = (bf16[32,896]{1,0:T(8,128)(2,1)S(1)}, bf16[32,896]{1,0:T(8,128)(2,1)S(1)}, u32[]{:S(2)}, u32[]{:S(2)}) collective-permute-start(bf16[32,896]{1,0:T(8,128)(2,1)S(1)} %shard_map.144.mid_ref.refs_0_), channel_id=1, source_target_pairs={{0,4},{4,0},{8,12},{12,8},{1,5},{5,1},{9,13},{13,9},{2,6},{6,2},{1... | collective-permute-start | bytes 172040 | tf_op jit(solution)/shard_map/ppermute | solution.py:19
  18.9 7.0 %collective-permute-start.6 = (bf16[32,896]{1,0:T(8,128)(2,1)S(1)}, bf16[32,896]{1,0:T(8,128)(2,1)S(1)}, u32[]{:S(2)}, u32[]{:S(2)}) collective-permute-start(bf16[32,896]{1,0:T(8,128)(2,1)S(1)} %shard_map.144.mid_ref.refs_0_), channel_id=1, source_target_pairs={{0,8},{4,12},{8,0},{12,4},{1,9},{5,13},{9,1},{13,5},{2,10},{6,14},... | collective-permute-start | bytes 172040 | tf_op jit(solution)/shard_map/ppermute | solution.py:19
  21.0 6.2 %collective-permute-start.7 = (bf16[32,896]{1,0:T(8,128)(2,1)S(1)}, bf16[32,896]{1,0:T(8,128)(2,1)S(1)}, u32[]{:S(2)}, u32[]{:S(2)}) collective-permute-start(bf16[32,896]{1,0:T(8,128)(2,1)S(1)} %shard_map.144.mid_ref.refs_0_), channel_id=1, source_target_pairs={{0,12},{4,8},{8,4},{12,0},{1,13},{5,9},{9,5},{13,1},{2,14},{6,10},... | collective-permute-start | bytes 172040 | tf_op jit(solution)/shard_map/ppermute | solution.py:19
  30.4 6.1 %collective-permute-start.10 = (bf16[8,3584]{1,0:T(8,128)(2,1)S(1)}, bf16[8,3584]{1,0:T(8,128)(2,1)S(1)}, u32[]{:S(2)}, u32[]{:S(2)}) collective-permute-start(bf16[8,3584]{1,0:T(8,128)(2,1)S(1)} %get-tuple-element.49), channel_id=1, source_target_pairs={{0,12},{4,8},{8,4},{12,0},{1,13},{5,9},{9,5},{13,1},{2,14},{6,10},... | collective-permute-start | bytes 172040 | tf_op jit(solution)/shard_map/ppermute | solution.py:19
  32.7 4.3 %collective-permute-start.8 = (bf16[8,3584]{1,0:T(8,128)(2,1)S(1)}, bf16[8,3584]{1,0:T(8,128)(2,1)S(1)}, u32[]{:S(2)}, u32[]{:S(2)}) collective-permute-start(bf16[8,3584]{1,0:T(8,128)(2,1)S(1)} %get-tuple-element.47), channel_id=1, source_target_pairs={{0,4},{4,0},{8,12},{12,8},{1,5},{5,1},{9,13},{13,9},{2,6},{6,2},{1... | collective-permute-start | bytes 172040 | tf_op jit(solution)/shard_map/ppermute | solution.py:19
  32.8 5.1 %collective-permute-start.9 = (bf16[8,3584]{1,0:T(8,128)(2,1)S(1)}, bf16[8,3584]{1,0:T(8,128)(2,1)S(1)}, u32[]{:S(2)}, u32[]{:S(2)}) collective-permute-start(bf16[8,3584]{1,0:T(8,128)(2,1)S(1)} %get-tuple-element.48), channel_id=1, source_target_pairs={{0,8},{4,12},{8,0},{12,4},{1,9},{5,13},{9,1},{13,5},{2,10},{6,14},... | collective-permute-start | bytes 172040 | tf_op jit(solution)/shard_map/ppermute | solution.py:19
  37.9 4.2 %collective-permute-start.11 = (bf16[8,3584]{1,0:T(8,128)(2,1)S(1)}, bf16[8,3584]{1,0:T(8,128)(2,1)S(1)}, u32[]{:S(2)}, u32[]{:S(2)}) collective-permute-start(bf16[8,3584]{1,0:T(8,128)(2,1)S(1)} %shard_map.149.a_ref), channel_id=1, source_target_pairs={{0,2},{1,3},{2,0},{3,1},{4,6},{5,7},{6,4},{7,5},{8,10},{9,11},{10,... | collective-permute-start | bytes 172040 | tf_op jit(solution)/shard_map/ppermute | solution.py:19
  42.1 1.3 %collective-permute-start.12 = (bf16[8,3584]{1,0:T(8,128)(2,1)S(1)}, bf16[8,3584]{1,0:T(8,128)(2,1)S(1)}, u32[]{:S(2)}, u32[]{:S(2)}) collective-permute-start(bf16[8,3584]{1,0:T(8,128)(2,1)S(1)} %shard_map.150.a_ref), channel_id=1, source_target_pairs={{0,1},{1,0},{2,3},{3,2},{4,5},{5,4},{6,7},{7,6},{8,9},{9,8},{10,11... | collective-permute-start | bytes 172040 | tf_op jit(solution)/shard_map/ppermute | solution.py:19
